TPU v7x, 32 devices: a whole 2x2x4 slice. The times are simulated.
32 devices in a mesh: dp: 16 (over z, x, core), tensor: 2 (over y).
Axes of the slice: x: 2, y: 2, z: 4, core: 2. Of those that a mesh axis runs over, the one named last changes fastest.
Arguments:
- tokens: bfloat16 [4096, 768], P(('dp', 'tensor')), may hold values from -6 to 6
- cotangent: bfloat16 [4096, 768], P(('dp', 'tensor')), may hold values from -6 to 6
- query_weight: bfloat16 [768, 768], P('dp', 'tensor'), may hold values from -0.21875 to 0.21875
- key_weight: bfloat16 [768, 768], P('dp', 'tensor'), may hold values from -0.21875 to 0.21875
- value_weight: bfloat16 [768, 768], P('dp', 'tensor'), may hold values from -0.21875 to 0.21875
- output_weight: bfloat16 [768, 768], P('dp', 'tensor'), may hold values from -0.875 to 0.875
- attention_scale: bfloat16 [768], P('dp'), may hold values from 0.5 to 1.5
- expert_scale: bfloat16 [768], P('dp'), may hold values from 0.5 to 1.5
- router: bfloat16 [768, 4], P('dp'), may hold values from -0.15625 to 0.15625
- bucket_bias: float32 [32, 12], P(None, 'tensor'), may hold values from -4 to 4
- expert_up_weight: bfloat16 [768, 12288], P(None, ('dp', 'tensor')), may hold values from -0.21875 to 0.21875
- expert_down_weight: bfloat16 [768, 12288], P(None, ('dp', 'tensor')), may hold values from -0.625 to 0.625
- routes: int32 [4096, 1], P('dp'), may hold values from 0 to 3; in each aligned block of 256 rows (0 to 255, 256 to 511, ...) at most 80 rows name the same one
- lengths: int32 [16, 2], P('dp'), may hold values from 0 to 256, as said below
- buckets: int32 [511], replicated, may hold values from 0 to 31
Outputs:
- layer_out: bfloat16 [4096, 768], P(('dp', 'tensor'))
- grad_tokens: bfloat16 [4096, 768], P(('dp', 'tensor'))
- grad_query: float32 [768, 768], P('dp', 'tensor')
- grad_key: float32 [768, 768], P('dp', 'tensor')
- grad_value: float32 [768, 768], P('dp', 'tensor')
- grad_output: float32 [768, 768], P('dp', 'tensor')
- grad_gain_attn: float32 [768], P('dp')
- grad_gain_moe: float32 [768], P('dp')
- grad_router: float32 [768, 4], P('dp')
- grad_table: float32 [32, 12], P(None, 'tensor')
- grad_w_in: float32 [768, 12288], P(None, ('dp', 'tensor'))
- grad_w_out: float32 [768, 12288], P(None, ('dp', 'tensor'))
Inputs may be any that keep to these rules, and one draw needn't show every extreme that they name: `routes`: in the 256 rows of one block no expert is named more than 80 times; some expert is named exactly 80 times in some block. The two lengths of a block sum to at most 256; some block holds one sequence of all 256 slots.
All inputs are finite; a program needn't handle non-finite values.
Results may differ from a plain program's by a relative error of at most 0.02.
Values may be sent and summed in bfloat16 or wider, within the bound.
No kernel may reach another device: no remote copies, remote signals or barrier semaphores. Data moves between devices by JAX's collectives and lax.ppermute only.
A program may use at most 128 MiB of HBM per device.

v0:
```python
import jax
import jax.numpy as jnp
from jax import lax
from jax.sharding import PartitionSpec as P

HEADS = 12
HEAD_DIM = 64
SPLIT = 4


EPSILON = 1e-06
MASKED_SCORE = -1e30
HIGHEST = lax.Precision.HIGHEST


def inverse_rms(values):
    return lax.rsqrt(jnp.mean(values * values, axis=-1, keepdims=True) + EPSILON)


def norm_backward(input_tokens, inv_scale, gain_vec, grad_normed):
    scaled = grad_normed * gain_vec
    grad_inputs = inv_scale * scaled - input_tokens * inv_scale**3 * jnp.mean(
        scaled * input_tokens, axis=-1, keepdims=True
    )
    grad_gain = jnp.sum(grad_normed * input_tokens * inv_scale, axis=0)
    return (grad_inputs, grad_gain)


def contract_rows(left_arr, right_arr, precision=None):
    return lax.dot_general(
        left_arr,
        right_arr,
        (((0,), (0,)), ((), ())),
        precision=precision,
        preferred_element_type=jnp.float32,
    )


def times_transposed(left_arr, right_arr):
    return lax.dot_general(
        left_arr, right_arr, (((1,), (1,)), ((), ())), preferred_element_type=jnp.float32
    )


def gelu_tanh(values):
    return jax.nn.gelu(values, approximate=True)


def body(
    tokens,
    cotangent,
    query_weight,
    key_weight,
    value_weight,
    output_weight,
    attention_scale,
    expert_scale,
    router,
    bucket_bias,
    expert_up_weight,
    expert_down_weight,
    routes,
    lengths,
    buckets,
):
    row_count = tokens.shape[0]
    model_width = tokens.shape[1]
    block_len = routes.shape[0]
    expert_count = router.shape[1]
    capacity = max(2, block_len * 5 // (4 * expert_count))
    data_count = lax.axis_size("dp")
    local_heads = bucket_bias.shape[1]
    head_width = local_heads * HEAD_DIM
    tensor_index = lax.axis_index("tensor")
    row_start = tensor_index * row_count
    gathered = (
        lax.all_gather(query_weight, "dp", axis=0, tiled=True),
        lax.all_gather(key_weight, "dp", axis=0, tiled=True),
        lax.all_gather(value_weight, "dp", axis=0, tiled=True),
        lax.all_gather(output_weight, "dp", axis=0, tiled=True),
        lax.all_gather(attention_scale, "dp", axis=0, tiled=True),
        lax.all_gather(expert_scale, "dp", axis=0, tiled=True),
        lax.all_gather(router, "dp", axis=0, tiled=True),
    )
    full_query, full_key, full_value, full_output = (
        gathered[0],
        gathered[1],
        gathered[2],
        gathered[3],
    )
    attn_gain = gathered[4].astype(jnp.float32)
    moe_gain = gathered[5].astype(jnp.float32)
    router_bf = gathered[6]
    router_full = router_bf.astype(jnp.float32)
    token_position = jnp.arange(block_len, dtype=jnp.int32)
    first_len = lengths[0, 0]
    active_count = first_len + lengths[0, 1]
    segment_ids = jnp.where(
        token_position < first_len, 0, jnp.where(token_position < active_count, 1, 2)
    )
    live_all = (token_position < active_count).astype(jnp.float32)
    live_own = lax.dynamic_slice_in_dim(live_all, row_start, row_count)
    token_rows = tokens.astype(jnp.float32)
    scale_attn = inverse_rms(token_rows)
    normed_attn = (token_rows * scale_attn * attn_gain).astype(jnp.bfloat16)
    seq_normed = lax.all_gather(normed_attn, "tensor", axis=0, tiled=True)

    def project(weight):
        projected = jnp.dot(seq_normed, weight, preferred_element_type=jnp.float32)
        return projected.astype(jnp.bfloat16).reshape(block_len, local_heads, HEAD_DIM)

    queries = project(full_query)
    key_rows = project(full_key)
    value_rows = project(full_value)
    bucket_pick = (
        buckets[:, None] == jnp.arange(bucket_bias.shape[0], dtype=jnp.int32)[None, :]
    ).astype(jnp.float32)
    head_table = lax.dot_general(
        bucket_bias,
        bucket_pick,
        (((0,), (1,)), ((), ())),
        precision=HIGHEST,
        preferred_element_type=jnp.float32,
    )
    offset = token_position[None, :] - token_position[:, None] + block_len - 1

    def expand_bias(head_rows):
        return jnp.take(head_rows, offset, axis=1)

    rel_bias, bias_back = jax.vjp(expand_bias, head_table)
    allowed = (segment_ids[:, None] == segment_ids[None, :])[None]
    score_scale = HEAD_DIM ** (-0.5)

    def masked_scores():
        raw_scores = jnp.einsum(
            "qhd,khd->hqk", queries, key_rows, preferred_element_type=jnp.float32
        )
        return jnp.where(allowed, raw_scores * score_scale + rel_bias, MASKED_SCORE)

    scores = masked_scores()
    score_peak = jnp.max(scores, axis=-1, keepdims=True)
    log_total = score_peak + jnp.log(jnp.sum(jnp.exp(scores - score_peak), axis=-1, keepdims=True))
    attn_probs = jnp.exp(scores - log_total)
    context_rows = jnp.einsum(
        "hqk,khd->qhd",
        attn_probs.astype(jnp.bfloat16),
        value_rows,
        preferred_element_type=jnp.float32,
    )
    context_rows = (context_rows.reshape(block_len, head_width) * live_all[:, None]).astype(
        jnp.bfloat16
    )
    attention_layer = lax.psum_scatter(
        times_transposed(context_rows, full_output).astype(jnp.bfloat16),
        "tensor",
        scatter_dimension=0,
        tiled=True,
    ).astype(jnp.float32)
    residual = token_rows + attention_layer
    scale_moe = inverse_rms(residual)
    normed_moe = (residual * scale_moe * moe_gain).astype(jnp.bfloat16)
    expert_routing = routes[:, 0]
    pick_block = (
        expert_routing[:, None] == jnp.arange(expert_count, dtype=jnp.int32)[None, :]
    ).astype(jnp.int32)
    capacity_index = jnp.sum((jnp.cumsum(pick_block, axis=0) - 1) * pick_block, axis=1)
    seq_mixed, seq_cotangent = (
        lax.all_gather(normed_moe, "tensor", axis=0, tiled=True),
        lax.all_gather(cotangent, "tensor", axis=0, tiled=True),
    )
    cot_rows = seq_cotangent.astype(jnp.float32)
    weight_in, weight_out = (expert_up_weight, expert_down_weight)
    hidden_local = weight_in.shape[1]
    logits = jnp.dot(seq_mixed, router_bf, preferred_element_type=jnp.float32)
    router_probs = jax.nn.softmax(logits, axis=-1)
    route_pick = (
        expert_routing[:, None] == jnp.arange(expert_count, dtype=jnp.int32)[None, :]
    ).astype(jnp.float32)
    gate_rows = jnp.sum(router_probs * route_pick, axis=1)

    def dispatch(row_data):
        placed = jnp.zeros((expert_count, capacity, model_width), row_data.dtype)
        placed = placed.at[expert_routing, capacity_index].set(row_data)
        copies = jnp.broadcast_to(placed[:, None], (expert_count, SPLIT, capacity, model_width))
        return copies.reshape(expert_count * SPLIT, capacity, model_width)

    def collect(returned):
        summed = jnp.sum(returned.reshape(expert_count, SPLIT, capacity, model_width), axis=1)
        return summed[expert_routing, capacity_index]

    received = lax.all_to_all(dispatch(seq_mixed), "dp", split_axis=0, concat_axis=0, tiled=True)
    source_count = received.shape[0]
    item_count = received.shape[1]
    flat_rows = received.reshape(source_count * item_count, model_width)
    pre_act = jnp.dot(flat_rows, weight_in, preferred_element_type=jnp.float32)
    hidden = gelu_tanh(pre_act).astype(jnp.bfloat16)
    part_sum = times_transposed(hidden, weight_out)
    expert_out = part_sum.reshape(source_count, item_count, model_width)
    kept_pre = pre_act.reshape(source_count, item_count, hidden_local)
    returned = lax.all_to_all(
        expert_out.astype(jnp.bfloat16), "dp", split_axis=0, concat_axis=0, tiled=True
    ).astype(expert_out.dtype)
    collected = collect(returned)
    expert_overall = lax.psum_scatter(
        collected.astype(jnp.bfloat16), "tensor", scatter_dimension=0, tiled=True
    ).astype(jnp.float32)
    gate_own = lax.dynamic_slice_in_dim(gate_rows, row_start, row_count)
    layer_out = residual + gate_own[:, None] * expert_overall * live_own[:, None]
    grad_out = cotangent.astype(jnp.float32)
    grad_gate = jnp.sum(grad_out * expert_overall, axis=1) * live_own
    grad_total = (cot_rows * live_all[:, None] * gate_rows[:, None]).astype(jnp.bfloat16)
    grad_received = lax.all_to_all(
        dispatch(grad_total), "dp", split_axis=0, concat_axis=0, tiled=True
    )
    grad_flat = grad_received.reshape(-1, model_width)
    rows_flat = received.reshape(-1, model_width)
    pre_flat = kept_pre.reshape(-1, hidden_local)
    hidden_f, gelu_back = jax.vjp(gelu_tanh, pre_flat)
    hidden_b = hidden_f.astype(jnp.bfloat16)
    grad_hidden = jnp.dot(grad_flat, weight_out, preferred_element_type=jnp.float32)
    grad_pre = gelu_back(grad_hidden)[0].astype(jnp.bfloat16)
    grad_w_out = contract_rows(grad_flat, hidden_b)
    grad_w_in = contract_rows(rows_flat, grad_pre)
    grad_back = times_transposed(grad_pre, weight_in).reshape(data_count, capacity, model_width)
    grad_home = lax.all_to_all(
        grad_back.astype(jnp.bfloat16), "dp", split_axis=0, concat_axis=0, tiled=True
    ).astype(grad_back.dtype)
    grad_collected = collect(grad_home)
    grad_moe_normed = lax.psum_scatter(
        grad_collected.astype(jnp.bfloat16), "tensor", scatter_dimension=0, tiled=True
    ).astype(jnp.float32)
    probs_own = lax.dynamic_slice_in_dim(router_probs, row_start, row_count, 0)
    pick_own = lax.dynamic_slice_in_dim(route_pick, row_start, row_count, 0)
    grad_logits = (grad_gate * gate_own)[:, None] * (pick_own - probs_own)
    grad_router = contract_rows(normed_moe.astype(jnp.float32), grad_logits, HIGHEST)
    grad_moe_normed = grad_moe_normed + jnp.dot(grad_logits, router_full.T, precision=HIGHEST)
    grad_mid, grad_moe_gain = norm_backward(residual, scale_moe, moe_gain, grad_moe_normed)
    grad_mid = grad_out + grad_mid
    grad_attention = lax.all_gather(grad_mid.astype(jnp.bfloat16), "tensor", axis=0, tiled=True)
    grad_w_output = contract_rows(grad_attention, context_rows)
    grad_context = jnp.dot(grad_attention, full_output, preferred_element_type=jnp.float32)
    grad_context = (
        (grad_context * live_all[:, None])
        .astype(jnp.bfloat16)
        .reshape(block_len, local_heads, HEAD_DIM)
    )
    scores = masked_scores()
    attn_probs = jnp.exp(scores - log_total)
    grad_values = jnp.einsum(
        "hqk,qhd->khd",
        attn_probs.astype(jnp.bfloat16),
        grad_context,
        preferred_element_type=jnp.float32,
    ).astype(jnp.bfloat16)
    grad_probs = jnp.einsum(
        "qhd,khd->hqk", grad_context, value_rows, preferred_element_type=jnp.float32
    )
    grad_scores = attn_probs * (
        grad_probs - jnp.sum(attn_probs * grad_probs, axis=-1, keepdims=True)
    )
    grad_scores = grad_scores.astype(jnp.bfloat16)
    grad_queries = (
        jnp.einsum("hqk,khd->qhd", grad_scores, key_rows, preferred_element_type=jnp.float32)
        * score_scale
    ).astype(jnp.bfloat16)
    grad_keys = (
        jnp.einsum("hqk,qhd->khd", grad_scores, queries, preferred_element_type=jnp.float32)
        * score_scale
    ).astype(jnp.bfloat16)
    grad_rel = bias_back(grad_scores.astype(jnp.float32))[0]
    grad_table = lax.dot_general(
        bucket_pick,
        grad_rel,
        (((0,), (1,)), ((), ())),
        precision=HIGHEST,
        preferred_element_type=jnp.float32,
    )
    flat_grads = (
        grad_queries.reshape(block_len, head_width),
        grad_keys.reshape(block_len, head_width),
        grad_values.reshape(block_len, head_width),
    )
    accumulated = jnp.zeros((row_count * lax.axis_size("tensor"), model_width), jnp.float32)
    for grad_piece, weight in zip(flat_grads, (full_query, full_key, full_value)):
        accumulated = accumulated + times_transposed(grad_piece, weight)
    grad_attn_normed = lax.psum_scatter(
        accumulated.astype(jnp.bfloat16), "tensor", scatter_dimension=0, tiled=True
    ).astype(jnp.float32)
    grad_inputs, grad_attn_gain = norm_backward(token_rows, scale_attn, attn_gain, grad_attn_normed)
    grad_tokens = grad_mid + grad_inputs
    grad_wq, grad_wk, grad_wv, grad_wo = (
        lax.psum_scatter(
            contract_rows(seq_normed, flat_grads[0]), "dp", scatter_dimension=0, tiled=True
        ),
        lax.psum_scatter(
            contract_rows(seq_normed, flat_grads[1]), "dp", scatter_dimension=0, tiled=True
        ),
        lax.psum_scatter(
            contract_rows(seq_normed, flat_grads[2]), "dp", scatter_dimension=0, tiled=True
        ),
        lax.psum_scatter(grad_w_output, "dp", scatter_dimension=0, tiled=True),
    )
    head_start = tensor_index * local_heads
    table_full = lax.dynamic_update_slice(
        jnp.zeros((bucket_bias.shape[0], HEADS), jnp.float32),
        grad_table,
        (jnp.zeros((), jnp.int32), head_start),
    )
    sum_attn_gain, sum_moe_gain, sum_router, sum_table = lax.psum(
        (grad_attn_gain, grad_moe_gain, grad_router, table_full), ("dp", "tensor")
    )
    shard_rows = model_width // data_count
    data_start = lax.axis_index("dp") * shard_rows
    return (
        layer_out.astype(jnp.bfloat16),
        grad_tokens.astype(jnp.bfloat16),
        grad_wq,
        grad_wk,
        grad_wv,
        grad_wo,
        lax.dynamic_slice_in_dim(sum_attn_gain, data_start, shard_rows),
        lax.dynamic_slice_in_dim(sum_moe_gain, data_start, shard_rows),
        lax.dynamic_slice_in_dim(sum_router, data_start, shard_rows, 0),
        lax.dynamic_slice_in_dim(sum_table, head_start, local_heads, 1),
        grad_w_in,
        grad_w_out,
    )


def solution(mesh):
    in_specs = (
        P(("dp", "tensor"), None),
        P(("dp", "tensor"), None),
        P("dp", "tensor"),
        P("dp", "tensor"),
        P("dp", "tensor"),
        P("dp", "tensor"),
        P("dp"),
        P("dp"),
        P("dp", None),
        P(None, "tensor"),
        P(None, ("dp", "tensor")),
        P(None, ("dp", "tensor")),
        P("dp", None),
        P("dp", None),
        P(),
    )
    out_specs = (
        P(("dp", "tensor"), None),
        P(("dp", "tensor"), None),
        P("dp", "tensor"),
        P("dp", "tensor"),
        P("dp", "tensor"),
        P("dp", "tensor"),
        P("dp"),
        P("dp"),
        P("dp", None),
        P(None, "tensor"),
        P(None, ("dp", "tensor")),
        P(None, ("dp", "tensor")),
    )
    return jax.shard_map(body, mesh=mesh, in_specs=in_specs, out_specs=out_specs, check_vma=False)
```

profile of v0, /device:TPU:0, one launch (start us, length us, event | category | flops | bytes accessed | tf_op | source)
XLA Modules:
  0.0 1135.8 jit_solution(7414931554689373371)
XLA Ops:
  15.7 35.5 %all-reduce.3 = (bf16[768]{0:T(1024)(128)(2,1)S(1)}, bf16[768]{0:T(1024)(128)(2,1)}) all-reduce(bf16[768]{0:T(1024)(128)(2,1)S(1)} %dynamic-update-slice, bf16[768]{0:T(1024)(128)(2,1)S(1)} %dynamic-update-slice.1), channel_id=1, replica_groups=mesh['dp'=16,'tensor'=2] {'dp'}, use_global_device_ids=true, to_apply=%add | all-reduce | flops 1536 | bytes 6144
  61.5 18.9 %all_gather.36 = bf16[768,384]{1,0:T(8,128)(2,1)S(1)} all-gather(bf16[48,384]{1,0:T(8,128)(2,1)S(1)} %copy-done.30), channel_id=1, replica_groups=mesh['dp'=16,'tensor'=2] {'dp'}, dimensions={0}, use_global_device_ids=true | all-gather | bytes 626688 | tf_op jit(solution)/shard_map/all_gather | solution.py:77
  81.7 21.1 %all_gather.37 = bf16[768,384]{1,0:T(8,128)(2,1)S(1)} all-gather(bf16[48,384]{1,0:T(8,128)(2,1)S(1)} %copy-done.31), channel_id=1, replica_groups=mesh['dp'=16,'tensor'=2] {'dp'}, dimensions={0}, use_global_device_ids=true | all-gather | bytes 626688 | tf_op jit(solution)/shard_map/all_gather | solution.py:78
  104.2 19.1 %all_gather.35 = bf16[768,384]{1,0:T(8,128)(2,1)S(1)} all-gather(bf16[48,384]{1,0:T(8,128)(2,1)S(1)} %copy-done.32), channel_id=1, replica_groups=mesh['dp'=16,'tensor'=2] {'dp'}, dimensions={0}, use_global_device_ids=true | all-gather | bytes 626688 | tf_op jit(solution)/shard_map/all_gather | solution.py:79
  125.3 20.4 %all_gather.38 = bf16[768,384]{1,0:T(8,128)(2,1)S(1)} all-gather(bf16[48,384]{1,0:T(8,128)(2,1)S(1)} %copy-done.33), channel_id=1, replica_groups=mesh['dp'=16,'tensor'=2] {'dp'}, dimensions={0}, use_global_device_ids=true | all-gather | bytes 626688 | tf_op jit(solution)/shard_map/all_gather | solution.py:80
  145.7 215.9 %gather_fusion = f32[65536,6]{1,0:T(8,128)} fusion(f32[6,511]{0,1:T(8,128)S(1)} %copy.63, s32[65536]{0:T(1024)S(1)} %broadcast_clamp_fusion), kind=kCustom, calls=%fused_computation | custom fusion | bytes 3407872 | tf_op jit(solution)/shard_map/jvp(jit(_take))/gather | solution.py:128
  361.6 19.9 %copy.65 = f32[256,256,6]{0,1,2:T(8,128)} copy(f32[256,256,6]{2,1,0:T(8,128)} %bitcast.122) | data formatting | bytes 3145728 | tf_op jit(solution)/shard_map/jvp(jit(_take))/gather | solution.py:128
  392.0 17.7 %all-gather = bf16[16,48,4]{1,2,0:T(4,128)(2,1)S(1)} all-gather(bf16[1,48,4]{1,2,0:T(4,128)(2,1)} %bitcast.151), channel_id=1, replica_groups=mesh['dp'=16,'tensor'=2] {'dp'}, dimensions={0}, use_global_device_ids=true | all-gather | bytes 6528 | tf_op jit(solution)/shard_map/all_gather | solution.py:83
  409.8 7.9 all_gather.42
  422.0 7.0 all_gather.40
  431.7 23.7 %scatter_fusion.1 = bf16[4,80,768]{2,1,0:T(8,128)(2,1)S(1)} fusion(bf16[4,80,768]{2,1,0:T(8,128)(2,1)S(1)} %broadcast.254.clone, s32[256]{0:T(256)S(1)} %bitcast.120, bf16[256,768]{1,0:T(8,128)(2,1)} %multiply_convert_fusion.2), kind=kCustom, calls=%fused_computation.4 | custom fusion | bytes 1181696 | tf_op jit(solution)/shard_map/scatter | solution.py:183
  461.3 23.7 %scatter_fusion = bf16[4,80,768]{2,1,0:T(8,128)(2,1)S(1)} fusion(bf16[4,80,768]{2,1,0:T(8,128)(2,1)S(1)} %broadcast.254.clone.1, s32[256]{0:T(256)S(1)} %bitcast.121, bf16[256,768]{1,0:T(8,128)(2,1)} %copy-done.13), kind=kCustom, calls=%fused_computation.3 | custom fusion | bytes 1181696 | tf_op jit(solution)/shard_map/scatter | solution.py:183
  485.0 15.0 %all-to-all-done.2 = bf16[16,80,768]{2,1,0:T(8,128)(2,1)} async-done(((bf16[16,80,768]{2,1,0:T(8,128)(2,1)}), bf16[16,80,768]{2,1,0:T(8,128)(2,1)}, u32[]{:S(2)}, u32[]{:S(2)}) %all-to-all-start.2) | async-done | bytes 1966112 | tf_op jit(solution)/shard_map/all_to_all | solution.py:212
  501.5 10.7 all-to-all-start
  516.3 34.8 %all-to-all-done = bf16[16,80,768]{2,1,0:T(8,128)(2,1)} async-done(((bf16[16,80,768]{2,1,0:T(8,128)(2,1)}), bf16[16,80,768]{2,1,0:T(8,128)(2,1)}, u32[]{:S(2)}, u32[]{:S(2)}) %all-to-all-start) | async-done | bytes 1966112 | tf_op jit(solution)/shard_map/all_to_all | solution.py:191
  559.4 10.7 all-to-all-start.1
  573.8 35.2 %all-to-all-done.1 = bf16[16,80,768]{2,1,0:T(8,128)(2,1)} async-done(((bf16[16,80,768]{2,1,0:T(8,128)(2,1)}), bf16[16,80,768]{2,1,0:T(8,128)(2,1)}, u32[]{:S(2)}, u32[]{:S(2)}) %all-to-all-start.1) | async-done | bytes 1966112 | tf_op jit(solution)/shard_map/all_to_all | solution.py:200
  609.0 10.7 all-to-all-start.3
  624.8 33.8 %all-to-all-done.3 = bf16[16,80,768]{2,1,0:T(8,128)(2,1)} async-done(((bf16[16,80,768]{2,1,0:T(8,128)(2,1)}), bf16[16,80,768]{2,1,0:T(8,128)(2,1)}, u32[]{:S(2)}, u32[]{:S(2)}) %all-to-all-start.3) | async-done | bytes 1966112 | tf_op jit(solution)/shard_map/all_to_all | solution.py:225
  666.0 17.0 %reduce-scatter.13.cloned.1.call-done = bf16[128,768]{1,0:T(8,128)(2,1)} async-done(((bf16[256,768]{1,0:T(8,128)(2,1)}), bf16[128,768]{1,0:T(8,128)(2,1)}) %reduce-scatter.13.cloned.1.call-update) | async-done | bytes 196624 | tf_op jit(solution)/shard_map/reduce_scatter | solution.py:229
  686.8 7.6 all_gather.43
  718.0 16.5 %copy.83 = f32[256,256,6]{2,1,0:T(8,128)} copy(f32[256,256,6]{0,1,2:T(8,128)S(1)} %copy-done.3) | data formatting | bytes 3145728 | tf_op jit(solution)/shard_map/convert_element_type | solution.py:270
  734.5 347.4 %scatter_custom_fusion.2 = f32[6,511]{0,1:T(8,128)S(1)} fusion(s32[65536]{0:T(1024)} %bitcast.144, f32[65536,6]{1,0:T(8,128)} %bitcast.123, f32[]{:T(128)} %constant.31.clone.1), kind=kCustom, calls=%fused_computation.85 | custom fusion | flops 393216 | bytes 12776 | tf_op jit(solution)/shard_map/transpose(jvp(jit(_take)))/scatter-add | solution.py:128
  1084.5 39.9 %all-reduce.2 = (f32[768]{0:T(1024)S(1)}, f32[768]{0:T(1024)S(1)}, f32[768,4]{0,1:T(4,128)S(1)}, f32[32,12]{0,1:T(8,128)S(1)}) all-reduce(f32[768]{0:T(1024)S(1)} %get-tuple-element.14, f32[768]{0:T(1024)} %get-tuple-element.12, f32[768,4]{0,1:T(4,128)S(1)} %fusion.46, ...), channel_id=1, replica_groups=mesh['dp'=16,'tensor'=2] {'dp','tensor'}, use_global_device_ids=true, to_apply=%region_27.28 | all-reduce | flops 4992 | bytes 39936 | tf_op jit(solution)/shard_map/psum | solution.py:309
  (222 shorter events, 108.8 us)
Async XLA Ops:
  7.2 543.9 %copy-start = (bf16[768,384]{1,0:T(8,128)(2,1)S(1)}, bf16[768,384]{1,0:T(8,128)(2,1)}, u32[]{:S(2)}) copy-start(bf16[768,384]{1,0:T(8,128)(2,1)} %param.25) | copy-start | bytes 1769476
  7.2 54.3 %copy-start.30 = (bf16[48,384]{1,0:T(8,128)(2,1)S(1)}, bf16[48,384]{1,0:T(8,128)(2,1)}, u32[]{:S(2)}) copy-start(bf16[48,384]{1,0:T(8,128)(2,1)} %param.17) | copy-start | bytes 110596
  7.2 412.0 %reduce-scatter.9.cloned.1.call-start = ((), (), s32[]{:S(2)}) async-start(), calls=%async_computation.12 | async-start | bytes 589824 | tf_op jit(solution)/shard_map/reduce_scatter | solution.py:153
  10.5 376.4 %copy-start.37 = (f32[256]{0:T(256)}, f32[256]{0:T(256)S(1)}, u32[]{:S(2)}) copy-start(f32[256]{0:T(256)S(1)} %fusion.45) | copy-start | bytes 3076
  12.2 47.2 %copy-start.44 = (f32[128]{0:T(128)}, f32[128]{0:T(128)S(1)}, u32[]{:S(2)}) copy-start(f32[128]{0:T(128)S(1)} %get-tuple-element.34) | copy-start | bytes 1540
  81.7 299.8 %copy-start.16 = (bf16[256,384]{0,1:T(8,128)(2,1)}, bf16[256,384]{0,1:T(8,128)(2,1)S(1)}, u32[]{:S(2)}) copy-start(bf16[256,384]{0,1:T(8,128)(2,1)S(1)} %copy.61) | copy-start | bytes 589828
  104.2 277.3 %copy-start.18 = (bf16[256,384]{0,1:T(8,128)(2,1)}, bf16[256,384]{0,1:T(8,128)(2,1)S(1)}, u32[]{:S(2)}) copy-start(bf16[256,384]{0,1:T(8,128)(2,1)S(1)} %copy.62) | copy-start | bytes 589828
  145.7 241.2 %copy-start.10 = (bf16[768,384]{1,0:T(8,128)(2,1)}, bf16[768,384]{1,0:T(8,128)(2,1)S(1)}, u32[]{:S(2)}) copy-start(bf16[768,384]{1,0:T(8,128)(2,1)S(1)} %all_gather.38) | copy-start | bytes 1769476
  456.8 43.2 %all-to-all-start.2 = ((bf16[16,80,768]{2,1,0:T(8,128)(2,1)}), bf16[16,80,768]{2,1,0:T(8,128)(2,1)}, u32[]{:S(2)}, u32[]{:S(2)}) async-start(bf16[16,80,768]{2,1,0:T(8,128)(2,1)} %bitcast.124), calls=%async_computation.4 | async-start | bytes 3932160 | tf_op jit(solution)/shard_map/all_to_all | solution.py:212
  501.5 49.6 %all-to-all-start = ((bf16[16,80,768]{2,1,0:T(8,128)(2,1)}), bf16[16,80,768]{2,1,0:T(8,128)(2,1)}, u32[]{:S(2)}, u32[]{:S(2)}) async-start(bf16[16,80,768]{2,1,0:T(8,128)(2,1)} %bitcast.125), calls=%async_computation.1 | async-start | bytes 3932160 | tf_op jit(solution)/shard_map/all_to_all | solution.py:191
  559.4 49.6 %all-to-all-start.1 = ((bf16[16,80,768]{2,1,0:T(8,128)(2,1)}), bf16[16,80,768]{2,1,0:T(8,128)(2,1)}, u32[]{:S(2)}, u32[]{:S(2)}) async-start(bf16[16,80,768]{2,1,0:T(8,128)(2,1)} %bitcast.127), calls=%async_computation.2 | async-start | bytes 3932160 | tf_op jit(solution)/shard_map/all_to_all | solution.py:200
  609.0 49.6 %all-to-all-start.3 = ((bf16[16,80,768]{2,1,0:T(8,128)(2,1)}), bf16[16,80,768]{2,1,0:T(8,128)(2,1)}, u32[]{:S(2)}, u32[]{:S(2)}) async-start(bf16[16,80,768]{2,1,0:T(8,128)(2,1)} %bitcast.126), calls=%async_computation.5 | async-start | bytes 3932160 | tf_op jit(solution)/shard_map/all_to_all | solution.py:225
  619.7 44.6 %reduce-scatter.11.cloned.1.call-start = ((), (), s32[]{:S(2)}) async-start(), calls=%async_computation.13 | async-start | bytes 589824 | tf_op jit(solution)/shard_map/reduce_scatter | solution.py:204
  624.8 58.2 %reduce-scatter.13.cloned.1.call-start = ((), (), s32[]{:S(2)}) async-start(), calls=%async_computation.14 | async-start | bytes 589824 | tf_op jit(solution)/shard_map/reduce_scatter | solution.py:229
  663.7 419.6 %reduce-scatter.15.cloned.1.call-start = ((), (), s32[]{:S(2)}) async-start(), calls=%async_computation.15 | async-start | bytes 589824 | tf_op jit(solution)/shard_map/reduce_scatter | solution.py:286
  703.9 424.9 %reduce-scatter.23.cloned.1.call-start = ((), (), s32[]{:S(2)}) async-start(), calls=%async_computation.19 | async-start | bytes 1253376 | tf_op jit(solution)/shard_map/reduce_scatter | solution.py:301
  705.5 423.3 %reduce-scatter.21.cloned.1.call-start = ((), (), s32[]{:S(2)}) async-start(), calls=%async_computation.18 | async-start | bytes 1253376 | tf_op jit(solution)/shard_map/reduce_scatter | solution.py:298
  707.0 421.8 %reduce-scatter.19.cloned.1.call-start = ((), (), s32[]{:S(2)}) async-start(), calls=%async_computation.17 | async-start | bytes 1253376 | tf_op jit(solution)/shard_map/reduce_scatter | solution.py:295
  708.5 420.4 %reduce-scatter.17.cloned.1.call-start = ((), (), s32[]{:S(2)}) async-start(), calls=%async_computation.16 | async-start | bytes 1253376 | tf_op jit(solution)/shard_map/reduce_scatter | solution.py:292
  718.0 363.9 %copy-start.46 = (s32[511]{0:T(512)S(1)}, s32[511]{0:T(512)}, u32[]{:S(2)}) copy-start(s32[511]{0:T(512)} %param.29) | copy-start | bytes 6136
  718.0 364.5 %copy-start.22 = (bf16[128,768]{1,0:T(8,128)(2,1)S(1)}, bf16[128,768]{1,0:T(8,128)(2,1)}, u32[]{:S(2)}) copy-start(bf16[128,768]{1,0:T(8,128)(2,1)} %copy-done.21) | copy-start | bytes 589828
  718.0 408.9 %copy-start.26 = (f32[128,768]{1,0:T(8,128)S(1)}, f32[128,768]{1,0:T(8,128)}, u32[]{:S(2)}) copy-start(f32[128,768]{1,0:T(8,128)} %copy-done.25) | copy-start | bytes 1179652
  718.0 408.9 %copy-start.29 = (bf16[128,768]{1,0:T(8,128)(2,1)S(1)}, bf16[128,768]{1,0:T(8,128)(2,1)}, u32[]{:S(2)}) copy-start(bf16[128,768]{1,0:T(8,128)(2,1)} %reduce-scatter.11.cloned.1.call-done) | copy-start | bytes 589828
  718.0 410.9 %copy-start.1 = (bf16[768,384]{1,0:T(8,128)(2,1)S(1)}, bf16[768,384]{1,0:T(8,128)(2,1)}, u32[]{:S(2)}) copy-start(bf16[768,384]{1,0:T(8,128)(2,1)} %param.25) | copy-start | bytes 1769476
  (39 other events, 379.0 us)
Sparse Core Ops, SparseCore 0:
  389.2 10.4 reduce-scatter.8
  624.9 14.4 reduce-scatter.10
  663.8 19.1 reduce-scatter.12
  704.1 13.1 reduce-scatter.14
  721.3 58.0 reduce-scatter.22
  783.4 57.0 reduce-scatter.20
  844.7 57.0 reduce-scatter.18
  906.0 57.1 reduce-scatter.16
where the time goes:
time: 1140 us
  other arithmetic  372 us (33%)
  local copies, waits for them, and re-layouts  326 us (29%)
  blocking collectives  201 us (18%)
  waiting for transfers between devices  136 us (12%)
  matrix products  47.1 us (4%)
  starting transfers between devices  36.9 us (3%)
  between operations  16.8 us (1%)
    scatter-add x1, other arithmetic, expand_bias(): return jnp.take(head_rows, offset, axis=1)  347 us
    gather x2, local copies, waits for them, and re-layouts, expand_bias(): return jnp.take(head_rows, offset, axis=1)  236 us
    scatter x2, local copies, waits for them, and re-layouts, dispatch(): placed = placed.at[expert_routing, capacity_index].set(row_data)  47.4 us
    psum x1, blocking collectives, body(): lax.psum((grad_attn_gain, grad_moe_gain, grad_router, table_full), ('dp',...  39.9 us
    unnamed x1, blocking collectives  35.5 us
    all_to_all x1, waiting for transfers between devices, body(): lax.all_to_all(expert_out.astype(jnp.bfloat16), 'dp', split_axis=0, conca...  35.2 us
    all_to_all x1, waiting for transfers between devices, body(): lax.all_to_all(dispatch(seq_mixed), 'dp', split_axis=0, concat_axis=0, ti...  34.8 us
    all_to_all x1, waiting for transfers between devices, body(): lax.all_to_all(grad_back.astype(jnp.bfloat16), 'dp', split_axis=0, concat...  33.8 us
  transfers between devices with their start and end apart: 12, of which 5 were waited for; matrix products, arithmetic and copies ran while one was open for 38% of the time, Pallas kernels for 0%

commit v1 on v0

v1 whole, which is shorter than its diff:
```python
import jax
import jax.numpy as jnp
from jax import lax
from jax.experimental import pallas as pl
from jax.experimental.pallas import tpu as pltpu
from jax.sharding import PartitionSpec as P

HEAD_DIM = 64
SPLIT = 4
EPSILON = 1e-06
MASKED_SCORE = -1e30
LANES = 128
SCORE_SCALE = HEAD_DIM ** (-0.5)
HIGHEST = lax.Precision.HIGHEST
VMEM_BYTES = 50 * 1024 * 1024
F32 = jnp.float32
BF16 = jnp.bfloat16

Z_AT, X_AT, C_AT, Y_AT, FIRST_AT, SECOND_AT = range(6)


def matmul(left, right, precision=None):
    return jnp.dot(left, right, precision=precision, preferred_element_type=F32)


def matmul_nt(left, right, precision=None):
    return lax.dot_general(
        left, right, (((1,), (1,)), ((), ())), precision=precision, preferred_element_type=F32
    )


def matmul_tn(left, right, precision=None):
    return lax.dot_general(
        left, right, (((0,), (0,)), ((), ())), precision=precision, preferred_element_type=F32
    )


def iota(shape, dim):
    return lax.broadcasted_iota(jnp.int32, shape, dim)


def shape_of(shape, dtype):
    return jax.ShapeDtypeStruct(shape, dtype)


def run(kernel, scalars, operands, outs, scratch=(), flops=0):
    moved = sum(x.size * x.dtype.itemsize for x in list(operands) + list(outs))
    return pl.pallas_call(
        kernel,
        out_shape=list(outs),
        in_specs=[pl.BlockSpec(memory_space=pltpu.SMEM)]
        + [pl.BlockSpec(memory_space=pltpu.VMEM)] * len(operands),
        out_specs=[pl.BlockSpec(memory_space=pltpu.VMEM)] * len(outs),
        scratch_shapes=list(scratch),
        compiler_params=pltpu.CompilerParams(vmem_limit_bytes=VMEM_BYTES),
        cost_estimate=pl.CostEstimate(flops=flops, bytes_accessed=moved, transcendentals=0),
    )(scalars, *operands)


def inverse_rms(values):
    return lax.rsqrt(jnp.mean(values * values, axis=-1, keepdims=True) + EPSILON)


def router_softmax(rows, router, expert_count):
    logits = matmul(rows, router)
    logits = jnp.where(iota(logits.shape, 1) < expert_count, logits, MASKED_SCORE)
    weights = jnp.exp(logits - jnp.max(logits, axis=-1, keepdims=True))
    return weights / jnp.sum(weights, axis=-1, keepdims=True)


def swap(values, axis, mask):
    count = lax.axis_size(axis)
    return lax.ppermute(values, axis, [(i, i ^ mask) for i in range(count)])


def stacked(pieces):
    parts = [piece[...].astype(F32) for piece in pieces]
    return parts[0] if len(parts) == 1 else jnp.concatenate(parts, axis=0)


def store_pieces(refs, values):
    rows = values.shape[0] // len(refs)
    for number, ref in enumerate(refs):
        ref[...] = values[number * rows : (number + 1) * rows].astype(ref.dtype)


def body(
    tokens,
    cotangent,
    query_weight,
    key_weight,
    value_weight,
    output_weight,
    attention_scale,
    expert_scale,
    router,
    bucket_bias,
    expert_up_weight,
    expert_down_weight,
    routes,
    lengths,
    buckets,
):
    row_count, width = tokens.shape
    block_len = routes.shape[0]
    expert_count = router.shape[1]
    bucket_count, local_heads = bucket_bias.shape
    head_width = local_heads * HEAD_DIM
    capacity = max(2, block_len * 5 // (4 * expert_count))
    half = (capacity + 1) // 2
    slot_rows = expert_count * half
    data_count = lax.axis_size("dp")
    shard_rows = width // data_count
    hidden_local = expert_up_weight.shape[1]
    tensor_count = lax.axis_size("tensor")
    span = 2 * block_len

    data_index = lax.axis_index("dp")
    z_index = data_index // SPLIT
    x_index = (data_index // 2) % 2
    c_index = data_index % 2
    y_index = lax.axis_index("tensor")
    scalars = jnp.stack(
        [z_index, x_index, c_index, y_index, lengths[0, 0], lengths[0, 1]]
    ).astype(jnp.int32)

    staged = shard_rows % 16 == 0
    slot_pieces = expert_count if half % 8 == 0 else 1
    z_masks = [j * SPLIT for j in range(expert_count)]

    def over_z(pieces):
        if len(pieces) == 1:
            stack = pieces[0].reshape((expert_count, half) + pieces[0].shape[1:])
            moved = [stack[0]] + [swap(stack[j], "dp", z_masks[j]) for j in range(1, expert_count)]
            return [jnp.concatenate(moved, axis=0)]
        return [pieces[0]] + [swap(pieces[j], "dp", z_masks[j]) for j in range(1, expert_count)]

    small_columns = -(-(expert_count + 2) // LANES) * LANES
    weight_columns = 4 * head_width
    packed = jnp.concatenate(
        [
            query_weight,
            key_weight,
            value_weight,
            output_weight,
            router,
            attention_scale[:, None],
            expert_scale[:, None],
            jnp.zeros((shard_rows, small_columns - expert_count - 2), BF16),
        ],
        axis=1,
    )
    if staged:
        gathered = [packed] + [swap(packed, "dp", mask) for mask in z_masks[1:]]
        gathered = gathered + [swap(piece, "dp", 2) for piece in gathered]
        gathered = gathered + [swap(piece, "dp", 1) for piece in gathered]
    else:
        gathered = [lax.all_gather(packed, "dp", axis=0, tiled=True)]

    def piece_offset(idx, number):
        j_z = number % expert_count
        j_x = (number // expert_count) % 2
        j_c = number // (2 * expert_count)
        index = (idx[Z_AT] ^ j_z) * SPLIT + (idx[X_AT] ^ j_x) * 2 + (idx[C_AT] ^ j_c)
        return pl.multiple_of(index * shard_rows, 16)

    tokens_other = swap(tokens, "tensor", 1)
    cotangent_other = swap(cotangent, "tensor", 1)

    def spread(weight):
        over_y = swap(weight, "tensor", 1)
        return [weight, over_y, swap(weight, "dp", 1), swap(over_y, "dp", 1)]

    up_parts = spread(expert_up_weight)
    down_parts = spread(expert_down_weight)

    bucket_row = jnp.pad(buckets, (0, span - buckets.shape[0]), constant_values=-1)[None, :]
    bucket_back = jnp.pad(buckets[::-1], (0, span - buckets.shape[0]), constant_values=-1)[None, :]
    table_rows = jnp.pad(bucket_bias.T, ((0, 8 - local_heads), (0, 0)))
    route_row = routes.reshape(1, block_len)

    def live_row(idx):
        position = iota((1, block_len), 1)
        return (position < idx[FIRST_AT] + idx[SECOND_AT]).astype(F32)

    def live_column(idx):
        position = iota((block_len, 1), 0)
        return (position < idx[FIRST_AT] + idx[SECOND_AT]).astype(F32)

    def prepare(idx, bucket_ref, table_ref, route_ref, tok, tok_other, cot, cot_other, *refs):
        x_ref, bias_ref, own_ref, other_ref, xs_ref, gs_ref, live_ref, pick_ref = refs[:8]
        live_parts = refs[8:-1]
        cot_full = refs[-1]
        own_at = pl.multiple_of(idx[Y_AT] * row_count, row_count)
        other_at = pl.multiple_of((1 - idx[Y_AT]) * row_count, row_count)
        x_ref[pl.ds(own_at, row_count), :] = tok[...]
        x_ref[pl.ds(other_at, row_count), :] = tok_other[...]
        cot_full[pl.ds(own_at, row_count), :] = cot[...]
        cot_full[pl.ds(other_at, row_count), :] = cot_other[...]

        first, active = idx[FIRST_AT], idx[FIRST_AT] + idx[SECOND_AT]

        def segment(position):
            return jnp.where(position < first, 0, jnp.where(position < active, 1, 2))

        allowed = segment(iota((block_len, block_len), 0)) == segment(
            iota((block_len, block_len), 1)
        )
        pick = (bucket_ref[...] == iota((bucket_count, span), 0)).astype(F32)
        head_table = matmul(table_ref[...], pick, HIGHEST)
        for head in range(local_heads):
            line = jnp.broadcast_to(head_table[head : head + 1, :], (block_len, span))
            turned = pltpu.roll(line, block_len + 1, 1, stride=1, stride_axis=0)
            bias_ref[head] = jnp.where(allowed, turned[:, :block_len], MASKED_SCORE)

        route = route_ref[...]
        chosen = (route == iota((LANES, block_len), 0)).astype(F32)
        earlier = (iota((block_len, block_len), 0) < iota((block_len, block_len), 1)).astype(F32)
        counts = matmul(chosen.astype(BF16), earlier.astype(BF16))
        slot = jnp.sum(chosen * counts, axis=0, keepdims=True).astype(jnp.int32)
        row_id = iota((slot_rows, block_len), 0)

        def selection(which):
            place = slot - half * which
            code = (route ^ idx[Z_AT]) * half + place
            code = jnp.where((place >= 0) & (place < half), code, -1)
            return (row_id == code).astype(F32)

        own_select = selection(idx[Y_AT])
        own_bf = own_select.astype(BF16)
        own_ref[...] = own_bf
        other_ref[...] = selection(1 - idx[Y_AT]).astype(BF16)
        xs_ref[...] = matmul(own_bf, x_ref[...]).astype(BF16)
        gs_ref[...] = matmul(own_bf, cot_full[...]).astype(BF16)
        live_select = own_select * live_row(idx)
        live_ref[...] = jnp.broadcast_to(
            jnp.sum(live_select, axis=1, keepdims=True), live_ref.shape
        )
        pick_ref[...] = matmul_nt(own_bf, chosen.astype(BF16))
        store_pieces(live_parts, matmul(live_select.astype(BF16), cot_full[...]))

    piece_shape = shape_of((slot_rows // slot_pieces, width), BF16)
    prepared = run(
        prepare,
        scalars,
        [bucket_row, table_rows, route_row, tokens, tokens_other, cotangent, cotangent_other],
        [
            shape_of((block_len, width), BF16),
            shape_of((local_heads, block_len, block_len), F32),
            shape_of((slot_rows, block_len), BF16),
            shape_of((slot_rows, block_len), BF16),
            shape_of((slot_rows, width), BF16),
            shape_of((slot_rows, width), BF16),
            shape_of((slot_rows, LANES), F32),
            shape_of((slot_rows, LANES), F32),
        ]
        + [piece_shape] * slot_pieces,
        [pltpu.VMEM((block_len, width), BF16)],
        flops=10**9,
    )
    x_full, bias, own_select, other_select, x_slot, g_slot, live_slot, pick_slot = prepared[:8]
    g_home = prepared[8:]

    def to_experts(pieces):
        arrived = over_z(list(pieces))
        return arrived + [swap(piece, "dp", 2) for piece in arrived]

    g_rows = to_experts(g_home)

    qkv_width = 3 * head_width
    piece_count = len(gathered)

    def attend(idx, x_ref, bias_ref, own_ref, other_ref, xs_ref, *refs):
        pieces = refs[:piece_count]
        (
            send_ref,
            keep_ref,
            normed_ref,
            qkv_ref,
            probs_ref,
            context_ref,
            weight_ref,
            small_ref,
            gain_ref,
        ) = refs[piece_count:]
        if piece_count == 1:
            weight_ref[...] = pieces[0][:, :weight_columns]
            small_ref[...] = pieces[0][:, weight_columns:]
        else:
            for number, piece in enumerate(pieces):
                at = piece_offset(idx, number)
                weight_ref[pl.ds(at, shard_rows), :] = piece[:, :weight_columns]
                small_ref[pl.ds(at, shard_rows), :] = piece[:, weight_columns:]
        turned = small_ref[...].astype(F32).T
        gain = turned[expert_count : expert_count + 1, :]
        gain_ref[...] = jnp.broadcast_to(gain, gain_ref.shape)
        gain_ref[1:2, :] = turned[expert_count + 1 : expert_count + 2, :]
        x = x_ref[...].astype(F32)
        normed = (x * inverse_rms(x) * gain).astype(BF16)
        normed_ref[...] = normed
        qkv_ref[...] = matmul(normed, weight_ref[:, :qkv_width]).astype(BF16)
        live = live_column(idx)
        for head in range(local_heads):
            at = head * HEAD_DIM
            query = qkv_ref[:, at : at + HEAD_DIM]
            key = qkv_ref[:, head_width + at : head_width + at + HEAD_DIM]
            value = qkv_ref[:, 2 * head_width + at : 2 * head_width + at + HEAD_DIM]
            scores = matmul_nt(query, key) * SCORE_SCALE + bias_ref[head]
            weights = jnp.exp(scores - jnp.max(scores, axis=-1, keepdims=True))
            probs = weights / jnp.sum(weights, axis=-1, keepdims=True)
            probs_ref[head] = probs
            context = matmul(probs.astype(BF16), value) * live
            context_ref[:, at : at + HEAD_DIM] = context.astype(BF16)
        out = matmul_nt(context_ref[...], weight_ref[:, qkv_width:]).astype(BF16)
        send_ref[...] = matmul(other_ref[...], out).astype(BF16)
        keep_ref[...] = matmul(own_ref[...], out) + xs_ref[...].astype(F32)

    send, keep, normed, qkv, probs, context, weights, router_small, gains = run(
        attend,
        scalars,
        [x_full, bias, own_select, other_select, x_slot] + gathered,
        [
            shape_of((slot_rows, width), BF16),
            shape_of((slot_rows, width), F32),
            shape_of((block_len, width), BF16),
            shape_of((block_len, qkv_width), BF16),
            shape_of((local_heads, block_len, block_len), F32),
            shape_of((block_len, head_width), BF16),
            shape_of((width, weight_columns), BF16),
            shape_of((width, small_columns), BF16),
            shape_of((8, width), F32),
        ],
        flops=10**9,
    )
    arrived = swap(send, "tensor", 1)

    def second_norm(idx, keep_ref, arrived_ref, gain_ref, residual_ref, scale_ref, nm_ref, *parts):
        residual = keep_ref[...] + arrived_ref[...].astype(F32)
        scale = inverse_rms(residual)
        residual_ref[...] = residual
        scale_ref[...] = jnp.broadcast_to(scale, scale_ref.shape)
        rows = residual * scale * gain_ref[1:2, :]
        nm_ref[...] = rows.astype(BF16)
        store_pieces(parts, rows)

    residual, scale_moe, normed_moe, *row_home = run(
        second_norm,
        scalars,
        [keep, arrived, gains],
        [
            shape_of((slot_rows, width), F32),
            shape_of((slot_rows, LANES), F32),
            shape_of((slot_rows, width), BF16),
        ]
        + [piece_shape] * slot_pieces,
        flops=10**6,
    )
    expert_rows = to_experts(row_home)

    expert_in = 2 * slot_rows
    parts = len(up_parts)

    def experts(idx, router_ref, *refs):
        count = 2 * slot_pieces
        row_parts, refs = refs[:count], refs[count:]
        g_parts, refs = refs[:count], refs[count:]
        up, refs = refs[:parts], refs[parts:]
        down, refs = refs[:parts], refs[parts:]
        send_ref, keep_ref, rows_ref, total_ref, hidden_ref, pre_ref = refs
        rows = stacked(row_parts).astype(BF16)
        rows_ref[...] = rows
        routed = router_softmax(rows, router_ref[...], expert_count)
        mine = (iota(routed.shape, 1) == idx[Z_AT]).astype(F32)
        gate = jnp.sum(routed * mine, axis=1, keepdims=True)
        total = (stacked(g_parts) * gate).astype(BF16)
        total_ref[...] = total
        forward = jnp.zeros((expert_in, width), F32)
        backward = jnp.zeros((expert_in, width), F32)
        for part in range(parts):
            at = part * hidden_local
            pre = matmul(rows, up[part][...])
            square = pre * pre
            inner = 0.7978845608028654 * pre * (1.0 + 0.044715 * square)
            tanh = jnp.tanh(inner)
            hidden = (0.5 * pre * (1.0 + tanh)).astype(BF16)
            slope = 0.5 * (1.0 + tanh) + 0.5 * pre * (1.0 - tanh * tanh) * (
                0.7978845608028654 * (1.0 + 3.0 * 0.044715 * square)
            )
            hidden_ref[:, at : at + hidden_local] = hidden
            grad_pre = (matmul(total, down[part][...]) * slope).astype(BF16)
            pre_ref[:, at : at + hidden_local] = grad_pre
            forward += matmul_nt(hidden, down[part][...])
            backward += matmul_nt(grad_pre, up[part][...])
        keep_ref[:, :width] = forward[:slot_rows]
        keep_ref[:, width:] = backward[:slot_rows]
        send_ref[:, :width] = forward[slot_rows:].astype(BF16)
        send_ref[:, width:] = backward[slot_rows:].astype(BF16)

    send, keep, rows_in, total_in, hidden, grad_pre = run(
        experts,
        scalars,
        [router_small] + expert_rows + g_rows + up_parts + down_parts,
        [
            shape_of((slot_rows, 2 * width), BF16),
            shape_of((slot_rows, 2 * width), F32),
            shape_of((expert_in, width), BF16),
            shape_of((expert_in, width), BF16),
            shape_of((expert_in, parts * hidden_local), BF16),
            shape_of((expert_in, parts * hidden_local), BF16),
        ],
        flops=3 * 10**9,
    )
    arrived = swap(send, "dp", 2)

    def add_x(idx, keep_ref, arrived_ref, *parts_out):
        store_pieces(parts_out, keep_ref[...] + arrived_ref[...].astype(F32))

    both_shape = shape_of((slot_rows // slot_pieces, 2 * width), BF16)
    back = run(add_x, scalars, [keep, arrived], [both_shape] * slot_pieces, flops=10**6)
    home = over_z(list(back))

    def expert_grads(idx, rows_ref, total_ref, hidden_ref, pre_ref, *outs):
        for part in range(parts):
            at = part * hidden_local
            up_grad, down_grad = outs[2 * part : 2 * part + 2]
            up_grad[...] = matmul_tn(rows_ref[...], pre_ref[:, at : at + hidden_local]).astype(
                up_grad.dtype
            )
            down_grad[...] = matmul_tn(
                total_ref[...], hidden_ref[:, at : at + hidden_local]
            ).astype(down_grad.dtype)

    weight_shape = (width, hidden_local)
    weight_grads = run(
        expert_grads,
        scalars,
        [rows_in, total_in, hidden, grad_pre],
        [shape_of(weight_shape, F32)] * 2 + [shape_of(weight_shape, BF16)] * (2 * parts - 2),
        flops=2 * 10**9,
    )

    def scatter_expert(own, over_y, over_c, over_yc):
        from_c = swap(over_c, "dp", 1)
        from_yc = swap(over_yc, "dp", 1)
        passed = (over_y.astype(F32) + from_yc.astype(F32)).astype(BF16)
        return own + from_c.astype(F32) + swap(passed, "tensor", 1).astype(F32)

    grad_w_in = scatter_expert(*weight_grads[0::2])
    grad_w_out = scatter_expert(*weight_grads[1::2])

    expert_pad = -(-expert_count // 8) * 8

    def at_home(idx, *refs):
        pieces, refs = refs[:slot_pieces], refs[slot_pieces:]
        (
            residual_ref,
            scale_ref,
            nm_ref,
            g_ref,
            live_ref,
            pick_ref,
            gain_ref,
            router_ref,
            mid_ref,
            layer_ref,
            gain_out,
            router_out,
        ) = refs
        returned = stacked(pieces)
        total, back_rows = returned[:, :width], returned[:, width:]
        residual = residual_ref[...]
        scale = scale_ref[:, :1]
        live = live_ref[:, :1]
        pick = pick_ref[...]
        gain = gain_ref[1:2, :]
        g = g_ref[...].astype(F32)
        routed = router_softmax(nm_ref[...], router_ref[...], expert_count)
        gate = jnp.sum(routed * pick, axis=1, keepdims=True)
        layer_ref[...] = (residual + gate * total * live).astype(BF16)
        grad_gate = jnp.sum(g * total, axis=1, keepdims=True) * live
        grad_logits = grad_gate * gate * (pick - routed)
        upstream = back_rows + matmul_nt(grad_logits, router_ref[...].astype(F32), HIGHEST)
        scaled = upstream * gain
        grad_mid = (
            g
            + scale * scaled
            - residual * scale**3 * jnp.mean(scaled * residual, axis=-1, keepdims=True)
        )
        mid_ref[...] = grad_mid.astype(BF16)
        gain_out[...] = jnp.broadcast_to(
            jnp.sum(upstream * residual * scale, axis=0, keepdims=True), gain_out.shape
        )
        router_grad = matmul_tn(grad_logits, nm_ref[...].astype(F32), HIGHEST)
        router_out[...] = router_grad[:expert_pad]

    mid_own, layer_own, gain_moe, router_part = run(
        at_home,
        scalars,
        home
        + [residual, scale_moe, normed_moe, g_slot, live_slot, pick_slot, gains, router_small],
        [
            shape_of((slot_rows, width), BF16),
            shape_of((slot_rows, width), BF16),
            shape_of((8, width), F32),
            shape_of((expert_pad, width), F32),
        ],
        flops=10**8,
    )
    mid_other = swap(mid_own, "tensor", 1)
    layer_other = swap(layer_own, "tensor", 1)

    half_pieces = 2 * expert_count

    def emit_rows(idx, full_ref, outs):
        if not staged:
            outs[0][...] = full_ref[...].astype(BF16)
            return
        keep_ref, send_ref = outs
        for number in range(half_pieces):
            at = piece_offset(idx, number)
            keep_ref[number] = full_ref[pl.ds(at, shard_rows), :]
            at = piece_offset(idx, number + half_pieces)
            send_ref[number] = full_ref[pl.ds(at, shard_rows), :].astype(BF16)

    def row_shapes(columns):
        if not staged:
            return [shape_of((width, columns), BF16)]
        return [
            shape_of((half_pieces, shard_rows, columns), F32),
            shape_of((half_pieces, shard_rows, columns), BF16),
        ]

    def reduce_rows(outs):
        if not staged:
            return lax.psum_scatter(
                outs[0].astype(F32), "dp", scatter_dimension=0, tiled=True
            )
        held, send = outs
        held = held + swap(send, "dp", 1).astype(F32)
        held = held[:expert_count] + swap(
            held[expert_count:].astype(BF16), "dp", 2
        ).astype(F32)
        total = held[0]
        for j in range(1, expert_count):
            total = total + swap(held[j].astype(BF16), "dp", z_masks[j]).astype(F32)
        return total

    def output_grad(idx, own_ref, other_ref, mid_ref, mid_other_ref, context_ref, ga_ref, *refs):
        full = refs[-1]
        grad = matmul_tn(own_ref[...], mid_ref[...]) + matmul_tn(
            other_ref[...], mid_other_ref[...]
        )
        grad = grad.astype(BF16)
        ga_ref[...] = grad
        full[...] = matmul_tn(grad, context_ref[...])
        emit_rows(idx, full, refs[:-1])

    grad_attention, *output_rows = run(
        output_grad,
        scalars,
        [own_select, other_select, mid_own, mid_other, context],
        [shape_of((block_len, width), BF16)] + row_shapes(head_width),
        [pltpu.VMEM((width, head_width), F32)],
        flops=4 * 10**8,
    )
    grad_wo = reduce_rows(output_rows)

    def attend_back(
        idx, ga_ref, weight_ref, qkv_ref, probs_ref, normed_ref, x_ref, bucket_ref, *refs
    ):
        keep_ref, send_ref, gain_ref, table_ref = refs[:4]
        outs = refs[4:-3]
        grads, full, upstream = refs[-3:]
        live = live_column(idx)
        grad_context = matmul(ga_ref[...], weight_ref[:, qkv_width:]) * live
        grad_context = grad_context.astype(BF16)
        mirror = (
            iota((block_len, block_len), 0) + iota((block_len, block_len), 1) == block_len - 1
        ).astype(BF16)
        lines = []
        for head in range(local_heads):
            at = head * HEAD_DIM
            query = qkv_ref[:, at : at + HEAD_DIM]
            key = qkv_ref[:, head_width + at : head_width + at + HEAD_DIM]
            value = qkv_ref[:, 2 * head_width + at : 2 * head_width + at + HEAD_DIM]
            back = grad_context[:, at : at + HEAD_DIM]
            probs = probs_ref[head]
            grad_value = matmul_tn(probs.astype(BF16), back)
            grad_probs = matmul_nt(back, value)
            grad_scores = probs * (
                grad_probs - jnp.sum(probs * grad_probs, axis=-1, keepdims=True)
            )
            grad_scores = grad_scores.astype(BF16)
            grad_query = matmul(grad_scores, key) * SCORE_SCALE
            grad_key = matmul_tn(grad_scores, query) * SCORE_SCALE
            grads[:, at : at + HEAD_DIM] = grad_query.astype(BF16)
            grads[:, head_width + at : head_width + at + HEAD_DIM] = grad_key.astype(BF16)
            grads[:, 2 * head_width + at : 2 * head_width + at + HEAD_DIM] = grad_value.astype(
                BF16
            )
            lines_left = jnp.concatenate(
                [matmul(grad_scores, mirror), jnp.zeros((block_len, span - block_len), F32)], axis=1
            )
            rows = block_len
            while rows > 8:
                rows //= 2
                lines_left = lines_left[:rows] + pltpu.roll(lines_left[rows:], rows, 1)
            lines_left = pltpu.roll(lines_left, 0, 1, stride=1, stride_axis=0)
            lines.append(jnp.sum(lines_left, axis=0, keepdims=True))
        lines.append(jnp.zeros((8 - local_heads, span), F32))
        diagonal = jnp.concatenate(lines, axis=0)
        pick = (bucket_ref[...] == iota((LANES, span), 0)).astype(F32)
        table = matmul_nt(diagonal, pick, HIGHEST)
        table_ref[...] = jnp.zeros(table_ref.shape, F32)
        for head in range(local_heads):
            table_ref[:1, head * LANES : (head + 1) * LANES] = table[head : head + 1, :]
        all_grads = grads[...]
        grad_normed = matmul_nt(all_grads, weight_ref[:, :qkv_width])
        upstream[...] = grad_normed
        x = x_ref[...].astype(F32)
        gain_ref[...] = jnp.broadcast_to(
            jnp.sum(grad_normed * x * inverse_rms(x), axis=0, keepdims=True), gain_ref.shape
        )
        own_at = pl.multiple_of(idx[Y_AT] * row_count, row_count)
        other_at = pl.multiple_of((1 - idx[Y_AT]) * row_count, row_count)
        keep_ref[...] = upstream[pl.ds(own_at, row_count), :]
        send_ref[...] = upstream[pl.ds(other_at, row_count), :].astype(BF16)
        full[...] = matmul_tn(normed_ref[...], all_grads)
        emit_rows(idx, full, outs)

    up_keep, up_send, gain_attn, table_part, *qkv_rows = run(
        attend_back,
        scalars,
        [grad_attention, weights, qkv, probs, normed, x_full, bucket_back],
        [
            shape_of((row_count, width), F32),
            shape_of((row_count, width), BF16),
            shape_of((8, width), F32),
            shape_of((8, local_heads * LANES), F32),
        ]
        + row_shapes(qkv_width),
        [
            pltpu.VMEM((block_len, qkv_width), BF16),
            pltpu.VMEM((width, qkv_width), F32),
            pltpu.VMEM((block_len, width), F32),
        ],
        flops=2 * 10**9,
    )
    up_other = swap(up_send, "tensor", 1)
    grad_qkv = reduce_rows(qkv_rows)

    table_line = jnp.pad(table_part[0], (0, width - local_heads * LANES))
    table_lines = jnp.where(
        jnp.arange(tensor_count)[:, None] == y_index, table_line[None, :], 0.0
    )
    small = jnp.concatenate(
        [gain_attn[:1], gain_moe[:1], router_part[:expert_count], table_lines], axis=0
    )
    small = jnp.pad(small, ((0, -small.shape[0] % 8), (0, 0)))
    small = small + swap(small, "tensor", 1)
    if staged:
        small = small + swap(small, "dp", 1)
        small = small + swap(small, "dp", 2)
        moved = [swap(small, "dp", mask) for mask in z_masks[1:]]
        for piece in moved:
            small = small + piece
    else:
        small = lax.psum(small, "dp")
    shard = lax.dynamic_slice_in_dim(small, data_index * shard_rows, shard_rows, 1)
    table = lax.dynamic_slice_in_dim(small, 2 + expert_count + y_index, 1, 0)
    table = table[0, : local_heads * LANES].reshape(local_heads, LANES)[:, :bucket_count].T

    def finish(
        idx, own_ref, other_ref, layer_ref, layer_other_ref, ga_ref, keep_ref, arrived_ref,
        tok_ref, gain_ref, layer_out, tokens_out, full
    ):
        own_at = pl.multiple_of(idx[Y_AT] * row_count, row_count)
        full[...] = matmul_tn(own_ref[...], layer_ref[...]) + matmul_tn(
            other_ref[...], layer_other_ref[...]
        )
        layer_out[...] = full[pl.ds(own_at, row_count), :].astype(BF16)
        x = tok_ref[...].astype(F32)
        scale = inverse_rms(x)
        scaled = (keep_ref[...] + arrived_ref[...].astype(F32)) * gain_ref[:1, :]
        grad = scale * scaled - x * scale**3 * jnp.mean(scaled * x, axis=-1, keepdims=True)
        grad = grad + ga_ref[pl.ds(own_at, row_count), :].astype(F32)
        tokens_out[...] = grad.astype(BF16)

    layer_out, grad_tokens = run(
        finish,
        scalars,
        [
            own_select, other_select, layer_own, layer_other, grad_attention, up_keep, up_other,
            tokens, gains,
        ],
        [shape_of((row_count, width), BF16)] * 2,
        [pltpu.VMEM((block_len, width), F32)],
        flops=10**8,
    )

    return (
        layer_out,
        grad_tokens,
        grad_qkv[:, :head_width],
        grad_qkv[:, head_width : 2 * head_width],
        grad_qkv[:, 2 * head_width :],
        grad_wo,
        shard[0],
        shard[1],
        shard[2 : 2 + expert_count].T,
        table,
        grad_w_in,
        grad_w_out,
    )


def solution(mesh):
    in_specs = (
        P(("dp", "tensor"), None),
        P(("dp", "tensor"), None),
        P("dp", "tensor"),
        P("dp", "tensor"),
        P("dp", "tensor"),
        P("dp", "tensor"),
        P("dp"),
        P("dp"),
        P("dp", None),
        P(None, "tensor"),
        P(None, ("dp", "tensor")),
        P(None, ("dp", "tensor")),
        P("dp", None),
        P("dp", None),
        P(),
    )
    out_specs = (
        P(("dp", "tensor"), None),
        P(("dp", "tensor"), None),
        P("dp", "tensor"),
        P("dp", "tensor"),
        P("dp", "tensor"),
        P("dp", "tensor"),
        P("dp"),
        P("dp"),
        P("dp", None),
        P(None, "tensor"),
        P(None, ("dp", "tensor")),
        P(None, ("dp", "tensor")),
    )
    return jax.shard_map(body, mesh=mesh, in_specs=in_specs, out_specs=out_specs, check_vma=False)
```

time: 1140 us -> 219 us (0.19)
  other arithmetic: 372 us -> 6.1 us
  local copies, waits for them, and re-layouts: 326 us -> 23.2 us
  blocking collectives: 201 us -> 0 us
  matrix products: 47.1 us -> 0 us
  waiting for transfers between devices: 136 us -> 89.1 us
  Pallas kernels: 0 us -> 35.1 us
  starting transfers between devices: 36.9 us -> 64 us
  between operations: 16.8 us -> 1.04 us
    scatter-add x1 -> x0, other arithmetic: 347 us -> none  [expand_bias(): return jnp.take(head_rows, offset, axis=1)]
    gather x4 -> x0, local copies, waits for them, and re-layouts: 242 us -> none  [the longest x2 236 us: expand_bias(): return jnp.take(head_rows, offset, axis=1)]
    all_gather x9 -> x0, blocking collectives: 126 us -> none  [the longest x1 21.1 us: body(): lax.all_gather(key_weight, 'dp', axis=0, tiled=True)]
    all_to_all x4 -> x0, waiting for transfers between devices: 119 us -> none  [the longest x1 35.2 us: body(): lax.all_to_all(expert_out.astype(jnp.bfloat16), 'dp', split_axis=0, conca...]
    ppermute x0 -> x67, waiting for transfers between devices: none -> 89.1 us  [swap(): return lax.ppermute(values, axis, [(i, i ^ mask) for i in range(count)])]
    ppermute x0 -> x67, starting transfers between devices: none -> 64 us  [swap(): return lax.ppermute(values, axis, [(i, i ^ mask) for i in range(count)])]
    scatter x2 -> x0, local copies, waits for them, and re-layouts: 47.4 us -> none  [dispatch(): placed = placed.at[expert_routing, capacity_index].set(row_data)]
    dot_general x29 -> x0, matrix products: 47.1 us -> none  [the longest x7 14.6 us: contract_rows(): lax.dot_general(left_arr, right_arr, (((0,), (0,)), ((), ())), precision=...]
  transfers between devices with their start and end apart: 12 -> 67, of which waited for: 5 -> 31; matrix products, arithmetic and copies ran while one was open for 38% -> 7% of each run, Pallas kernels for 0% -> 11%
where the time goes in v1:
time: 219 us; the launch traced here: 218 us
  waiting for transfers between devices  89.1 us (41%)
  starting transfers between devices  64 us (29%)
  Pallas kernels  35.1 us (16%)
  local copies, waits for them, and re-layouts  23.2 us (11%)
  other arithmetic  6.1 us (3%)
    ppermute x67, waiting for transfers between devices, swap(): return lax.ppermute(values, axis, [(i, i ^ mask) for i in range(count)])  89.1 us
    ppermute x67, starting transfers between devices, swap(): return lax.ppermute(values, axis, [(i, i ^ mask) for i in range(count)])  64 us
    pallas_call x10, Pallas kernels, run(): pl.pallas_call(kernel, out_shape=list(outs), in_specs=[pl.BlockSpec(memor...  35.1 us
    unnamed x75, local copies, waits for them, and re-layouts  14 us
  transfers between devices with their start and end apart: 67, of which 31 were waited for; matrix products, arithmetic and copies ran while one was open for 7% of the time, Pallas kernels for 11%

profile of v1, /device:TPU:0, one launch (start us, length us, event | category | flops | bytes accessed | tf_op | source)
XLA Modules:
  0.0 218.5 jit_solution(913058211912261656)
XLA Ops:
  0.6 3.0 %collective-permute-start = (bf16[128,768]{1,0:T(8,128)(2,1)}, bf16[128,768]{1,0:T(8,128)(2,1)S(1)}, u32[]{:S(2)}, u32[]{:S(2)}) collective-permute-start(bf16[128,768]{1,0:T(8,128)(2,1)} %tok_ref.1), channel_id=1, source_target_pairs={{0,1},{1,0},{2,3},{3,2},{4,5},{5,4},{6,7},{7,6},{8,9},{9,8},{10,11... | collective-permute-start | bytes 589832 | tf_op jit(solution)/shard_map/ppermute | solution.py:73
  9.0 2.6 %collective-permute-start.3 = (bf16[48,1664]{1,0:T(8,128)(2,1)S(1)}, bf16[48,1664]{1,0:T(8,128)(2,1)S(1)}, u32[]{:S(2)}, u32[]{:S(2)}) collective-permute-start(bf16[48,1664]{1,0:T(8,128)(2,1)S(1)} %concatenate.6.refs_0_), channel_id=1, source_target_pairs={{0,16},{2,18},{4,20},{6,22},{8,24},{10,26},{12,28},{14,30},{16,0},... | collective-permute-start | bytes 479240 | tf_op jit(solution)/shard_map/ppermute | solution.py:73
  11.6 2.8 %collective-permute-done.2.refs_1_ = bf16[48,1664]{1,0:T(8,128)(2,1)S(1)} collective-permute-done((bf16[48,1664]{1,0:T(8,128)(2,1)S(1)}, bf16[48,1664]{1,0:T(8,128)(2,1)S(1)}, u32[]{:S(2)}, u32[]{:S(2)}) %collective-permute-start.2) | collective-permute-done | bytes 159776 | tf_op jit(solution)/shard_map/ppermute | solution.py:73
  26.9 3.7 %collective-permute-start.26 = (bf16[40,768]{1,0:T(8,128)(2,1)S(1)}, bf16[40,768]{1,0:T(8,128)(2,1)S(1)}, u32[]{:S(2)}, u32[]{:S(2)}) collective-permute-start(bf16[40,768]{1,0:T(8,128)(2,1)S(1)} %get-tuple-element.88), channel_id=1, source_target_pairs={{0,16},{2,18},{4,20},{6,22},{8,24},{10,26},{12,28},{14,30},{16,0},... | collective-permute-start | bytes 184328 | tf_op jit(solution)/shard_map/ppermute | solution.py:73
  39.4 2.3 %collective-permute-done.8.refs_7_ = bf16[48,1664]{1,0:T(8,128)(2,1)S(1)} collective-permute-done((bf16[48,1664]{1,0:T(8,128)(2,1)S(1)}, bf16[48,1664]{1,0:T(8,128)(2,1)S(1)}, u32[]{:S(2)}, u32[]{:S(2)}) %collective-permute-start.8) | collective-permute-done | bytes 159776 | tf_op jit(solution)/shard_map/ppermute | solution.py:73
  44.2 3.3 %collective-permute-done.29.refs_13_ = bf16[40,768]{1,0:T(8,128)(2,1)S(1)} collective-permute-done((bf16[40,768]{1,0:T(8,128)(2,1)S(1)}, bf16[40,768]{1,0:T(8,128)(2,1)S(1)}, u32[]{:S(2)}, u32[]{:S(2)}) %collective-permute-start.29) | collective-permute-done | bytes 61472 | tf_op jit(solution)/shard_map/ppermute | solution.py:73
  48.1 4.9 %collective-permute-done.32.refs_17_ = bf16[768,384]{1,0:T(8,128)(2,1)S(1)} collective-permute-done((bf16[768,384]{1,0:T(8,128)(2,1)S(1)}, bf16[768,384]{1,0:T(8,128)(2,1)S(1)}, u32[]{:S(2)}, u32[]{:S(2)}) %collective-permute-start.32) | collective-permute-done | bytes 589856 | tf_op jit(solution)/shard_map/ppermute | solution.py:73
  53.0 10.2 %collective-permute-done.35.refs_21_ = bf16[768,384]{1,0:T(8,128)(2,1)S(1)} collective-permute-done((bf16[768,384]{1,0:T(8,128)(2,1)S(1)}, bf16[768,384]{1,0:T(8,128)(2,1)S(1)}, u32[]{:S(2)}, u32[]{:S(2)}) %collective-permute-start.35) | collective-permute-done | bytes 589856 | tf_op jit(solution)/shard_map/ppermute | solution.py:73
  64.7 5.4 %shard_map.239 = (bf16[160,768]{1,0:T(8,128)(2,1)S(1)}, f32[160,768]{1,0:T(8,128)}, bf16[256,768]{1,0:T(8,128)(2,1)S(1)}, bf16[256,1152]{1,0:T(8,128)(2,1)}, f32...) custom-call(s32[6]{0:T(128)S(1)} %stack.19.idx, ...), custom_call_target="tpu_custom_call" | custom-call | flops 1000000000 | bytes 11001856 | tf_op jit(solution)/shard_map/pallas_call | solution.py:48
  71.0 7.7 %collective-permute-done.17.arrived_ref = bf16[160,768]{1,0:T(8,128)(2,1)S(1)} collective-permute-done((bf16[160,768]{1,0:T(8,128)(2,1)S(1)}, bf16[160,768]{1,0:T(8,128)(2,1)S(1)}, u32[]{:S(2)}, u32[]{:S(2)}) %collective-permute-start.17) | collective-permute-done | bytes 245792 | tf_op jit(solution)/shard_map/ppermute | solution.py:73
  97.5 7.9 %shard_map.241 = (bf16[160,1536]{1,0:T(8,128)(2,1)S(1)}, f32[160,1536]{1,0:T(8,128)}, bf16[320,768]{1,0:T(8,128)(2,1)S(1)}, bf16[320,768]{1,0:T(8,128)(2,1)S(1)}...) custom-call(s32[6]{0:T(128)S(1)} %stack.19.idx, bf16[768,128]{1,0:T(8,128)(2,1)S(1)} %get-tuple-element.78.router_ref.refs_11_, ...), custom_call_target="tpu_custom_call" | custom-call | flops 3000000000 | bytes 10321920 | tf_op jit(solution)/shard_map/pallas_call | solution.py:48
  106.8 8.0 %collective-permute-done.38.arrived_ref = bf16[160,1536]{1,0:T(8,128)(2,1)S(1)} collective-permute-done((bf16[160,1536]{1,0:T(8,128)(2,1)S(1)}, bf16[160,1536]{1,0:T(8,128)(2,1)S(1)}, u32[]{:S(2)}, u32[]{:S(2)}) %collective-permute-start.38) | collective-permute-done | bytes 491552 | tf_op jit(solution)/shard_map/ppermute | solution.py:73
  117.1 2.4 %collective-permute-start.40 = (bf16[40,1536]{1,0:T(8,128)(2,1)S(1)}, bf16[40,1536]{1,0:T(8,128)(2,1)S(1)}, u32[]{:S(2)}, u32[]{:S(2)}) collective-permute-start(bf16[40,1536]{1,0:T(8,128)(2,1)S(1)} %get-tuple-element.94), channel_id=1, source_target_pairs={{0,16},{2,18},{4,20},{6,22},{8,24},{10,26},{12,28},{14,30},{16,0},... | collective-permute-start | bytes 368648 | tf_op jit(solution)/shard_map/ppermute | solution.py:73
  121.6 2.6 %collective-permute-done.40.refs_2_ = bf16[40,1536]{1,0:T(8,128)(2,1)S(1)} collective-permute-done((bf16[40,1536]{1,0:T(8,128)(2,1)S(1)}, bf16[40,1536]{1,0:T(8,128)(2,1)S(1)}, u32[]{:S(2)}, u32[]{:S(2)}) %collective-permute-start.40) | collective-permute-done | bytes 122912 | tf_op jit(solution)/shard_map/ppermute | solution.py:73
  124.2 2.1 collective-permute-done.41.refs_3_
  126.3 2.3 %shard_map.243 = (bf16[160,768]{1,0:T(8,128)(2,1)S(1)}, bf16[160,768]{1,0:T(8,128)(2,1)S(1)}, f32[8,768]{1,0:T(8,128)S(1)}, f32[8,768]{1,0:T(8,128)S(1)}) custom-call(s32[6]{0:T(128)S(1)} %stack.19.idx, bf16[40,1536]{1,0:T(8,128)(2,1)S(1)} %get-tuple-element.92.refs_0_, bf16[40,1536]{1,0:T(8,128)(2,1)S(1)} %collective-permute-done.39.refs_1_, ...), custom_call_target="tpu_custom_call" | custom-call | flops 100000000 | bytes 2482176 | tf_op jit(solution)/shard_map/pallas_call | solution.py:48
  129.0 5.8 %shard_map.247 = (f32[768,384]{1,0:T(8,128)}, f32[768,384]{1,0:T(8,128)}, bf16[768,384]{1,0:T(8,128)(2,1)S(1)}, bf16[768,384]{1,0:T(8,128)(2,1)S(1)}, bf16[768,3...) custom-call(s32[6]{0:T(128)S(1)} %stack.19.idx, ...), custom_call_target="tpu_custom_call" | custom-call | flops 2000000000 | bytes 8847360 | tf_op jit(solution)/shard_map/pallas_call | solution.py:48
  139.0 8.0 %shard_map.245 = (f32[128,768]{1,0:T(8,128)S(1)}, bf16[128,768]{1,0:T(8,128)(2,1)S(1)}, f32[8,768]{1,0:T(8,128)S(1)}, f32[8,768]{1,0:T(8,128)S(1)}, f32[8,48,115...) custom-call(s32[6]{0:T(128)S(1)} %stack.19.idx, bf16[256,768]{1,0:T(8,128)(2,1)S(1)} %get-tuple-element.105.ga_ref, ...), custom_call_target="tpu_custom_call" | custom-call | flops 2000000000 | bytes 8996864 | tf_op jit(solution)/shard_map/pallas_call | solution.py:48
  150.6 2.1 collective-permute-done.55
  167.5 9.8 %collective-permute-done.42.layer_other_ref = bf16[160,768]{1,0:T(8,128)(2,1)S(1)} collective-permute-done((bf16[160,768]{1,0:T(8,128)(2,1)S(1)}, bf16[160,768]{1,0:T(8,128)(2,1)S(1)}, u32[]{:S(2)}, u32[]{:S(2)}) %collective-permute-start.42) | collective-permute-done | bytes 245792 | tf_op jit(solution)/shard_map/ppermute | solution.py:73
  177.3 3.1 %collective-permute-done.44.arrived_ref = bf16[128,768]{1,0:T(8,128)(2,1)S(1)} collective-permute-done((bf16[128,768]{1,0:T(8,128)(2,1)S(1)}, bf16[128,768]{1,0:T(8,128)(2,1)S(1)}, u32[]{:S(2)}, u32[]{:S(2)}) %collective-permute-start.44) | collective-permute-done | bytes 196640 | tf_op jit(solution)/shard_map/ppermute | solution.py:73
  187.3 7.4 %collective-permute-done.66 = bf16[768,384]{1,0:T(8,128)(2,1)S(1)} collective-permute-done((bf16[768,384]{1,0:T(8,128)(2,1)S(1)}, bf16[768,384]{1,0:T(8,128)(2,1)S(1)}, u32[]{:S(2)}, u32[]{:S(2)}) %collective-permute-start.66) | collective-permute-done | bytes 589856 | tf_op jit(solution)/shard_map/ppermute | solution.py:73
  202.9 4.2 %collective-permute-done.46 = bf16[4,48,1152]{2,1,0:T(8,128)(2,1)S(1)} collective-permute-done((bf16[4,48,1152]{2,1,0:T(8,128)(2,1)S(1)}, bf16[4,48,1152]{2,1,0:T(8,128)(2,1)S(1)}, u32[]{:S(2)}, u32[]{:S(2)}) %collective-permute-start.46) | collective-permute-done | bytes 442400 | tf_op jit(solution)/shard_map/ppermute | solution.py:73
  214.0 3.8 %collective-permute-done.48 = bf16[48,1152]{1,0:T(8,128)(2,1)S(1)} collective-permute-done((bf16[48,1152]{1,0:T(8,128)(2,1)S(1)}, bf16[48,1152]{1,0:T(8,128)(2,1)S(1)}, u32[]{:S(2)}, u32[]{:S(2)}) %collective-permute-start.48) | collective-permute-done | bytes 110624 | tf_op jit(solution)/shard_map/ppermute | solution.py:73
  (235 shorter events, 102.2 us)
Async XLA Ops:
  0.6 15.3 %collective-permute-start = (bf16[128,768]{1,0:T(8,128)(2,1)}, bf16[128,768]{1,0:T(8,128)(2,1)S(1)}, u32[]{:S(2)}, u32[]{:S(2)}) collective-permute-start(bf16[128,768]{1,0:T(8,128)(2,1)} %tok_ref.1), channel_id=1, source_target_pairs={{0,1},{1,0},{2,3},{3,2},{4,5},{5,4},{6,7},{7,6},{8,9},{9,8},{10,11... | collective-permute-start | bytes 589832 | tf_op jit(solution)/shard_map/ppermute | solution.py:73
  9.0 17.4 %collective-permute-start.3 = (bf16[48,1664]{1,0:T(8,128)(2,1)S(1)}, bf16[48,1664]{1,0:T(8,128)(2,1)S(1)}, u32[]{:S(2)}, u32[]{:S(2)}) collective-permute-start(bf16[48,1664]{1,0:T(8,128)(2,1)S(1)} %concatenate.6.refs_0_), channel_id=1, source_target_pairs={{0,16},{2,18},{4,20},{6,22},{8,24},{10,26},{12,28},{14,30},{16,0},... | collective-permute-start | bytes 479240 | tf_op jit(solution)/shard_map/ppermute | solution.py:73
  11.6 15.3 %collective-permute-start.4 = (bf16[48,1664]{1,0:T(8,128)(2,1)S(1)}, bf16[48,1664]{1,0:T(8,128)(2,1)S(1)}, u32[]{:S(2)}, u32[]{:S(2)}) collective-permute-start(bf16[48,1664]{1,0:T(8,128)(2,1)S(1)} %concatenate.6.refs_0_), channel_id=1, source_target_pairs={{0,24},{2,26},{4,28},{6,30},{8,16},{10,18},{12,20},{14,22},{16,8},... | collective-permute-start | bytes 479240 | tf_op jit(solution)/shard_map/ppermute | solution.py:73
  14.4 16.2 %collective-permute-start.5 = (bf16[48,1664]{1,0:T(8,128)(2,1)S(1)}, bf16[48,1664]{1,0:T(8,128)(2,1)S(1)}, u32[]{:S(2)}, u32[]{:S(2)}) collective-permute-start(bf16[48,1664]{1,0:T(8,128)(2,1)S(1)} %concatenate.6.refs_0_), channel_id=1, source_target_pairs={{0,4},{2,6},{4,0},{6,2},{8,12},{10,14},{12,8},{14,10},{16,20},{18,... | collective-permute-start | bytes 479240 | tf_op jit(solution)/shard_map/ppermute | solution.py:73
  15.9 14.9 %collective-permute-start.9 = (bf16[48,1664]{1,0:T(8,128)(2,1)S(1)}, bf16[48,1664]{1,0:T(8,128)(2,1)S(1)}, u32[]{:S(2)}, u32[]{:S(2)}) collective-permute-start(bf16[48,1664]{1,0:T(8,128)(2,1)S(1)} %concatenate.6.refs_0_), channel_id=1, source_target_pairs={{0,2},{2,0},{4,6},{6,4},{8,10},{10,8},{12,14},{14,12},{16,18},{18,... | collective-permute-start | bytes 479240 | tf_op jit(solution)/shard_map/ppermute | solution.py:73
  20.0 18.7 %collective-permute-start.6 = (bf16[48,1664]{1,0:T(8,128)(2,1)S(1)}, bf16[48,1664]{1,0:T(8,128)(2,1)S(1)}, u32[]{:S(2)}, u32[]{:S(2)}) collective-permute-start(bf16[48,1664]{1,0:T(8,128)(2,1)S(1)} %collective-permute-done.2.refs_1_), channel_id=1, source_target_pairs={{0,4},{2,6},{4,0},{6,2},{8,12},{10,14},{12,8},{14,10},{16,20},{18,... | collective-permute-start | bytes 479240 | tf_op jit(solution)/shard_map/ppermute | solution.py:73
  36.7 16.3 %collective-permute-start.32 = (bf16[768,384]{1,0:T(8,128)(2,1)S(1)}, bf16[768,384]{1,0:T(8,128)(2,1)S(1)}, u32[]{:S(2)}, u32[]{:S(2)}) collective-permute-start(bf16[768,384]{1,0:T(8,128)(2,1)S(1)} %copy-done.9), channel_id=1, source_target_pairs={{0,1},{1,0},{2,3},{3,2},{4,5},{5,4},{6,7},{7,6},{8,9},{9,8},{10,11... | collective-permute-start | bytes 1769480 | tf_op jit(solution)/shard_map/ppermute | solution.py:73
  36.7 26.4 %collective-permute-start.35 = (bf16[768,384]{1,0:T(8,128)(2,1)S(1)}, bf16[768,384]{1,0:T(8,128)(2,1)S(1)}, u32[]{:S(2)}, u32[]{:S(2)}) collective-permute-start(bf16[768,384]{1,0:T(8,128)(2,1)S(1)} %copy-done.30), channel_id=1, source_target_pairs={{0,1},{1,0},{2,3},{3,2},{4,5},{5,4},{6,7},{7,6},{8,9},{9,8},{10,11... | collective-permute-start | bytes 1769480 | tf_op jit(solution)/shard_map/ppermute | solution.py:73
  47.5 15.6 %collective-permute-start.16 = (bf16[48,1664]{1,0:T(8,128)(2,1)S(1)}, bf16[48,1664]{1,0:T(8,128)(2,1)S(1)}, u32[]{:S(2)}, u32[]{:S(2)}) collective-permute-start(bf16[48,1664]{1,0:T(8,128)(2,1)S(1)} %collective-permute-done.8.refs_7_), channel_id=1, source_target_pairs={{0,2},{2,0},{4,6},{6,4},{8,10},{10,8},{12,14},{14,12},{16,18},{18,... | collective-permute-start | bytes 479240 | tf_op jit(solution)/shard_map/ppermute | solution.py:73
  47.5 36.5 %collective-permute-start.33 = (bf16[768,384]{1,0:T(8,128)(2,1)S(1)}, bf16[768,384]{1,0:T(8,128)(2,1)S(1)}, u32[]{:S(2)}, u32[]{:S(2)}) collective-permute-start(bf16[768,384]{1,0:T(8,128)(2,1)S(1)} %copy-done.9), channel_id=1, source_target_pairs={{0,2},{2,0},{4,6},{6,4},{8,10},{10,8},{12,14},{14,12},{16,18},{18,... | collective-permute-start | bytes 1769480 | tf_op jit(solution)/shard_map/ppermute | solution.py:73
  48.0 37.4 %collective-permute-start.36 = (bf16[768,384]{1,0:T(8,128)(2,1)S(1)}, bf16[768,384]{1,0:T(8,128)(2,1)S(1)}, u32[]{:S(2)}, u32[]{:S(2)}) collective-permute-start(bf16[768,384]{1,0:T(8,128)(2,1)S(1)} %copy-done.30), channel_id=1, source_target_pairs={{0,2},{2,0},{4,6},{6,4},{8,10},{10,8},{12,14},{14,12},{16,18},{18,... | collective-permute-start | bytes 1769480 | tf_op jit(solution)/shard_map/ppermute | solution.py:73
  53.0 43.5 %collective-permute-start.34 = (bf16[768,384]{1,0:T(8,128)(2,1)S(1)}, bf16[768,384]{1,0:T(8,128)(2,1)S(1)}, u32[]{:S(2)}, u32[]{:S(2)}) collective-permute-start(bf16[768,384]{1,0:T(8,128)(2,1)S(1)} %collective-permute-done.32.refs_17_), channel_id=1, source_target_pairs={{0,2},{2,0},{4,6},{6,4},{8,10},{10,8},{12,14},{14,12},{16,18},{18,... | collective-permute-start | bytes 1769480 | tf_op jit(solution)/shard_map/ppermute | solution.py:73
  63.1 33.4 %collective-permute-start.37 = (bf16[768,384]{1,0:T(8,128)(2,1)S(1)}, bf16[768,384]{1,0:T(8,128)(2,1)S(1)}, u32[]{:S(2)}, u32[]{:S(2)}) collective-permute-start(bf16[768,384]{1,0:T(8,128)(2,1)S(1)} %collective-permute-done.35.refs_21_), channel_id=1, source_target_pairs={{0,2},{2,0},{4,6},{6,4},{8,10},{10,8},{12,14},{14,12},{16,18},{18,... | collective-permute-start | bytes 1769480 | tf_op jit(solution)/shard_map/ppermute | solution.py:73
  136.4 18.1 %collective-permute-start.62 = (bf16[768,384]{1,0:T(8,128)(2,1)}, bf16[768,384]{1,0:T(8,128)(2,1)}, u32[]{:S(2)}, u32[]{:S(2)}) collective-permute-start(bf16[768,384]{1,0:T(8,128)(2,1)} %get-tuple-element.129), channel_id=1, source_target_pairs={{0,2},{2,0},{4,6},{6,4},{8,10},{10,8},{12,14},{14,12},{16,18},{18,... | collective-permute-start | bytes 1769480 | tf_op jit(solution)/shard_map/ppermute | solution.py:73
  136.4 24.4 %collective-permute-start.65 = (bf16[768,384]{1,0:T(8,128)(2,1)}, bf16[768,384]{1,0:T(8,128)(2,1)}, u32[]{:S(2)}, u32[]{:S(2)}) collective-permute-start(bf16[768,384]{1,0:T(8,128)(2,1)} %get-tuple-element.133), channel_id=1, source_target_pairs={{0,2},{2,0},{4,6},{6,4},{8,10},{10,8},{12,14},{14,12},{16,18},{18,... | collective-permute-start | bytes 1769480 | tf_op jit(solution)/shard_map/ppermute | solution.py:73
  152.8 31.9 %collective-permute-start.61 = (bf16[768,384]{1,0:T(8,128)(2,1)}, bf16[768,384]{1,0:T(8,128)(2,1)S(1)}, u32[]{:S(2)}, u32[]{:S(2)}) collective-permute-start(bf16[768,384]{1,0:T(8,128)(2,1)} %copy-done.13), channel_id=1, source_target_pairs={{0,2},{2,0},{4,6},{6,4},{8,10},{10,8},{12,14},{14,12},{16,18},{18,... | collective-permute-start | bytes 1769480 | tf_op jit(solution)/shard_map/ppermute | solution.py:73
  155.8 30.4 %collective-permute-start.63 = (bf16[768,384]{1,0:T(8,128)(2,1)S(1)}, bf16[768,384]{1,0:T(8,128)(2,1)S(1)}, u32[]{:S(2)}, u32[]{:S(2)}) collective-permute-start(bf16[768,384]{1,0:T(8,128)(2,1)S(1)} %add_convert_fusion.1), channel_id=1, source_target_pairs={{0,1},{1,0},{2,3},{3,2},{4,5},{5,4},{6,7},{7,6},{8,9},{9,8},{10,11... | collective-permute-start | bytes 1769480 | tf_op jit(solution)/shard_map/ppermute | solution.py:73
  163.4 13.9 %collective-permute-start.42 = (bf16[160,768]{1,0:T(8,128)(2,1)S(1)}, bf16[160,768]{1,0:T(8,128)(2,1)S(1)}, u32[]{:S(2)}, u32[]{:S(2)}) collective-permute-start(bf16[160,768]{1,0:T(8,128)(2,1)S(1)} %get-tuple-element.102.layer_ref), channel_id=1, source_target_pairs={{0,1},{1,0},{2,3},{3,2},{4,5},{5,4},{6,7},{7,6},{8,9},{9,8},{10,11... | collective-permute-start | bytes 737288 | tf_op jit(solution)/shard_map/ppermute | solution.py:73
  165.3 15.2 %collective-permute-start.44 = (bf16[128,768]{1,0:T(8,128)(2,1)S(1)}, bf16[128,768]{1,0:T(8,128)(2,1)S(1)}, u32[]{:S(2)}, u32[]{:S(2)}) collective-permute-start(bf16[128,768]{1,0:T(8,128)(2,1)S(1)} %copy-done.20), channel_id=1, source_target_pairs={{0,1},{1,0},{2,3},{3,2},{4,5},{5,4},{6,7},{7,6},{8,9},{9,8},{10,11... | collective-permute-start | bytes 589832 | tf_op jit(solution)/shard_map/ppermute | solution.py:73
  166.2 18.3 %collective-permute-start.50 = (bf16[8,48,384]{2,1,0:T(8,128)(2,1)S(1)}, bf16[8,48,384]{2,1,0:T(8,128)(2,1)S(1)}, u32[]{:S(2)}, u32[]{:S(2)}) collective-permute-start(bf16[8,48,384]{2,1,0:T(8,128)(2,1)S(1)} %copy-done.15), channel_id=1, source_target_pairs={{0,2},{2,0},{4,6},{6,4},{8,10},{10,8},{12,14},{14,12},{16,18},{18,... | collective-permute-start | bytes 884744 | tf_op jit(solution)/shard_map/ppermute | solution.py:73
  180.5 14.3 %collective-permute-start.66 = (bf16[768,384]{1,0:T(8,128)(2,1)S(1)}, bf16[768,384]{1,0:T(8,128)(2,1)S(1)}, u32[]{:S(2)}, u32[]{:S(2)}) collective-permute-start(bf16[768,384]{1,0:T(8,128)(2,1)S(1)} %add_convert_fusion), channel_id=1, source_target_pairs={{0,1},{1,0},{2,3},{3,2},{4,5},{5,4},{6,7},{7,6},{8,9},{9,8},{10,11... | collective-permute-start | bytes 1769480 | tf_op jit(solution)/shard_map/ppermute | solution.py:73
  184.5 11.5 %collective-permute-start.45 = (bf16[8,48,1152]{2,1,0:T(8,128)(2,1)S(1)}, bf16[8,48,1152]{2,1,0:T(8,128)(2,1)S(1)}, u32[]{:S(2)}, u32[]{:S(2)}) collective-permute-start(bf16[8,48,1152]{2,1,0:T(8,128)(2,1)S(1)} %copy-done.8), channel_id=1, source_target_pairs={{0,2},{2,0},{4,6},{6,4},{8,10},{10,8},{12,14},{14,12},{16,18},{18,... | collective-permute-start | bytes 2654216 | tf_op jit(solution)/shard_map/ppermute | solution.py:73
  184.6 13.8 %collective-permute-start.51 = (bf16[4,48,384]{2,1,0:T(8,128)(2,1)S(1)}, bf16[4,48,384]{2,1,0:T(8,128)(2,1)S(1)}, u32[]{:S(2)}, u32[]{:S(2)}) collective-permute-start(bf16[4,48,384]{2,1,0:T(8,128)(2,1)S(1)} %slice.154), channel_id=1, source_target_pairs={{0,4},{2,6},{4,0},{6,2},{8,12},{10,14},{12,8},{14,10},{16,20},{18,... | collective-permute-start | bytes 442376 | tf_op jit(solution)/shard_map/ppermute | solution.py:73
  198.5 12.0 %collective-permute-start.54 = (bf16[48,384]{1,0:T(8,128)(2,1)S(1)}, bf16[48,384]{1,0:T(8,128)(2,1)S(1)}, u32[]{:S(2)}, u32[]{:S(2)}) collective-permute-start(bf16[48,384]{1,0:T(8,128)(2,1)S(1)} %get-tuple-element.145), channel_id=1, source_target_pairs={{0,24},{2,26},{4,28},{6,30},{8,16},{10,18},{12,20},{14,22},{16,8},... | collective-permute-start | bytes 110600 | tf_op jit(solution)/shard_map/ppermute | solution.py:73
  (79 other events, 510.9 us)

commit v2 on v1

--- a/solution.py
+++ b/solution.py
@@ -12,11 +12,27 @@
 LANES = 128
 SCORE_SCALE = HEAD_DIM ** (-0.5)
 HIGHEST = lax.Precision.HIGHEST
-VMEM_BYTES = 50 * 1024 * 1024
+VMEM_BYTES = 20 * 1024 * 1024
+VMEM_MOST = 60 * 1024 * 1024
 F32 = jnp.float32
 BF16 = jnp.bfloat16
 
-Z_AT, X_AT, C_AT, Y_AT, FIRST_AT, SECOND_AT = range(6)
+Z_AT, X_AT, C_AT, Y_AT, DATA_AT = range(5)
+
+
+class Place:
+    def __init__(self, ref):
+        self.ref = ref
+
+    def __getitem__(self, which):
+        place = self.ref[0]
+        return {
+            Z_AT: place // (2 * SPLIT),
+            X_AT: (place // 4) % 2,
+            C_AT: (place // 2) % 2,
+            Y_AT: place % 2,
+            DATA_AT: place // 2,
+        }[which]
 
 
 def matmul(left, right, precision=None):
@@ -43,18 +59,25 @@
     return jax.ShapeDtypeStruct(shape, dtype)
 
 
-def run(kernel, scalars, operands, outs, scratch=(), flops=0):
-    moved = sum(x.size * x.dtype.itemsize for x in list(operands) + list(outs))
+def run(kernel, scalars, operands, outs, scratch=(), flops=1, after=(), far=0, far_outs=0, vmem=VMEM_BYTES):
+    waits = len(after)
+
+    def wrapped(place_ref, *refs):
+        kernel(Place(place_ref), *refs[waits:])
+
     return pl.pallas_call(
-        kernel,
+        wrapped,
         out_shape=list(outs),
         in_specs=[pl.BlockSpec(memory_space=pltpu.SMEM)]
-        + [pl.BlockSpec(memory_space=pltpu.VMEM)] * len(operands),
-        out_specs=[pl.BlockSpec(memory_space=pltpu.VMEM)] * len(outs),
+        + [pl.BlockSpec(memory_space=pl.ANY)] * waits
+        + [pl.BlockSpec(memory_space=pltpu.HBM)] * far
+        + [pl.BlockSpec(memory_space=pltpu.VMEM)] * (len(operands) - far),
+        out_specs=[pl.BlockSpec(memory_space=pltpu.HBM)] * far_outs
+        + [pl.BlockSpec(memory_space=pltpu.VMEM)] * (len(outs) - far_outs),
         scratch_shapes=list(scratch),
-        compiler_params=pltpu.CompilerParams(vmem_limit_bytes=VMEM_BYTES),
-        cost_estimate=pl.CostEstimate(flops=flops, bytes_accessed=moved, transcendentals=0),
-    )(scalars, *operands)
+        compiler_params=pltpu.CompilerParams(vmem_limit_bytes=vmem),
+        cost_estimate=pl.CostEstimate(flops=flops, bytes_accessed=1, transcendentals=0),
+    )(scalars, *after, *operands)
 
 
 def inverse_rms(values):
@@ -114,15 +137,11 @@
     hidden_local = expert_up_weight.shape[1]
     tensor_count = lax.axis_size("tensor")
     span = 2 * block_len
+    distances = buckets.shape[0]
 
     data_index = lax.axis_index("dp")
-    z_index = data_index // SPLIT
-    x_index = (data_index // 2) % 2
-    c_index = data_index % 2
     y_index = lax.axis_index("tensor")
-    scalars = jnp.stack(
-        [z_index, x_index, c_index, y_index, lengths[0, 0], lengths[0, 1]]
-    ).astype(jnp.int32)
+    scalars = (data_index * 2 + y_index).astype(jnp.int32).reshape(1)
 
     staged = shard_rows % 16 == 0
     slot_pieces = expert_count if half % 8 == 0 else 1
@@ -137,18 +156,81 @@
 
     small_columns = -(-(expert_count + 2) // LANES) * LANES
     weight_columns = 4 * head_width
-    packed = jnp.concatenate(
+    def pack(idx, *refs):
+        sources, refs = refs[:15], refs[15:]
+        (both_ref, out_ref, rows_ref, *small_refs), refs = refs[:7], refs[7:]
+        router_ref, attn_ref, moe_ref, sems = refs
+        targets = (
+            [out_ref.at[:, pl.ds(number * head_width, head_width)] for number in range(4)]
+            + [router_ref, attn_ref, moe_ref]
+            + [rows_ref.at[pl.ds(number * row_count, row_count), :] for number in range(2)]
+            + small_refs
+            + [both_ref.at[number] for number in range(2)]
+        )
+        copies = [
+            pltpu.make_async_copy(source, target, sems.at[number])
+            for number, (source, target) in enumerate(zip(sources, targets))
+        ]
+        for copy in copies:
+            copy.start()
+        for copy in copies[4:7]:
+            copy.wait()
+        diagonal = iota((shard_rows, shard_rows), 0) == iota((shard_rows, shard_rows), 1)
+        lane = iota((shard_rows, small_columns), 1)
+
+        def column(row_ref):
+            row = row_ref[...].astype(F32)
+            return jnp.sum(jnp.where(diagonal, row, 0.0), axis=1, keepdims=True)
+
+        spread_router = matmul_tn(
+            router_ref[...],
+            (iota((expert_count, small_columns), 0) == iota((expert_count, small_columns), 1))
+            .astype(F32)
+            .astype(BF16),
+        )
+        small = jnp.where(lane == expert_count, column(attn_ref), spread_router)
+        small = jnp.where(lane == expert_count + 1, column(moe_ref), small)
+        out_ref[:, weight_columns:] = small.astype(BF16)
+        for copy in copies[:4] + copies[7:]:
+            copy.wait()
+
+    expert_own, packed, rows_own, length_row, bucket_row, table_rows, route_row = run(
+        pack,
+        scalars,
         [
             query_weight,
             key_weight,
             value_weight,
             output_weight,
-            router,
-            attention_scale[:, None],
-            expert_scale[:, None],
-            jnp.zeros((shard_rows, small_columns - expert_count - 2), BF16),
+            router.T,
+            attention_scale[None, :],
+            expert_scale[None, :],
+            tokens,
+            cotangent,
+            lengths,
+            buckets[None, :],
+            bucket_bias.T,
+            routes.reshape(1, block_len),
+            expert_up_weight,
+            expert_down_weight,
         ],
-        axis=1,
+        [
+            shape_of((2, width, hidden_local), BF16),
+            shape_of((shard_rows, weight_columns + small_columns), BF16),
+            shape_of((2 * row_count, width), BF16),
+            shape_of(lengths.shape, jnp.int32),
+            shape_of((1, distances), jnp.int32),
+            shape_of((local_heads, bucket_count), F32),
+            shape_of((1, block_len), jnp.int32),
+        ],
+        [
+            pltpu.VMEM((expert_count, shard_rows), BF16),
+            pltpu.VMEM((1, shard_rows), BF16),
+            pltpu.VMEM((1, shard_rows), BF16),
+            pltpu.SemaphoreType.DMA((15,)),
+        ],
+        far=15,
+        vmem=VMEM_MOST,
     )
     if staged:
         gathered = [packed] + [swap(packed, "dp", mask) for mask in z_masks[1:]]
@@ -164,41 +246,24 @@
         index = (idx[Z_AT] ^ j_z) * SPLIT + (idx[X_AT] ^ j_x) * 2 + (idx[C_AT] ^ j_c)
         return pl.multiple_of(index * shard_rows, 16)
 
-    tokens_other = swap(tokens, "tensor", 1)
-    cotangent_other = swap(cotangent, "tensor", 1)
-
-    def spread(weight):
-        over_y = swap(weight, "tensor", 1)
-        return [weight, over_y, swap(weight, "dp", 1), swap(over_y, "dp", 1)]
-
-    up_parts = spread(expert_up_weight)
-    down_parts = spread(expert_down_weight)
-
-    bucket_row = jnp.pad(buckets, (0, span - buckets.shape[0]), constant_values=-1)[None, :]
-    bucket_back = jnp.pad(buckets[::-1], (0, span - buckets.shape[0]), constant_values=-1)[None, :]
-    table_rows = jnp.pad(bucket_bias.T, ((0, 8 - local_heads), (0, 0)))
-    route_row = routes.reshape(1, block_len)
-
-    def live_row(idx):
-        position = iota((1, block_len), 1)
-        return (position < idx[FIRST_AT] + idx[SECOND_AT]).astype(F32)
-
-    def live_column(idx):
-        position = iota((block_len, 1), 0)
-        return (position < idx[FIRST_AT] + idx[SECOND_AT]).astype(F32)
-
-    def prepare(idx, bucket_ref, table_ref, route_ref, tok, tok_other, cot, cot_other, *refs):
-        x_ref, bias_ref, own_ref, other_ref, xs_ref, gs_ref, live_ref, pick_ref = refs[:8]
-        live_parts = refs[8:-1]
-        cot_full = refs[-1]
+    rows_other = swap(rows_own, "tensor", 1)
+
+    def prepare(idx, length_ref, bucket_ref, table_ref, route_ref, mine, others, *refs):
+        x_ref, bias_ref, own_ref, other_ref, xs_ref, gs_ref, live_ref = refs[:7]
+        pick_ref, back_ref, live_rows_ref = refs[7:10]
+        live_parts = refs[10:-2]
+        cot_full, head_table = refs[-2:]
         own_at = pl.multiple_of(idx[Y_AT] * row_count, row_count)
         other_at = pl.multiple_of((1 - idx[Y_AT]) * row_count, row_count)
-        x_ref[pl.ds(own_at, row_count), :] = tok[...]
-        x_ref[pl.ds(other_at, row_count), :] = tok_other[...]
-        cot_full[pl.ds(own_at, row_count), :] = cot[...]
-        cot_full[pl.ds(other_at, row_count), :] = cot_other[...]
-
-        first, active = idx[FIRST_AT], idx[FIRST_AT] + idx[SECOND_AT]
+        for at, rows in ((own_at, mine), (other_at, others)):
+            x_ref[pl.ds(at, row_count), :] = rows[:row_count, :]
+            cot_full[pl.ds(at, row_count), :] = rows[row_count:, :]
+
+        first = length_ref[:, 0:1]
+        active = first + length_ref[:, 1:2]
+        live_rows_ref[...] = jnp.broadcast_to(
+            (iota((block_len, 1), 0) < active).astype(F32), live_rows_ref.shape
+        )
 
         def segment(position):
             return jnp.where(position < first, 0, jnp.where(position < active, 1, 2))
@@ -206,8 +271,15 @@
         allowed = segment(iota((block_len, block_len), 0)) == segment(
             iota((block_len, block_len), 1)
         )
-        pick = (bucket_ref[...] == iota((bucket_count, span), 0)).astype(F32)
-        head_table = matmul(table_ref[...], pick, HIGHEST)
+        pick = (bucket_ref[...] == iota((LANES, distances), 0)).astype(F32)
+        head_table[...] = jnp.zeros(head_table.shape, F32)
+        head_table[:local_heads, :distances] = matmul(
+            table_ref[...], pick[:bucket_count], HIGHEST
+        )
+        mirror = (
+            iota((distances, span), 0) + iota((distances, span), 1) == distances - 1
+        ).astype(F32)
+        back_ref[...] = matmul(pick.astype(BF16), mirror.astype(BF16)).astype(BF16)
         for head in range(local_heads):
             line = jnp.broadcast_to(head_table[head : head + 1, :], (block_len, span))
             turned = pltpu.roll(line, block_len + 1, 1, stride=1, stride_axis=0)
@@ -232,7 +304,7 @@
         other_ref[...] = selection(1 - idx[Y_AT]).astype(BF16)
         xs_ref[...] = matmul(own_bf, x_ref[...]).astype(BF16)
         gs_ref[...] = matmul(own_bf, cot_full[...]).astype(BF16)
-        live_select = own_select * live_row(idx)
+        live_select = own_select * (iota((1, block_len), 1) < active).astype(F32)
         live_ref[...] = jnp.broadcast_to(
             jnp.sum(live_select, axis=1, keepdims=True), live_ref.shape
         )
@@ -243,7 +315,7 @@
     prepared = run(
         prepare,
         scalars,
-        [bucket_row, table_rows, route_row, tokens, tokens_other, cotangent, cotangent_other],
+        [length_row, bucket_row, table_rows, route_row, rows_own, rows_other],
         [
             shape_of((block_len, width), BF16),
             shape_of((local_heads, block_len, block_len), F32),
@@ -253,24 +325,32 @@
             shape_of((slot_rows, width), BF16),
             shape_of((slot_rows, LANES), F32),
             shape_of((slot_rows, LANES), F32),
+            shape_of((LANES, span), BF16),
+            shape_of((block_len, LANES), F32),
         ]
         + [piece_shape] * slot_pieces,
-        [pltpu.VMEM((block_len, width), BF16)],
-        flops=10**9,
-    )
-    x_full, bias, own_select, other_select, x_slot, g_slot, live_slot, pick_slot = prepared[:8]
-    g_home = prepared[8:]
+        [pltpu.VMEM((block_len, width), BF16), pltpu.VMEM((8, span), F32)],
+    )
+    x_full, bias, own_select, other_select, x_slot, g_slot = prepared[:6]
+    live_slot, pick_slot, pick_back, live_rows = prepared[6:10]
+    g_home = prepared[10:]
+    if staged:
+        g_home = lax.optimization_barrier((*g_home, *gathered[expert_count : 2 * expert_count]))
+        g_home = g_home[:slot_pieces]
+    expert_y = swap(expert_own, "tensor", 1)
+    expert_c = swap(expert_own, "dp", 1)
 
     def to_experts(pieces):
         arrived = over_z(list(pieces))
         return arrived + [swap(piece, "dp", 2) for piece in arrived]
 
-    g_rows = to_experts(g_home)
+    g_rows = over_z(list(g_home))
+    g_rows = g_rows + [swap(jnp.concatenate(g_rows, axis=0), "dp", 2)]
 
     qkv_width = 3 * head_width
     piece_count = len(gathered)
 
-    def attend(idx, x_ref, bias_ref, own_ref, other_ref, xs_ref, *refs):
+    def attend(idx, live_ref, x_ref, bias_ref, own_ref, other_ref, xs_ref, *refs):
         pieces = refs[:piece_count]
         (
             send_ref,
@@ -299,7 +379,7 @@
         normed = (x * inverse_rms(x) * gain).astype(BF16)
         normed_ref[...] = normed
         qkv_ref[...] = matmul(normed, weight_ref[:, :qkv_width]).astype(BF16)
-        live = live_column(idx)
+        live = live_ref[:, :1]
         for head in range(local_heads):
             at = head * HEAD_DIM
             query = qkv_ref[:, at : at + HEAD_DIM]
@@ -318,7 +398,7 @@
     send, keep, normed, qkv, probs, context, weights, router_small, gains = run(
         attend,
         scalars,
-        [x_full, bias, own_select, other_select, x_slot] + gathered,
+        [live_rows, x_full, bias, own_select, other_select, x_slot] + gathered,
         [
             shape_of((slot_rows, width), BF16),
             shape_of((slot_rows, width), F32),
@@ -330,9 +410,10 @@
             shape_of((width, small_columns), BF16),
             shape_of((8, width), F32),
         ],
-        flops=10**9,
     )
     arrived = swap(send, "tensor", 1)
+    expert_y, _ = lax.optimization_barrier((expert_y, send))
+    expert_parts = [expert_own, expert_y, expert_c, swap(expert_y, "dp", 1)]
 
     def second_norm(idx, keep_ref, arrived_ref, gain_ref, residual_ref, scale_ref, nm_ref, *parts):
         residual = keep_ref[...] + arrived_ref[...].astype(F32)
@@ -353,19 +434,17 @@
             shape_of((slot_rows, width), BF16),
         ]
         + [piece_shape] * slot_pieces,
-        flops=10**6,
     )
     expert_rows = to_experts(row_home)
 
     expert_in = 2 * slot_rows
-    parts = len(up_parts)
+    parts = len(expert_parts)
 
     def experts(idx, router_ref, *refs):
         count = 2 * slot_pieces
         row_parts, refs = refs[:count], refs[count:]
-        g_parts, refs = refs[:count], refs[count:]
-        up, refs = refs[:parts], refs[parts:]
-        down, refs = refs[:parts], refs[parts:]
+        g_parts, refs = refs[: slot_pieces + 1], refs[slot_pieces + 1 :]
+        both, refs = refs[:parts], refs[parts:]
         send_ref, keep_ref, rows_ref, total_ref, hidden_ref, pre_ref = refs
         rows = stacked(row_parts).astype(BF16)
         rows_ref[...] = rows
@@ -378,7 +457,7 @@
         backward = jnp.zeros((expert_in, width), F32)
         for part in range(parts):
             at = part * hidden_local
-            pre = matmul(rows, up[part][...])
+            pre = matmul(rows, both[part][0])
             square = pre * pre
             inner = 0.7978845608028654 * pre * (1.0 + 0.044715 * square)
             tanh = jnp.tanh(inner)
@@ -387,10 +466,10 @@
                 0.7978845608028654 * (1.0 + 3.0 * 0.044715 * square)
             )
             hidden_ref[:, at : at + hidden_local] = hidden
-            grad_pre = (matmul(total, down[part][...]) * slope).astype(BF16)
+            grad_pre = (matmul(total, both[part][1]) * slope).astype(BF16)
             pre_ref[:, at : at + hidden_local] = grad_pre
-            forward += matmul_nt(hidden, down[part][...])
-            backward += matmul_nt(grad_pre, up[part][...])
+            forward += matmul_nt(hidden, both[part][1])
+            backward += matmul_nt(grad_pre, both[part][0])
         keep_ref[:, :width] = forward[:slot_rows]
         keep_ref[:, width:] = backward[:slot_rows]
         send_ref[:, :width] = forward[slot_rows:].astype(BF16)
@@ -399,7 +478,7 @@
     send, keep, rows_in, total_in, hidden, grad_pre = run(
         experts,
         scalars,
-        [router_small] + expert_rows + g_rows + up_parts + down_parts,
+        [router_small] + expert_rows + g_rows + expert_parts,
         [
             shape_of((slot_rows, 2 * width), BF16),
             shape_of((slot_rows, 2 * width), F32),
@@ -408,45 +487,60 @@
             shape_of((expert_in, parts * hidden_local), BF16),
             shape_of((expert_in, parts * hidden_local), BF16),
         ],
-        flops=3 * 10**9,
     )
     arrived = swap(send, "dp", 2)
+
+    def expert_grads(idx, rows_ref, total_ref, hidden_ref, pre_ref, own_ref, y_ref, c_ref):
+        for part in range(parts):
+            at = part * hidden_local
+            up_grad = matmul_tn(rows_ref[...], pre_ref[:, at : at + hidden_local])
+            down_grad = matmul_tn(total_ref[...], hidden_ref[:, at : at + hidden_local])
+            ref, first = ((own_ref, 0), (y_ref, 0), (c_ref, 0), (c_ref, 2))[part]
+            ref[first] = up_grad.astype(ref.dtype)
+            ref[first + 1] = down_grad.astype(ref.dtype)
+
+    weight_shape = (width, hidden_local)
+    grads_own, grads_y, grads_c = run(
+        expert_grads,
+        scalars,
+        [rows_in, total_in, hidden, grad_pre],
+        [
+            shape_of((2,) + weight_shape, F32),
+            shape_of((2,) + weight_shape, BF16),
+            shape_of((4,) + weight_shape, BF16),
+        ],
+    )
+    from_c = swap(grads_c, "dp", 1)
+
+    def fold_y(idx, y_ref, c_ref, up_ref, down_ref):
+        for number, ref in enumerate((up_ref, down_ref)):
+            ref[...] = (y_ref[number].astype(F32) + c_ref[2 + number].astype(F32)).astype(BF16)
+
+    up_passed, down_passed = run(
+        fold_y, scalars, [grads_y, from_c], [shape_of(weight_shape, BF16)] * 2
+    )
+    up_from_y = swap(up_passed, "tensor", 1)
 
     def add_x(idx, keep_ref, arrived_ref, *parts_out):
         store_pieces(parts_out, keep_ref[...] + arrived_ref[...].astype(F32))
 
     both_shape = shape_of((slot_rows // slot_pieces, 2 * width), BF16)
-    back = run(add_x, scalars, [keep, arrived], [both_shape] * slot_pieces, flops=10**6)
+    back = run(add_x, scalars, [keep, arrived], [both_shape] * slot_pieces)
     home = over_z(list(back))
 
-    def expert_grads(idx, rows_ref, total_ref, hidden_ref, pre_ref, *outs):
-        for part in range(parts):
-            at = part * hidden_local
-            up_grad, down_grad = outs[2 * part : 2 * part + 2]
-            up_grad[...] = matmul_tn(rows_ref[...], pre_ref[:, at : at + hidden_local]).astype(
-                up_grad.dtype
-            )
-            down_grad[...] = matmul_tn(
-                total_ref[...], hidden_ref[:, at : at + hidden_local]
-            ).astype(down_grad.dtype)
-
-    weight_shape = (width, hidden_local)
-    weight_grads = run(
-        expert_grads,
-        scalars,
-        [rows_in, total_in, hidden, grad_pre],
-        [shape_of(weight_shape, F32)] * 2 + [shape_of(weight_shape, BF16)] * (2 * parts - 2),
-        flops=2 * 10**9,
-    )
-
-    def scatter_expert(own, over_y, over_c, over_yc):
-        from_c = swap(over_c, "dp", 1)
-        from_yc = swap(over_yc, "dp", 1)
-        passed = (over_y.astype(F32) + from_yc.astype(F32)).astype(BF16)
-        return own + from_c.astype(F32) + swap(passed, "tensor", 1).astype(F32)
-
-    grad_w_in = scatter_expert(*weight_grads[0::2])
-    grad_w_out = scatter_expert(*weight_grads[1::2])
+    def fold_grad(number):
+        def fold(idx, own_ref, c_ref, y_ref, out_ref):
+            out_ref[...] = own_ref[number] + c_ref[number].astype(F32) + y_ref[...].astype(F32)
+
+        return fold
+
+    (grad_w_in,) = run(
+        fold_grad(0),
+        scalars,
+        [grads_own, from_c, up_from_y],
+        [shape_of(weight_shape, F32)],
+        after=[back[0]],
+    )
 
     expert_pad = -(-expert_count // 8) * 8
 
@@ -504,16 +598,16 @@
             shape_of((8, width), F32),
             shape_of((expert_pad, width), F32),
         ],
-        flops=10**8,
+        after=[grad_w_in],
     )
     mid_other = swap(mid_own, "tensor", 1)
-    layer_other = swap(layer_own, "tensor", 1)
 
     half_pieces = 2 * expert_count
+    first_part = weight_columns * 2 // 3 // LANES * LANES
 
     def emit_rows(idx, full_ref, outs):
         if not staged:
-            outs[0][...] = full_ref[...].astype(BF16)
+            outs[0][...] = full_ref[...]
             return
         keep_ref, send_ref = outs
         for number in range(half_pieces):
@@ -522,56 +616,53 @@
             at = piece_offset(idx, number + half_pieces)
             send_ref[number] = full_ref[pl.ds(at, shard_rows), :].astype(BF16)
 
-    def row_shapes(columns):
-        if not staged:
-            return [shape_of((width, columns), BF16)]
-        return [
-            shape_of((half_pieces, shard_rows, columns), F32),
-            shape_of((half_pieces, shard_rows, columns), BF16),
+    if staged:
+        row_shapes = [
+            shape_of((half_pieces, shard_rows, weight_columns), F32),
+            shape_of((half_pieces, shard_rows, weight_columns), BF16),
         ]
-
-    def reduce_rows(outs):
-        if not staged:
-            return lax.psum_scatter(
-                outs[0].astype(F32), "dp", scatter_dimension=0, tiled=True
-            )
-        held, send = outs
-        held = held + swap(send, "dp", 1).astype(F32)
-        held = held[:expert_count] + swap(
-            held[expert_count:].astype(BF16), "dp", 2
-        ).astype(F32)
-        total = held[0]
-        for j in range(1, expert_count):
-            total = total + swap(held[j].astype(BF16), "dp", z_masks[j]).astype(F32)
-        return total
-
-    def output_grad(idx, own_ref, other_ref, mid_ref, mid_other_ref, context_ref, ga_ref, *refs):
-        full = refs[-1]
-        grad = matmul_tn(own_ref[...], mid_ref[...]) + matmul_tn(
-            other_ref[...], mid_other_ref[...]
-        )
-        grad = grad.astype(BF16)
-        ga_ref[...] = grad
-        full[...] = matmul_tn(grad, context_ref[...])
-        emit_rows(idx, full, refs[:-1])
-
-    grad_attention, *output_rows = run(
-        output_grad,
-        scalars,
-        [own_select, other_select, mid_own, mid_other, context],
-        [shape_of((block_len, width), BF16)] + row_shapes(head_width),
-        [pltpu.VMEM((width, head_width), F32)],
-        flops=4 * 10**8,
-    )
-    grad_wo = reduce_rows(output_rows)
+    else:
+        row_shapes = [shape_of((width, weight_columns), F32)]
+
+    small_rows = -(-(expert_count + 2 + tensor_count) // 8) * 8
+
+    def store_halves(ref, at, values):
+        high = values.astype(BF16)
+        ref[at : at + 2 * small_rows, :width] = jnp.concatenate(
+            [high.astype(F32), values - high.astype(F32)], axis=0
+        ).astype(BF16)
+
+    def load_halves(ref, at):
+        both = ref[at : at + 2 * small_rows, :width].astype(F32)
+        return both[:small_rows] + both[small_rows:]
 
     def attend_back(
-        idx, ga_ref, weight_ref, qkv_ref, probs_ref, normed_ref, x_ref, bucket_ref, *refs
+        idx,
+        own_ref,
+        other_ref,
+        mid_ref,
+        mid_other_ref,
+        context_ref,
+        weight_ref,
+        qkv_ref,
+        probs_ref,
+        normed_ref,
+        x_ref,
+        back_ref,
+        live_ref,
+        moe_ref,
+        router_ref,
+        *refs,
     ):
-        keep_ref, send_ref, gain_ref, table_ref = refs[:4]
+        ga_ref, keep_ref, send_ref, small_ref = refs[:4]
         outs = refs[4:-3]
         grads, full, upstream = refs[-3:]
-        live = live_column(idx)
+        live = live_ref[:, :1]
+        grad_attention = matmul_tn(own_ref[...], mid_ref[...]) + matmul_tn(
+            other_ref[...], mid_other_ref[...]
+        )
+        ga_ref[...] = grad_attention.astype(BF16)
+        full[:, qkv_width:] = matmul_tn(ga_ref[...], context_ref[...])
         grad_context = matmul(ga_ref[...], weight_ref[:, qkv_width:]) * live
         grad_context = grad_context.astype(BF16)
         mirror = (
@@ -609,66 +700,204 @@
             lines.append(jnp.sum(lines_left, axis=0, keepdims=True))
         lines.append(jnp.zeros((8 - local_heads, span), F32))
         diagonal = jnp.concatenate(lines, axis=0)
-        pick = (bucket_ref[...] == iota((LANES, span), 0)).astype(F32)
-        table = matmul_nt(diagonal, pick, HIGHEST)
-        table_ref[...] = jnp.zeros(table_ref.shape, F32)
-        for head in range(local_heads):
-            table_ref[:1, head * LANES : (head + 1) * LANES] = table[head : head + 1, :]
+        table = matmul_nt(diagonal, back_ref[...].astype(F32), HIGHEST)
+        line = [table[head : head + 1, :] for head in range(local_heads)]
+        line.append(jnp.zeros((1, width - local_heads * LANES), F32))
+        line = jnp.concatenate(line[: local_heads + (width > local_heads * LANES)], axis=1)
         all_grads = grads[...]
         grad_normed = matmul_nt(all_grads, weight_ref[:, :qkv_width])
         upstream[...] = grad_normed
         x = x_ref[...].astype(F32)
-        gain_ref[...] = jnp.broadcast_to(
-            jnp.sum(grad_normed * x * inverse_rms(x), axis=0, keepdims=True), gain_ref.shape
-        )
+        gain = jnp.sum(grad_normed * x * inverse_rms(x), axis=0, keepdims=True)
+        row = iota((small_rows, width), 0)
+        small = jnp.where(row == expert_count, gain, 0.0)
+        small = jnp.where(row == expert_count + 1, moe_ref[:1, :], small)
+        small_ref[...] = jnp.where(row == expert_count + 2 + idx[Y_AT], line, small)
+        small_ref[:expert_count, :] = router_ref[:expert_count, :]
         own_at = pl.multiple_of(idx[Y_AT] * row_count, row_count)
         other_at = pl.multiple_of((1 - idx[Y_AT]) * row_count, row_count)
         keep_ref[...] = upstream[pl.ds(own_at, row_count), :]
-        send_ref[...] = upstream[pl.ds(other_at, row_count), :].astype(BF16)
-        full[...] = matmul_tn(normed_ref[...], all_grads)
+        send_ref[:row_count, :] = upstream[pl.ds(other_at, row_count), :].astype(BF16)
+        store_halves(send_ref, row_count, small_ref[...])
+        full[:, :qkv_width] = matmul_tn(normed_ref[...], all_grads)
         emit_rows(idx, full, outs)
 
-    up_keep, up_send, gain_attn, table_part, *qkv_rows = run(
+    grad_attention, up_keep, up_send, small, *partial_rows = run(
         attend_back,
         scalars,
-        [grad_attention, weights, qkv, probs, normed, x_full, bucket_back],
-        [
+        [
+            own_select,
+            other_select,
+            mid_own,
+            mid_other,
+            context,
+            weights,
+            qkv,
+            probs,
+            normed,
+            x_full,
+            pick_back,
+            live_rows,
+            gain_moe,
+            router_part,
+        ],
+        [
+            shape_of((block_len, width), BF16),
             shape_of((row_count, width), F32),
-            shape_of((row_count, width), BF16),
-            shape_of((8, width), F32),
-            shape_of((8, local_heads * LANES), F32),
+            shape_of((row_count + 2 * small_rows, width), BF16),
+            shape_of((small_rows, width), F32),
         ]
-        + row_shapes(qkv_width),
+        + row_shapes,
         [
             pltpu.VMEM((block_len, qkv_width), BF16),
-            pltpu.VMEM((width, qkv_width), F32),
+            pltpu.VMEM((width, weight_columns), F32),
             pltpu.VMEM((block_len, width), F32),
         ],
-        flops=2 * 10**9,
     )
     up_other = swap(up_send, "tensor", 1)
-    grad_qkv = reduce_rows(qkv_rows)
-
-    table_line = jnp.pad(table_part[0], (0, width - local_heads * LANES))
-    table_lines = jnp.where(
-        jnp.arange(tensor_count)[:, None] == y_index, table_line[None, :], 0.0
-    )
-    small = jnp.concatenate(
-        [gain_attn[:1], gain_moe[:1], router_part[:expert_count], table_lines], axis=0
-    )
-    small = jnp.pad(small, ((0, -small.shape[0] % 8), (0, 0)))
-    small = small + swap(small, "tensor", 1)
+    down_passed, _ = lax.optimization_barrier((down_passed, up_other))
+    down_from_y = swap(down_passed, "tensor", 1)
+
+    def small_over_y(idx, small_ref, other_ref, out_ref):
+        out_ref[...] = small_ref[...] + load_halves(other_ref, row_count)
+
+    (small,) = run(
+        small_over_y, scalars, [small, up_other], [shape_of((small_rows, width), F32)]
+    )
+
+    out_shapes = [shape_of((shard_rows, head_width), F32)] * 4
     if staged:
+        held, outgoing = partial_rows
+        from_core = swap(outgoing, "dp", 1)
+
+        def after_core(idx, held_ref, from_ref, x_send, x_keep, *z_refs):
+            z_sends, z_keep = z_refs[:-1], z_refs[-1]
+
+            def total(number, columns):
+                return held_ref[number, :, columns] + from_ref[number, :, columns].astype(F32)
+
+            front, rest = slice(0, first_part), slice(first_part, weight_columns)
+            for j in range(expert_count):
+                x_keep[j] = total(j, front)
+                x_send[j] = total(expert_count + j, front).astype(BF16)
+                for x in range(2):
+                    piece = total(x * expert_count + j, rest)
+                    if j == 0:
+                        z_keep[x] = piece
+                    else:
+                        z_sends[j - 1][x] = piece.astype(BF16)
+
+        rest_part = weight_columns - first_part
+        x_send, x_keep, *z_sends, z_keep = run(
+            after_core,
+            scalars,
+            [held, from_core],
+            [
+                shape_of((expert_count, shard_rows, first_part), BF16),
+                shape_of((expert_count, shard_rows, first_part), F32),
+            ]
+            + [shape_of((2, shard_rows, rest_part), BF16)] * (expert_count - 1)
+            + [shape_of((2, shard_rows, rest_part), F32)],
+        )
+        from_x = swap(x_send, "dp", 2)
+        from_z = [swap(piece, "dp", z_masks[j + 1]) for j, piece in enumerate(z_sends)]
+
         small = small + swap(small, "dp", 1)
-        small = small + swap(small, "dp", 2)
-        moved = [swap(small, "dp", mask) for mask in z_masks[1:]]
-        for piece in moved:
-            small = small + piece
+        small_x = swap(small, "dp", 2)
+
+        def after_first(idx, small_ref, small_x_ref, x_keep, from_x, z_keep, *refs):
+            from_z, refs = refs[: expert_count - 1], refs[expert_count - 1 :]
+            z_sends, (front_keep, x_send, rest_keep, small_keep) = refs[:-4], refs[-4:]
+            small = small_ref[...] + small_x_ref[...]
+            small_keep[...] = small
+            front_keep[...] = x_keep[0] + from_x[0].astype(F32)
+            for j in range(1, expert_count):
+                z_sends[j - 1][...] = jnp.zeros(z_sends[j - 1].shape, BF16)
+                z_sends[j - 1][:shard_rows, :] = (x_keep[j] + from_x[j].astype(F32)).astype(BF16)
+                store_halves(z_sends[j - 1], shard_rows, small)
+            rest = z_keep[...]
+            for ref in from_z:
+                rest = rest + ref[...].astype(F32)
+            rest_keep[...] = rest[0]
+            x_send[...] = rest[1].astype(BF16)
+
+        *z_sends, front_keep, x_send, rest_keep, small = run(
+            after_first,
+            scalars,
+            [small, small_x, x_keep, from_x, z_keep] + from_z,
+            [shape_of((shard_rows + 2 * small_rows, first_part), BF16)] * (expert_count - 1)
+            + [
+                shape_of((shard_rows, first_part), F32),
+                shape_of((shard_rows, rest_part), BF16),
+                shape_of((shard_rows, rest_part), F32),
+                shape_of((small_rows, width), F32),
+            ],
+        )
+        from_z = [swap(piece, "dp", z_masks[j + 1]) for j, piece in enumerate(z_sends)]
+        from_x = swap(x_send, "dp", 2)
+        late = [front_keep]
+
+        def last_sum(idx, small_ref, front_keep, rest_keep, from_x, *refs):
+            from_z, refs = refs[: expert_count - 1], refs[expert_count - 1 :]
+            outs, (attn_out, moe_out, router_out, table_out, full) = refs[:-5], refs[-5:]
+            front = front_keep[...]
+            small = small_ref[...]
+            for ref in from_z:
+                front = front + ref[:shard_rows, :].astype(F32)
+                small = small + load_halves(ref, shard_rows)
+            column = iota((LANES, width), 1) - idx[DATA_AT] * shard_rows
+            select = (column == iota((LANES, width), 0)).astype(F32)
+            shard = matmul_nt(small, select, HIGHEST)
+            attn_out[...] = shard[expert_count : expert_count + 1, :shard_rows]
+            moe_out[...] = shard[expert_count + 1 : expert_count + 2, :shard_rows]
+            router_out[...] = shard[:expert_count, :shard_rows]
+            mine = iota((small_rows, width), 0) == expert_count + 2 + idx[Y_AT]
+            line = jnp.sum(jnp.where(mine, small, 0.0), axis=0, keepdims=True)
+            lines = [line[:, head * LANES : (head + 1) * LANES] for head in range(local_heads)]
+            table_out[...] = jnp.concatenate(lines, axis=0)[:, :bucket_count]
+            full[:, :first_part] = front
+            full[:, first_part:] = rest_keep[...] + from_x[...].astype(F32)
+            for number, out in enumerate(outs):
+                out[...] = full[:, number * head_width : (number + 1) * head_width]
+
+        *grad_matrices, grad_attn_scale, grad_moe_scale, grad_router, table = run(
+            last_sum,
+            scalars,
+            [small, front_keep, rest_keep, from_x] + from_z,
+            out_shapes
+            + [
+                shape_of((1, shard_rows), F32),
+                shape_of((1, shard_rows), F32),
+                shape_of((expert_count, shard_rows), F32),
+                shape_of((local_heads, bucket_count), F32),
+            ],
+            [pltpu.VMEM((shard_rows, weight_columns), F32)],
+        )
+        grad_attn_scale, grad_moe_scale = grad_attn_scale[0], grad_moe_scale[0]
+        grad_router, table = grad_router.T, table.T
     else:
+        late = []
+        summed = lax.psum_scatter(partial_rows[0], "dp", scatter_dimension=0, tiled=True)
+        grad_matrices = [
+            summed[:, number * head_width : (number + 1) * head_width] for number in range(4)
+        ]
         small = lax.psum(small, "dp")
-    shard = lax.dynamic_slice_in_dim(small, data_index * shard_rows, shard_rows, 1)
-    table = lax.dynamic_slice_in_dim(small, 2 + expert_count + y_index, 1, 0)
-    table = table[0, : local_heads * LANES].reshape(local_heads, LANES)[:, :bucket_count].T
+        shard = lax.dynamic_slice_in_dim(small, data_index * shard_rows, shard_rows, 1)
+        grad_router = shard[:expert_count].T
+        grad_attn_scale, grad_moe_scale = shard[expert_count], shard[expert_count + 1]
+        table = lax.dynamic_slice_in_dim(small, expert_count + 2 + y_index, 1, 0)
+        table = table[0, : local_heads * LANES].reshape(local_heads, LANES)[:, :bucket_count].T
+
+    (grad_w_out,) = run(
+        fold_grad(1),
+        scalars,
+        [grads_own, from_c, down_from_y],
+        [shape_of(weight_shape, F32)],
+        after=late,
+    )
+    if late:
+        layer_own, _ = lax.optimization_barrier((layer_own, late[0]))
+    layer_other = swap(layer_own, "tensor", 1)
 
     def finish(
         idx, own_ref, other_ref, layer_ref, layer_other_ref, ga_ref, keep_ref, arrived_ref,
@@ -681,7 +910,7 @@
         layer_out[...] = full[pl.ds(own_at, row_count), :].astype(BF16)
         x = tok_ref[...].astype(F32)
         scale = inverse_rms(x)
-        scaled = (keep_ref[...] + arrived_ref[...].astype(F32)) * gain_ref[:1, :]
+        scaled = (keep_ref[...] + arrived_ref[:row_count, :].astype(F32)) * gain_ref[:1, :]
         grad = scale * scaled - x * scale**3 * jnp.mean(scaled * x, axis=-1, keepdims=True)
         grad = grad + ga_ref[pl.ds(own_at, row_count), :].astype(F32)
         tokens_out[...] = grad.astype(BF16)
@@ -695,19 +924,16 @@
         ],
         [shape_of((row_count, width), BF16)] * 2,
         [pltpu.VMEM((block_len, width), F32)],
-        flops=10**8,
+        after=late,
     )
 
     return (
         layer_out,
         grad_tokens,
-        grad_qkv[:, :head_width],
-        grad_qkv[:, head_width : 2 * head_width],
-        grad_qkv[:, 2 * head_width :],
-        grad_wo,
-        shard[0],
-        shard[1],
-        shard[2 : 2 + expert_count].T,
+        *grad_matrices,
+        grad_attn_scale,
+        grad_moe_scale,
+        grad_router,
         table,
         grad_w_in,
         grad_w_out,

time: 219 us -> 171 us (0.78)
  local copies, waits for them, and re-layouts: 23.2 us -> 5.89 us
  waiting for transfers between devices: 89.1 us -> 80.2 us
  starting transfers between devices: 64 us -> 56 us
  Pallas kernels: 35.1 us -> 27.8 us
  other arithmetic: 6.1 us -> 0.02 us
    ppermute x67 -> x52, waiting for transfers between devices: 89.1 us -> 80.2 us  [swap(): return lax.ppermute(values, axis, [(i, i ^ mask) for i in range(count)])]
    unnamed x75 -> x18, local copies, waits for them, and re-layouts: 14 us -> 5.89 us
    ppermute x67 -> x52, starting transfers between devices: 64 us -> 56 us  [swap(): return lax.ppermute(values, axis, [(i, i ^ mask) for i in range(count)])]
    pallas_call x10 -> x17, Pallas kernels: 35.1 us -> 27.8 us  [run(): pl.pallas_call(wrapped, out_shape=list(outs), in_specs=[pl.BlockSpec(memo...]
    add x9 -> x0, other arithmetic: 3.4 us -> none  [the longest x2 2.4 us: scatter_expert(): return own + from_c.astype(F32) + swap(passed, 'tensor', 1).astype(F32)]
    convert_element_type x2 -> x0, other arithmetic: 2.44 us -> none  [scatter_expert(): passed = (over_y.astype(F32) + from_yc.astype(F32)).astype(BF16)]
  transfers between devices with their start and end apart: 67 -> 52, of which waited for: 31 -> 27; matrix products, arithmetic and copies ran while one was open for 7% -> 0% of each run, Pallas kernels for 11% -> 5%
where the time goes in v2:
time: 171 us
  waiting for transfers between devices  80.2 us (47%)
  starting transfers between devices  56 us (33%)
  Pallas kernels  27.8 us (16%)
  local copies, waits for them, and re-layouts  5.89 us (3%)
    ppermute x52, waiting for transfers between devices, swap(): return lax.ppermute(values, axis, [(i, i ^ mask) for i in range(count)])  80.2 us
    ppermute x52, starting transfers between devices, swap(): return lax.ppermute(values, axis, [(i, i ^ mask) for i in range(count)])  56 us
    pallas_call x17, Pallas kernels, run(): pl.pallas_call(wrapped, out_shape=list(outs), in_specs=[pl.BlockSpec(memo...  27.8 us
    unnamed x18, local copies, waits for them, and re-layouts  5.89 us
  transfers between devices with their start and end apart: 52, of which 27 were waited for; matrix products, arithmetic and copies ran while one was open for 0% of the time, Pallas kernels for 5%

profile of v2, /device:TPU:0, one launch (start us, length us, event | category | flops | bytes accessed | tf_op | source)
XLA Modules:
  0.0 170.8 jit_solution(11072462974161084109)
XLA Ops:
  0.7 2.9 %shard_map.238 = (bf16[2,768,384]{2,1,0:T(8,128)(2,1)}, bf16[48,1664]{1,0:T(8,128)(2,1)}, bf16[256,768]{1,0:T(8,128)(2,1)}, s32[1,2]{1,0:T(1,128)}, s32[1,511]{1...) custom-call(s32[1]{0:T(128)} %bitcast.place_ref, bf16[48,384]{1,0:T(8,128)(2,1)} %refs_0_.1, bf16[48,384]{1,0:T(8,128)(2,1)} %refs_1_.1, ...), custom_call_target="tpu_custom_call" | custom-call | flops 1 | bytes 1 | tf_op jit(solution)/shard_map/pallas_call | solution.py:68
  3.6 3.0 %collective-permute-start.28 = (bf16[2,768,384]{2,1,0:T(8,128)(2,1)}, bf16[2,768,384]{2,1,0:T(8,128)(2,1)S(1)}, u32[]{:S(2)}, u32[]{:S(2)}) collective-permute-start(bf16[2,768,384]{2,1,0:T(8,128)(2,1)} %get-tuple-element.132.refs_14_), channel_id=1, source_target_pairs={{0,1},{1,0},{2,3},{3,2},{4,5},{5,4},{6,7},{7,6},{8,9},{9,8},{10,11... | collective-permute-start | bytes 3538952 | tf_op jit(solution)/shard_map/ppermute | solution.py:96
  8.1 3.6 %collective-permute-start.3 = (bf16[48,1664]{1,0:T(8,128)(2,1)}, bf16[48,1664]{1,0:T(8,128)(2,1)S(1)}, u32[]{:S(2)}, u32[]{:S(2)}) collective-permute-start(bf16[48,1664]{1,0:T(8,128)(2,1)} %get-tuple-element.115.refs_6_), channel_id=1, source_target_pairs={{0,24},{2,26},{4,28},{6,30},{8,16},{10,18},{12,20},{14,22},{16,8},... | collective-permute-start | bytes 479240 | tf_op jit(solution)/shard_map/ppermute | solution.py:96
  13.6 3.5 %collective-permute-done.3.refs_9_ = bf16[48,1664]{1,0:T(8,128)(2,1)S(1)} collective-permute-done((bf16[48,1664]{1,0:T(8,128)(2,1)}, bf16[48,1664]{1,0:T(8,128)(2,1)S(1)}, u32[]{:S(2)}, u32[]{:S(2)}) %collective-permute-start.3) | collective-permute-done | bytes 159776 | tf_op jit(solution)/shard_map/ppermute | solution.py:96
  17.2 8.7 %collective-permute-done.2.refs_8_ = bf16[48,1664]{1,0:T(8,128)(2,1)S(1)} collective-permute-done((bf16[48,1664]{1,0:T(8,128)(2,1)}, bf16[48,1664]{1,0:T(8,128)(2,1)S(1)}, u32[]{:S(2)}, u32[]{:S(2)}) %collective-permute-start.2) | collective-permute-done | bytes 159776 | tf_op jit(solution)/shard_map/ppermute | solution.py:96
  28.1 4.6 %collective-permute-done.7.refs_13_ = bf16[48,1664]{1,0:T(8,128)(2,1)S(1)} collective-permute-done((bf16[48,1664]{1,0:T(8,128)(2,1)S(1)}, bf16[48,1664]{1,0:T(8,128)(2,1)S(1)}, u32[]{:S(2)}, u32[]{:S(2)}) %collective-permute-start.7) | collective-permute-done | bytes 159776 | tf_op jit(solution)/shard_map/ppermute | solution.py:96
  33.3 2.9 %collective-permute-done.6.refs_12_ = bf16[48,1664]{1,0:T(8,128)(2,1)S(1)} collective-permute-done((bf16[48,1664]{1,0:T(8,128)(2,1)S(1)}, bf16[48,1664]{1,0:T(8,128)(2,1)S(1)}, u32[]{:S(2)}, u32[]{:S(2)}) %collective-permute-start.6) | collective-permute-done | bytes 159776 | tf_op jit(solution)/shard_map/ppermute | solution.py:96
  36.2 3.0 %collective-permute-done.5.refs_11_ = bf16[48,1664]{1,0:T(8,128)(2,1)S(1)} collective-permute-done((bf16[48,1664]{1,0:T(8,128)(2,1)S(1)}, bf16[48,1664]{1,0:T(8,128)(2,1)S(1)}, u32[]{:S(2)}, u32[]{:S(2)}) %collective-permute-start.5) | collective-permute-done | bytes 159776 | tf_op jit(solution)/shard_map/ppermute | solution.py:96
  47.3 3.1 %shard_map.240 = (bf16[160,768]{1,0:T(8,128)(2,1)S(1)}, f32[160,768]{1,0:T(8,128)S(1)}, bf16[256,768]{1,0:T(8,128)(2,1)S(1)}, bf16[256,1152]{1,0:T(8,128)(2,1)S(...) custom-call(s32[1]{0:T(128)} %bitcast.place_ref, ...), custom_call_target="tpu_custom_call" | custom-call | flops 1 | bytes 1 | tf_op jit(solution)/shard_map/pallas_call | solution.py:68
  52.4 2.6 %collective-permute-start.25 = (bf16[40,768]{1,0:T(8,128)(2,1)S(1)}, bf16[40,768]{1,0:T(8,128)(2,1)S(1)}, u32[]{:S(2)}, u32[]{:S(2)}) collective-permute-start(bf16[40,768]{1,0:T(8,128)(2,1)S(1)} %get-tuple-element.130), channel_id=1, source_target_pairs={{0,16},{2,18},{4,20},{6,22},{8,24},{10,26},{12,28},{14,30},{16,0},... | collective-permute-start | bytes 184328 | tf_op jit(solution)/shard_map/ppermute | solution.py:96
  56.8 2.5 %collective-permute-done.25.refs_11_ = bf16[40,768]{1,0:T(8,128)(2,1)S(1)} collective-permute-done((bf16[40,768]{1,0:T(8,128)(2,1)S(1)}, bf16[40,768]{1,0:T(8,128)(2,1)S(1)}, u32[]{:S(2)}, u32[]{:S(2)}) %collective-permute-start.25) | collective-permute-done | bytes 61472 | tf_op jit(solution)/shard_map/ppermute | solution.py:96
  64.5 2.6 %collective-permute-start.18 = (bf16[40,768]{1,0:T(8,128)(2,1)S(1)}, bf16[40,768]{1,0:T(8,128)(2,1)S(1)}, u32[]{:S(2)}, u32[]{:S(2)}) collective-permute-start(bf16[40,768]{1,0:T(8,128)(2,1)S(1)} %get-tuple-element.122), channel_id=1, source_target_pairs={{0,16},{2,18},{4,20},{6,22},{8,24},{10,26},{12,28},{14,30},{16,0},... | collective-permute-start | bytes 184328 | tf_op jit(solution)/shard_map/ppermute | solution.py:96
  79.6 5.0 %shard_map.242 = (bf16[160,1536]{1,0:T(8,128)(2,1)S(1)}, f32[160,1536]{1,0:T(8,128)S(1)}, bf16[320,768]{1,0:T(8,128)(2,1)S(1)}, bf16[320,768]{1,0:T(8,128)(2,1)S...) custom-call(s32[1]{0:T(128)} %bitcast.place_ref, ...), custom_call_target="tpu_custom_call" | custom-call | flops 1 | bytes 1 | tf_op jit(solution)/shard_map/pallas_call | solution.py:68
  84.6 3.3 %shard_map.244 = (f32[2,768,384]{2,1,0:T(8,128)S(1)}, bf16[2,768,384]{2,1,0:T(8,128)(2,1)S(1)}, bf16[4,768,384]{2,1,0:T(8,128)(2,1)S(1)}) custom-call(s32[1]{0:T(128)} %bitcast.place_ref, bf16[320,768]{1,0:T(8,128)(2,1)S(1)} %get-tuple-element.137.refs_0_, bf16[320,768]{1,0:T(8,128)(2,1)S(1)} %get-tuple-element.138.refs_1_, ...), custom_call_target="tpu_custom_call" | custom-call | flops 1 | bytes 1 | tf_op jit(solution)/shard_map/pallas_call | solution.py:68
  88.7 3.8 %collective-permute-done.32.refs_1_.refs_2_ = bf16[4,768,384]{2,1,0:T(8,128)(2,1)S(1)} collective-permute-done((bf16[4,768,384]{2,1,0:T(8,128)(2,1)S(1)}, bf16[4,768,384]{2,1,0:T(8,128)(2,1)S(1)}, u32[]{:S(2)}, u32[]{:S(2)}) %collective-permute-start.32) | collective-permute-done | bytes 2359328 | tf_op jit(solution)/shard_map/ppermute | solution.py:96
  94.4 7.2 %collective-permute-done.31.refs_1_ = bf16[160,1536]{1,0:T(8,128)(2,1)S(1)} collective-permute-done((bf16[160,1536]{1,0:T(8,128)(2,1)S(1)}, bf16[160,1536]{1,0:T(8,128)(2,1)S(1)}, u32[]{:S(2)}, u32[]{:S(2)}) %collective-permute-start.31) | collective-permute-done | bytes 491552 | tf_op jit(solution)/shard_map/ppermute | solution.py:96
  109.4 4.7 %collective-permute-done.35.refs_3_ = bf16[40,1536]{1,0:T(8,128)(2,1)S(1)} collective-permute-done((bf16[40,1536]{1,0:T(8,128)(2,1)S(1)}, bf16[40,1536]{1,0:T(8,128)(2,1)S(1)}, u32[]{:S(2)}, u32[]{:S(2)}) %collective-permute-start.35) | collective-permute-done | bytes 122912 | tf_op jit(solution)/shard_map/ppermute | solution.py:96
  118.6 4.7 %collective-permute-done.37.refs_3_ = bf16[160,768]{1,0:T(8,128)(2,1)S(1)} collective-permute-done((bf16[160,768]{1,0:T(8,128)(2,1)S(1)}, bf16[160,768]{1,0:T(8,128)(2,1)S(1)}, u32[]{:S(2)}, u32[]{:S(2)}) %collective-permute-start.37) | collective-permute-done | bytes 245792 | tf_op jit(solution)/shard_map/ppermute | solution.py:96
  123.2 5.6 %shard_map.248 = (bf16[256,768]{1,0:T(8,128)(2,1)S(1)}, f32[128,768]{1,0:T(8,128)S(1)}, bf16[144,768]{1,0:T(8,128)(2,1)S(1)}, f32[8,768]{1,0:T(8,128)S(1)}, f32[...) custom-call(s32[1]{0:T(128)} %bitcast.place_ref, ...), custom_call_target="tpu_custom_call" | custom-call | flops 1 | bytes 1 | tf_op jit(solution)/shard_map/pallas_call | solution.py:68
  130.5 6.3 %collective-permute-done.38.refs_1_.refs_7_ = bf16[144,768]{1,0:T(8,128)(2,1)S(1)} collective-permute-done((bf16[144,768]{1,0:T(8,128)(2,1)S(1)}, bf16[144,768]{1,0:T(8,128)(2,1)S(1)}, u32[]{:S(2)}, u32[]{:S(2)}) %collective-permute-start.38) | collective-permute-done | bytes 221216 | tf_op jit(solution)/shard_map/ppermute | solution.py:96
  141.7 2.6 %collective-permute-start.43 = (bf16[2,48,512]{2,1,0:T(8,128)(2,1)S(1)}, bf16[2,48,512]{2,1,0:T(8,128)(2,1)S(1)}, u32[]{:S(2)}, u32[]{:S(2)}) collective-permute-start(bf16[2,48,512]{2,1,0:T(8,128)(2,1)S(1)} %get-tuple-element.170), channel_id=1, source_target_pairs={{0,8},{2,10},{4,12},{6,14},{8,0},{10,2},{12,4},{14,6},{16,24},{18,... | collective-permute-start | bytes 294920 | tf_op jit(solution)/shard_map/ppermute | solution.py:96
  145.3 4.2 %collective-permute-done.40.refs_1_ = f32[8,768]{1,0:T(8,128)S(1)} collective-permute-done((f32[8,768]{1,0:T(8,128)S(1)}, f32[8,768]{1,0:T(8,128)S(1)}, u32[]{:S(2)}, u32[]{:S(2)}) %collective-permute-start.40) | collective-permute-done | bytes 24608 | tf_op jit(solution)/shard_map/ppermute | solution.py:96
  151.6 4.3 %collective-permute-done.45.refs_7_ = bf16[2,48,512]{2,1,0:T(8,128)(2,1)S(1)} collective-permute-done((bf16[2,48,512]{2,1,0:T(8,128)(2,1)S(1)}, bf16[2,48,512]{2,1,0:T(8,128)(2,1)S(1)}, u32[]{:S(2)}, u32[]{:S(2)}) %collective-permute-start.45) | collective-permute-done | bytes 98336 | tf_op jit(solution)/shard_map/ppermute | solution.py:96
  165.1 3.4 %collective-permute-done.49.refs_5_ = bf16[64,1024]{1,0:T(8,128)(2,1)S(1)} collective-permute-done((bf16[64,1024]{1,0:T(8,128)(2,1)S(1)}, bf16[64,1024]{1,0:T(8,128)(2,1)S(1)}, u32[]{:S(2)}, u32[]{:S(2)}) %collective-permute-start.49) | collective-permute-done | bytes 131104 | tf_op jit(solution)/shard_map/ppermute | solution.py:96
  (117 shorter events, 71.9 us)
Async XLA Ops:
  3.6 46.9 %collective-permute-start.28 = (bf16[2,768,384]{2,1,0:T(8,128)(2,1)}, bf16[2,768,384]{2,1,0:T(8,128)(2,1)S(1)}, u32[]{:S(2)}, u32[]{:S(2)}) collective-permute-start(bf16[2,768,384]{2,1,0:T(8,128)(2,1)} %get-tuple-element.132.refs_14_), channel_id=1, source_target_pairs={{0,1},{1,0},{2,3},{3,2},{4,5},{5,4},{6,7},{7,6},{8,9},{9,8},{10,11... | collective-permute-start | bytes 3538952 | tf_op jit(solution)/shard_map/ppermute | solution.py:96
  8.1 9.0 %collective-permute-start.3 = (bf16[48,1664]{1,0:T(8,128)(2,1)}, bf16[48,1664]{1,0:T(8,128)(2,1)S(1)}, u32[]{:S(2)}, u32[]{:S(2)}) collective-permute-start(bf16[48,1664]{1,0:T(8,128)(2,1)} %get-tuple-element.115.refs_6_), channel_id=1, source_target_pairs={{0,24},{2,26},{4,28},{6,30},{8,16},{10,18},{12,20},{14,22},{16,8},... | collective-permute-start | bytes 479240 | tf_op jit(solution)/shard_map/ppermute | solution.py:96
  11.7 14.1 %collective-permute-start.2 = (bf16[48,1664]{1,0:T(8,128)(2,1)}, bf16[48,1664]{1,0:T(8,128)(2,1)S(1)}, u32[]{:S(2)}, u32[]{:S(2)}) collective-permute-start(bf16[48,1664]{1,0:T(8,128)(2,1)} %get-tuple-element.115.refs_6_), channel_id=1, source_target_pairs={{0,16},{2,18},{4,20},{6,22},{8,24},{10,26},{12,28},{14,30},{16,0},... | collective-permute-start | bytes 479240 | tf_op jit(solution)/shard_map/ppermute | solution.py:96
  11.7 14.1 %collective-permute-start.1 = (bf16[48,1664]{1,0:T(8,128)(2,1)}, bf16[48,1664]{1,0:T(8,128)(2,1)S(1)}, u32[]{:S(2)}, u32[]{:S(2)}) collective-permute-start(bf16[48,1664]{1,0:T(8,128)(2,1)} %get-tuple-element.115.refs_6_), channel_id=1, source_target_pairs={{0,8},{2,10},{4,12},{6,14},{8,0},{10,2},{12,4},{14,6},{16,24},{18,... | collective-permute-start | bytes 479240 | tf_op jit(solution)/shard_map/ppermute | solution.py:96
  13.4 27.9 %collective-permute-start = (bf16[256,768]{1,0:T(8,128)(2,1)}, bf16[256,768]{1,0:T(8,128)(2,1)S(1)}, u32[]{:S(2)}, u32[]{:S(2)}) collective-permute-start(bf16[256,768]{1,0:T(8,128)(2,1)} %get-tuple-element.108.refs_4_), channel_id=1, source_target_pairs={{0,1},{1,0},{2,3},{3,2},{4,5},{5,4},{6,7},{7,6},{8,9},{9,8},{10,11... | collective-permute-start | bytes 1179656 | tf_op jit(solution)/shard_map/ppermute | solution.py:96
  17.2 9.2 %collective-permute-start.12 = (bf16[48,1664]{1,0:T(8,128)(2,1)S(1)}, bf16[48,1664]{1,0:T(8,128)(2,1)S(1)}, u32[]{:S(2)}, u32[]{:S(2)}) collective-permute-start(bf16[48,1664]{1,0:T(8,128)(2,1)S(1)} %collective-permute-done.4.refs_10_), channel_id=1, source_target_pairs={{0,2},{2,0},{4,6},{6,4},{8,10},{10,8},{12,14},{14,12},{16,18},{18,... | collective-permute-start | bytes 479240 | tf_op jit(solution)/shard_map/ppermute | solution.py:96
  27.2 8.9 %collective-permute-start.6 = (bf16[48,1664]{1,0:T(8,128)(2,1)S(1)}, bf16[48,1664]{1,0:T(8,128)(2,1)S(1)}, u32[]{:S(2)}, u32[]{:S(2)}) collective-permute-start(bf16[48,1664]{1,0:T(8,128)(2,1)S(1)} %collective-permute-done.2.refs_8_), channel_id=1, source_target_pairs={{0,4},{2,6},{4,0},{6,2},{8,12},{10,14},{12,8},{14,10},{16,20},{18,... | collective-permute-start | bytes 479240 | tf_op jit(solution)/shard_map/ppermute | solution.py:96
  33.3 12.5 %collective-permute-start.9 = (bf16[48,1664]{1,0:T(8,128)(2,1)S(1)}, bf16[48,1664]{1,0:T(8,128)(2,1)S(1)}, u32[]{:S(2)}, u32[]{:S(2)}) collective-permute-start(bf16[48,1664]{1,0:T(8,128)(2,1)S(1)} %collective-permute-done.1.refs_7_), channel_id=1, source_target_pairs={{0,2},{2,0},{4,6},{6,4},{8,10},{10,8},{12,14},{14,12},{16,18},{18,... | collective-permute-start | bytes 479240 | tf_op jit(solution)/shard_map/ppermute | solution.py:96
  36.2 10.2 %collective-permute-start.15 = (bf16[48,1664]{1,0:T(8,128)(2,1)S(1)}, bf16[48,1664]{1,0:T(8,128)(2,1)S(1)}, u32[]{:S(2)}, u32[]{:S(2)}) collective-permute-start(bf16[48,1664]{1,0:T(8,128)(2,1)S(1)} %collective-permute-done.7.refs_13_), channel_id=1, source_target_pairs={{0,2},{2,0},{4,6},{6,4},{8,10},{10,8},{12,14},{14,12},{16,18},{18,... | collective-permute-start | bytes 479240 | tf_op jit(solution)/shard_map/ppermute | solution.py:96
  45.8 33.7 %collective-permute-start.29 = (bf16[2,768,384]{2,1,0:T(8,128)(2,1)}, bf16[2,768,384]{2,1,0:T(8,128)(2,1)S(1)}, u32[]{:S(2)}, u32[]{:S(2)}) collective-permute-start(bf16[2,768,384]{2,1,0:T(8,128)(2,1)} %get-tuple-element.132.refs_14_), channel_id=1, source_target_pairs={{0,2},{2,0},{4,6},{6,4},{8,10},{10,8},{12,14},{14,12},{16,18},{18,... | collective-permute-start | bytes 3538952 | tf_op jit(solution)/shard_map/ppermute | solution.py:96
  50.5 29.1 %collective-permute-start.30 = (bf16[2,768,384]{2,1,0:T(8,128)(2,1)S(1)}, bf16[2,768,384]{2,1,0:T(8,128)(2,1)S(1)}, u32[]{:S(2)}, u32[]{:S(2)}) collective-permute-start(bf16[2,768,384]{2,1,0:T(8,128)(2,1)S(1)} %collective-permute-done.28.refs_15_), channel_id=1, source_target_pairs={{0,2},{2,0},{4,6},{6,4},{8,10},{10,8},{12,14},{14,12},{16,18},{18,... | collective-permute-start | bytes 3538952 | tf_op jit(solution)/shard_map/ppermute | solution.py:96
  88.0 13.6 %collective-permute-start.31 = (bf16[160,1536]{1,0:T(8,128)(2,1)S(1)}, bf16[160,1536]{1,0:T(8,128)(2,1)S(1)}, u32[]{:S(2)}, u32[]{:S(2)}) collective-permute-start(bf16[160,1536]{1,0:T(8,128)(2,1)S(1)} %get-tuple-element.135), channel_id=1, source_target_pairs={{0,4},{2,6},{4,0},{6,2},{8,12},{10,14},{12,8},{14,10},{16,20},{18,... | collective-permute-start | bytes 1474568 | tf_op jit(solution)/shard_map/ppermute | solution.py:96
  92.8 15.4 %collective-permute-start.33 = (bf16[768,384]{1,0:T(8,128)(2,1)S(1)}, bf16[768,384]{1,0:T(8,128)(2,1)S(1)}, u32[]{:S(2)}, u32[]{:S(2)}) collective-permute-start(bf16[768,384]{1,0:T(8,128)(2,1)S(1)} %get-tuple-element.144), channel_id=1, source_target_pairs={{0,1},{1,0},{2,3},{3,2},{4,5},{5,4},{6,7},{7,6},{8,9},{9,8},{10,11... | collective-permute-start | bytes 1769480 | tf_op jit(solution)/shard_map/ppermute | solution.py:96
  101.8 12.3 %collective-permute-start.35 = (bf16[40,1536]{1,0:T(8,128)(2,1)S(1)}, bf16[40,1536]{1,0:T(8,128)(2,1)S(1)}, u32[]{:S(2)}, u32[]{:S(2)}) collective-permute-start(bf16[40,1536]{1,0:T(8,128)(2,1)S(1)} %get-tuple-element.146), channel_id=1, source_target_pairs={{0,16},{2,18},{4,20},{6,22},{8,24},{10,26},{12,28},{14,30},{16,0},... | collective-permute-start | bytes 368648 | tf_op jit(solution)/shard_map/ppermute | solution.py:96
  104.1 10.1 %collective-permute-start.36 = (bf16[40,1536]{1,0:T(8,128)(2,1)S(1)}, bf16[40,1536]{1,0:T(8,128)(2,1)S(1)}, u32[]{:S(2)}, u32[]{:S(2)}) collective-permute-start(bf16[40,1536]{1,0:T(8,128)(2,1)S(1)} %get-tuple-element.147), channel_id=1, source_target_pairs={{0,24},{2,26},{4,28},{6,30},{8,16},{10,18},{12,20},{14,22},{16,8},... | collective-permute-start | bytes 368648 | tf_op jit(solution)/shard_map/ppermute | solution.py:96
  128.8 9.4 %collective-permute-start.41 = (bf16[8,48,1536]{2,1,0:T(8,128)(2,1)S(1)}, bf16[8,48,1536]{2,1,0:T(8,128)(2,1)S(1)}, u32[]{:S(2)}, u32[]{:S(2)}) collective-permute-start(bf16[8,48,1536]{2,1,0:T(8,128)(2,1)S(1)} %get-tuple-element.166), channel_id=1, source_target_pairs={{0,2},{2,0},{4,6},{6,4},{8,10},{10,8},{12,14},{14,12},{16,18},{18,... | collective-permute-start | bytes 3538952 | tf_op jit(solution)/shard_map/ppermute | solution.py:96
  136.7 24.3 %collective-permute-start.51 = (bf16[768,384]{1,0:T(8,128)(2,1)S(1)}, bf16[768,384]{1,0:T(8,128)(2,1)S(1)}, u32[]{:S(2)}, u32[]{:S(2)}) collective-permute-start(bf16[768,384]{1,0:T(8,128)(2,1)S(1)} %get-tuple-element.195), channel_id=1, source_target_pairs={{0,1},{1,0},{2,3},{3,2},{4,5},{5,4},{6,7},{7,6},{8,9},{9,8},{10,11... | collective-permute-start | bytes 1769480 | tf_op jit(solution)/shard_map/ppermute | solution.py:96
  138.4 17.5 %collective-permute-start.42 = (bf16[4,48,1024]{2,1,0:T(8,128)(2,1)S(1)}, bf16[4,48,1024]{2,1,0:T(8,128)(2,1)S(1)}, u32[]{:S(2)}, u32[]{:S(2)}) collective-permute-start(bf16[4,48,1024]{2,1,0:T(8,128)(2,1)S(1)} %get-tuple-element.168), channel_id=1, source_target_pairs={{0,4},{2,6},{4,0},{6,2},{8,12},{10,14},{12,8},{14,10},{16,20},{18,... | collective-permute-start | bytes 1179656 | tf_op jit(solution)/shard_map/ppermute | solution.py:96
  140.8 8.6 %collective-permute-start.40 = (f32[8,768]{1,0:T(8,128)S(1)}, f32[8,768]{1,0:T(8,128)S(1)}, u32[]{:S(2)}, u32[]{:S(2)}) collective-permute-start(f32[8,768]{1,0:T(8,128)S(1)} %add.7.refs_0_), channel_id=1, source_target_pairs={{0,4},{2,6},{4,0},{6,2},{8,12},{10,14},{12,8},{14,10},{16,20},{18,... | collective-permute-start | bytes 73736 | tf_op jit(solution)/shard_map/ppermute | solution.py:96
  141.7 9.9 %collective-permute-start.43 = (bf16[2,48,512]{2,1,0:T(8,128)(2,1)S(1)}, bf16[2,48,512]{2,1,0:T(8,128)(2,1)S(1)}, u32[]{:S(2)}, u32[]{:S(2)}) collective-permute-start(bf16[2,48,512]{2,1,0:T(8,128)(2,1)S(1)} %get-tuple-element.170), channel_id=1, source_target_pairs={{0,8},{2,10},{4,12},{6,14},{8,0},{10,2},{12,4},{14,6},{16,24},{18,... | collective-permute-start | bytes 294920 | tf_op jit(solution)/shard_map/ppermute | solution.py:96
  156.1 13.5 %collective-permute-start.46 = (bf16[160,768]{1,0:T(8,128)(2,1)S(1)}, bf16[160,768]{1,0:T(8,128)(2,1)S(1)}, u32[]{:S(2)}, u32[]{:S(2)}) collective-permute-start(bf16[160,768]{1,0:T(8,128)(2,1)S(1)} %get-tuple-element.175.refs_3_), channel_id=1, source_target_pairs={{0,1},{1,0},{2,3},{3,2},{4,5},{5,4},{6,7},{7,6},{8,9},{9,8},{10,11... | collective-permute-start | bytes 737288 | tf_op jit(solution)/shard_map/ppermute | solution.py:96
  156.7 8.5 %collective-permute-start.48 = (bf16[64,1024]{1,0:T(8,128)(2,1)S(1)}, bf16[64,1024]{1,0:T(8,128)(2,1)S(1)}, u32[]{:S(2)}, u32[]{:S(2)}) collective-permute-start(bf16[64,1024]{1,0:T(8,128)(2,1)S(1)} %get-tuple-element.183), channel_id=1, source_target_pairs={{0,8},{2,10},{4,12},{6,14},{8,0},{10,2},{12,4},{14,6},{16,24},{18,... | collective-permute-start | bytes 393224 | tf_op jit(solution)/shard_map/ppermute | solution.py:96
  158.2 10.3 %collective-permute-start.49 = (bf16[64,1024]{1,0:T(8,128)(2,1)S(1)}, bf16[64,1024]{1,0:T(8,128)(2,1)S(1)}, u32[]{:S(2)}, u32[]{:S(2)}) collective-permute-start(bf16[64,1024]{1,0:T(8,128)(2,1)S(1)} %get-tuple-element.184), channel_id=1, source_target_pairs={{0,16},{2,18},{4,20},{6,22},{8,24},{10,26},{12,28},{14,30},{16,0},... | collective-permute-start | bytes 393224 | tf_op jit(solution)/shard_map/ppermute | solution.py:96
  159.4 9.2 %collective-permute-start.50 = (bf16[64,1024]{1,0:T(8,128)(2,1)S(1)}, bf16[64,1024]{1,0:T(8,128)(2,1)S(1)}, u32[]{:S(2)}, u32[]{:S(2)}) collective-permute-start(bf16[64,1024]{1,0:T(8,128)(2,1)S(1)} %get-tuple-element.185), channel_id=1, source_target_pairs={{0,24},{2,26},{4,28},{6,30},{8,16},{10,18},{12,20},{14,22},{16,8},... | collective-permute-start | bytes 393224 | tf_op jit(solution)/shard_map/ppermute | solution.py:96
  (37 other events, 205.0 us)

commit v3 on v2

--- a/solution.py
+++ b/solution.py
@@ -138,6 +138,7 @@
     tensor_count = lax.axis_size("tensor")
     span = 2 * block_len
     distances = buckets.shape[0]
+    cut = width // 3
 
     data_index = lax.axis_index("dp")
     y_index = lax.axis_index("tensor")
@@ -158,15 +159,27 @@
     weight_columns = 4 * head_width
     def pack(idx, *refs):
         sources, refs = refs[:15], refs[15:]
-        (both_ref, out_ref, rows_ref, *small_refs), refs = refs[:7], refs[7:]
-        router_ref, attn_ref, moe_ref, sems = refs
+        (out_ref, rows_ref, rest_ref, facts_ref), refs = refs[:4], refs[4:]
+        router_ref, attn_ref, moe_ref, *small_refs, sems = refs
         targets = (
             [out_ref.at[:, pl.ds(number * head_width, head_width)] for number in range(4)]
             + [router_ref, attn_ref, moe_ref]
             + [rows_ref.at[pl.ds(number * row_count, row_count), :] for number in range(2)]
             + small_refs
-            + [both_ref.at[number] for number in range(2)]
-        )
+            + [
+                ref.at[pl.ds(at, rows), pl.ds(number * hidden_local, hidden_local)]
+                for number in range(2)
+                for ref, at, rows in (
+                    (rows_ref, 2 * row_count, cut),
+                    (rest_ref, 0, width - cut),
+                )
+            ]
+        )
+        sources = list(sources[:13]) + [
+            source.at[pl.ds(at, rows), :]
+            for source in sources[13:]
+            for at, rows in ((0, cut), (cut, width - cut))
+        ]
         copies = [
             pltpu.make_async_copy(source, target, sems.at[number])
             for number, (source, target) in enumerate(zip(sources, targets))
@@ -193,8 +206,14 @@
         out_ref[:, weight_columns:] = small.astype(BF16)
         for copy in copies[:4] + copies[7:]:
             copy.wait()
-
-    expert_own, packed, rows_own, length_row, bucket_row, table_rows, route_row = run(
+        length_ref, bucket_ref, table_ref, route_ref = small_refs
+        facts_ref[...] = jnp.zeros(facts_ref.shape, F32)
+        facts_ref[0:1, :2] = length_ref[...].astype(F32)
+        facts_ref[1:2, :distances] = bucket_ref[...].astype(F32)
+        facts_ref[2:3, :block_len] = route_ref[...].astype(F32)
+        facts_ref[8 : 8 + local_heads, :bucket_count] = table_ref[...]
+
+    packed, rows_own, rest_own, facts = run(
         pack,
         scalars,
         [
@@ -215,27 +234,26 @@
             expert_down_weight,
         ],
         [
-            shape_of((2, width, hidden_local), BF16),
             shape_of((shard_rows, weight_columns + small_columns), BF16),
-            shape_of((2 * row_count, width), BF16),
-            shape_of(lengths.shape, jnp.int32),
-            shape_of((1, distances), jnp.int32),
-            shape_of((local_heads, bucket_count), F32),
-            shape_of((1, block_len), jnp.int32),
+            shape_of((2 * row_count + cut, 2 * hidden_local), BF16),
+            shape_of((width - cut, 2 * hidden_local), BF16),
+            shape_of((16, span), F32),
         ],
         [
             pltpu.VMEM((expert_count, shard_rows), BF16),
             pltpu.VMEM((1, shard_rows), BF16),
             pltpu.VMEM((1, shard_rows), BF16),
-            pltpu.SemaphoreType.DMA((15,)),
+            pltpu.VMEM(lengths.shape, jnp.int32),
+            pltpu.VMEM((1, distances), jnp.int32),
+            pltpu.VMEM((local_heads, bucket_count), F32),
+            pltpu.VMEM((1, block_len), jnp.int32),
+            pltpu.SemaphoreType.DMA((17,)),
         ],
         far=15,
         vmem=VMEM_MOST,
     )
     if staged:
         gathered = [packed] + [swap(packed, "dp", mask) for mask in z_masks[1:]]
-        gathered = gathered + [swap(piece, "dp", 2) for piece in gathered]
-        gathered = gathered + [swap(piece, "dp", 1) for piece in gathered]
     else:
         gathered = [lax.all_gather(packed, "dp", axis=0, tiled=True)]
 
@@ -248,7 +266,7 @@
 
     rows_other = swap(rows_own, "tensor", 1)
 
-    def prepare(idx, length_ref, bucket_ref, table_ref, route_ref, mine, others, *refs):
+    def prepare(idx, facts_ref, mine, others, *refs):
         x_ref, bias_ref, own_ref, other_ref, xs_ref, gs_ref, live_ref = refs[:7]
         pick_ref, back_ref, live_rows_ref = refs[7:10]
         live_parts = refs[10:-2]
@@ -257,10 +275,10 @@
         other_at = pl.multiple_of((1 - idx[Y_AT]) * row_count, row_count)
         for at, rows in ((own_at, mine), (other_at, others)):
             x_ref[pl.ds(at, row_count), :] = rows[:row_count, :]
-            cot_full[pl.ds(at, row_count), :] = rows[row_count:, :]
-
-        first = length_ref[:, 0:1]
-        active = first + length_ref[:, 1:2]
+            cot_full[pl.ds(at, row_count), :] = rows[row_count : 2 * row_count, :]
+
+        first = facts_ref[0:1, 0:1].astype(jnp.int32)
+        active = first + facts_ref[0:1, 1:2].astype(jnp.int32)
         live_rows_ref[...] = jnp.broadcast_to(
             (iota((block_len, 1), 0) < active).astype(F32), live_rows_ref.shape
         )
@@ -271,10 +289,11 @@
         allowed = segment(iota((block_len, block_len), 0)) == segment(
             iota((block_len, block_len), 1)
         )
-        pick = (bucket_ref[...] == iota((LANES, distances), 0)).astype(F32)
+        pick = facts_ref[1:2, :distances].astype(jnp.int32) == iota((LANES, distances), 0)
+        pick = pick.astype(F32)
         head_table[...] = jnp.zeros(head_table.shape, F32)
         head_table[:local_heads, :distances] = matmul(
-            table_ref[...], pick[:bucket_count], HIGHEST
+            facts_ref[8 : 8 + local_heads, :bucket_count], pick[:bucket_count], HIGHEST
         )
         mirror = (
             iota((distances, span), 0) + iota((distances, span), 1) == distances - 1
@@ -285,7 +304,7 @@
             turned = pltpu.roll(line, block_len + 1, 1, stride=1, stride_axis=0)
             bias_ref[head] = jnp.where(allowed, turned[:, :block_len], MASKED_SCORE)
 
-        route = route_ref[...]
+        route = facts_ref[2:3, :block_len].astype(jnp.int32)
         chosen = (route == iota((LANES, block_len), 0)).astype(F32)
         earlier = (iota((block_len, block_len), 0) < iota((block_len, block_len), 1)).astype(F32)
         counts = matmul(chosen.astype(BF16), earlier.astype(BF16))
@@ -315,7 +334,7 @@
     prepared = run(
         prepare,
         scalars,
-        [length_row, bucket_row, table_rows, route_row, rows_own, rows_other],
+        [facts, rows_own, rows_other],
         [
             shape_of((block_len, width), BF16),
             shape_of((local_heads, block_len, block_len), F32),
@@ -334,18 +353,25 @@
     x_full, bias, own_select, other_select, x_slot, g_slot = prepared[:6]
     live_slot, pick_slot, pick_back, live_rows = prepared[6:10]
     g_home = prepared[10:]
+    g_wait = []
     if staged:
-        g_home = lax.optimization_barrier((*g_home, *gathered[expert_count : 2 * expert_count]))
-        g_home = g_home[:slot_pieces]
-    expert_y = swap(expert_own, "tensor", 1)
-    expert_c = swap(expert_own, "dp", 1)
+        g_home = lax.optimization_barrier((*g_home, *gathered[1:expert_count]))[:slot_pieces]
+        gathered = gathered + [swap(piece, "dp", 2) for piece in gathered]
+        *gathered, _ = lax.optimization_barrier((*gathered, x_full))
+        gathered = gathered + [swap(piece, "dp", 1) for piece in gathered]
+    g_rows = over_z(list(g_home))
+    if staged:
+        g_wait = g_rows[1:]
+    g_rows = g_rows + [swap(jnp.concatenate(g_rows, axis=0), "dp", 2)]
+    rest_send, _ = lax.optimization_barrier((rest_own, rows_other))
+    rest_y = swap(rest_send, "tensor", 1)
+    expert_parts = [rows_own, rest_own, rows_other, rest_y]
+    expert_parts += [swap(rows_own, "dp", 1), swap(rest_own, "dp", 1), swap(rows_other, "dp", 1)]
 
     def to_experts(pieces):
         arrived = over_z(list(pieces))
         return arrived + [swap(piece, "dp", 2) for piece in arrived]
 
-    g_rows = over_z(list(g_home))
-    g_rows = g_rows + [swap(jnp.concatenate(g_rows, axis=0), "dp", 2)]
 
     qkv_width = 3 * head_width
     piece_count = len(gathered)
@@ -410,10 +436,11 @@
             shape_of((width, small_columns), BF16),
             shape_of((8, width), F32),
         ],
+        after=g_wait,
     )
     arrived = swap(send, "tensor", 1)
-    expert_y, _ = lax.optimization_barrier((expert_y, send))
-    expert_parts = [expert_own, expert_y, expert_c, swap(expert_y, "dp", 1)]
+    rest_y, _ = lax.optimization_barrier((rest_y, arrived))
+    expert_parts.append(swap(rest_y, "dp", 1))
 
     def second_norm(idx, keep_ref, arrived_ref, gain_ref, residual_ref, scale_ref, nm_ref, *parts):
         residual = keep_ref[...] + arrived_ref[...].astype(F32)
@@ -434,17 +461,18 @@
             shape_of((slot_rows, width), BF16),
         ]
         + [piece_shape] * slot_pieces,
+        after=expert_parts[4:7],
     )
     expert_rows = to_experts(row_home)
 
     expert_in = 2 * slot_rows
-    parts = len(expert_parts)
+    parts = 4
 
     def experts(idx, router_ref, *refs):
         count = 2 * slot_pieces
         row_parts, refs = refs[:count], refs[count:]
         g_parts, refs = refs[: slot_pieces + 1], refs[slot_pieces + 1 :]
-        both, refs = refs[:parts], refs[parts:]
+        weights, refs = refs[: 2 * parts], refs[2 * parts :]
         send_ref, keep_ref, rows_ref, total_ref, hidden_ref, pre_ref = refs
         rows = stacked(row_parts).astype(BF16)
         rows_ref[...] = rows
@@ -457,7 +485,18 @@
         backward = jnp.zeros((expert_in, width), F32)
         for part in range(parts):
             at = part * hidden_local
-            pre = matmul(rows, both[part][0])
+            head, rest = weights[2 * part : 2 * part + 2]
+            up, down = [
+                jnp.concatenate(
+                    [
+                        head[2 * row_count :, number * hidden_local : (number + 1) * hidden_local],
+                        rest[:, number * hidden_local : (number + 1) * hidden_local],
+                    ],
+                    axis=0,
+                )
+                for number in range(2)
+            ]
+            pre = matmul(rows, up)
             square = pre * pre
             inner = 0.7978845608028654 * pre * (1.0 + 0.044715 * square)
             tanh = jnp.tanh(inner)
@@ -466,10 +505,10 @@
                 0.7978845608028654 * (1.0 + 3.0 * 0.044715 * square)
             )
             hidden_ref[:, at : at + hidden_local] = hidden
-            grad_pre = (matmul(total, both[part][1]) * slope).astype(BF16)
+            grad_pre = (matmul(total, down) * slope).astype(BF16)
             pre_ref[:, at : at + hidden_local] = grad_pre
-            forward += matmul_nt(hidden, both[part][1])
-            backward += matmul_nt(grad_pre, both[part][0])
+            forward += matmul_nt(hidden, down)
+            backward += matmul_nt(grad_pre, up)
         keep_ref[:, :width] = forward[:slot_rows]
         keep_ref[:, width:] = backward[:slot_rows]
         send_ref[:, :width] = forward[slot_rows:].astype(BF16)
@@ -490,34 +529,45 @@
     )
     arrived = swap(send, "dp", 2)
 
-    def expert_grads(idx, rows_ref, total_ref, hidden_ref, pre_ref, own_ref, y_ref, c_ref):
-        for part in range(parts):
-            at = part * hidden_local
-            up_grad = matmul_tn(rows_ref[...], pre_ref[:, at : at + hidden_local])
-            down_grad = matmul_tn(total_ref[...], hidden_ref[:, at : at + hidden_local])
-            ref, first = ((own_ref, 0), (y_ref, 0), (c_ref, 0), (c_ref, 2))[part]
-            ref[first] = up_grad.astype(ref.dtype)
-            ref[first + 1] = down_grad.astype(ref.dtype)
+    def expert_grads(first):
+        def grads(idx, rows_ref, total_ref, hidden_ref, pre_ref, *outs):
+            for part in range(2):
+                at = (first + part) * hidden_local
+                up_grad = matmul_tn(rows_ref[...], pre_ref[:, at : at + hidden_local])
+                down_grad = matmul_tn(total_ref[...], hidden_ref[:, at : at + hidden_local])
+                ref, place = (outs[0], 2 * part) if len(outs) == 1 else (outs[part], 0)
+                ref[place] = up_grad.astype(ref.dtype)
+                ref[place + 1] = down_grad.astype(ref.dtype)
+
+        return grads
 
     weight_shape = (width, hidden_local)
-    grads_own, grads_y, grads_c = run(
-        expert_grads,
-        scalars,
-        [rows_in, total_in, hidden, grad_pre],
-        [
-            shape_of((2,) + weight_shape, F32),
-            shape_of((2,) + weight_shape, BF16),
-            shape_of((4,) + weight_shape, BF16),
-        ],
+    grad_inputs = [rows_in, total_in, hidden, grad_pre]
+    (grads_c,) = run(
+        expert_grads(2), scalars, grad_inputs, [shape_of((4,) + weight_shape, BF16)]
+    )
+    grads_own, grads_y = run(
+        expert_grads(0),
+        scalars,
+        grad_inputs,
+        [shape_of((2,) + weight_shape, F32), shape_of((2,) + weight_shape, BF16)],
     )
     from_c = swap(grads_c, "dp", 1)
 
     def fold_y(idx, y_ref, c_ref, up_ref, down_ref):
         for number, ref in enumerate((up_ref, down_ref)):
-            ref[...] = (y_ref[number].astype(F32) + c_ref[2 + number].astype(F32)).astype(BF16)
+            total = y_ref[number].astype(F32) + c_ref[2 + number].astype(F32)
+            if number == 0:
+                ref[...] = total.astype(BF16)
+            else:
+                ref[:, :hidden_local] = total[: width // 2].astype(BF16)
+                ref[:, hidden_local:] = total[width // 2 :].astype(BF16)
 
     up_passed, down_passed = run(
-        fold_y, scalars, [grads_y, from_c], [shape_of(weight_shape, BF16)] * 2
+        fold_y,
+        scalars,
+        [grads_y, from_c],
+        [shape_of(weight_shape, BF16), shape_of((width // 2, 2 * hidden_local), BF16)],
     )
     up_from_y = swap(up_passed, "tensor", 1)
 
@@ -529,16 +579,27 @@
     home = over_z(list(back))
 
     def fold_grad(number):
-        def fold(idx, own_ref, c_ref, y_ref, out_ref):
-            out_ref[...] = own_ref[number] + c_ref[number].astype(F32) + y_ref[...].astype(F32)
+        def fold(idx, own_ref, c_ref, y_ref, out_ref, done_ref):
+            done_ref[...] = jnp.zeros(done_ref.shape, F32)
+            if number == 0:
+                out_ref[...] = own_ref[0] + c_ref[0].astype(F32) + y_ref[...].astype(F32)
+                return
+            for part in range(2):
+                rows = slice(part * (width // 2), (part + 1) * (width // 2))
+                columns = slice(part * hidden_local, (part + 1) * hidden_local)
+                out_ref[rows, :] = (
+                    own_ref[1, rows, :]
+                    + c_ref[1, rows, :].astype(F32)
+                    + y_ref[slot_rows + row_count :, columns].astype(F32)
+                )
 
         return fold
 
-    (grad_w_in,) = run(
+    grad_w_in, up_done = run(
         fold_grad(0),
         scalars,
         [grads_own, from_c, up_from_y],
-        [shape_of(weight_shape, F32)],
+        [shape_of(weight_shape, F32), shape_of((8, LANES), F32)],
         after=[back[0]],
     )
 
@@ -598,12 +659,12 @@
             shape_of((8, width), F32),
             shape_of((expert_pad, width), F32),
         ],
-        after=[grad_w_in],
+        after=[up_done],
     )
     mid_other = swap(mid_own, "tensor", 1)
 
     half_pieces = 2 * expert_count
-    first_part = weight_columns * 2 // 3 // LANES * LANES
+    first_part = weight_columns * 3 // 4 // LANES * LANES
 
     def emit_rows(idx, full_ref, outs):
         if not staged:
@@ -652,6 +713,8 @@
         live_ref,
         moe_ref,
         router_ref,
+        layer_ref,
+        down_ref,
         *refs,
     ):
         ga_ref, keep_ref, send_ref, small_ref = refs[:4]
@@ -717,8 +780,11 @@
         own_at = pl.multiple_of(idx[Y_AT] * row_count, row_count)
         other_at = pl.multiple_of((1 - idx[Y_AT]) * row_count, row_count)
         keep_ref[...] = upstream[pl.ds(own_at, row_count), :]
-        send_ref[:row_count, :] = upstream[pl.ds(other_at, row_count), :].astype(BF16)
-        store_halves(send_ref, row_count, small_ref[...])
+        send_ref[slot_rows : slot_rows + row_count, :] = upstream[
+            pl.ds(other_at, row_count), :
+        ].astype(BF16)
+        send_ref[:slot_rows, :] = layer_ref[...]
+        send_ref[slot_rows + row_count :, :] = down_ref[...]
         full[:, :qkv_width] = matmul_tn(normed_ref[...], all_grads)
         emit_rows(idx, full, outs)
 
@@ -740,11 +806,13 @@
             live_rows,
             gain_moe,
             router_part,
+            layer_own,
+            down_passed,
         ],
         [
             shape_of((block_len, width), BF16),
             shape_of((row_count, width), F32),
-            shape_of((row_count + 2 * small_rows, width), BF16),
+            shape_of((slot_rows + row_count + width // 2, width), BF16),
             shape_of((small_rows, width), F32),
         ]
         + row_shapes,
@@ -754,24 +822,32 @@
             pltpu.VMEM((block_len, width), F32),
         ],
     )
+    def small_over_y(idx, small_ref, other_ref, out_ref):
+        out_ref[...] = small_ref[...] + other_ref[...]
+
+    (small,) = run(
+        small_over_y,
+        scalars,
+        [small, swap(small, "tensor", 1)],
+        [shape_of((small_rows, width), F32)],
+    )
+    up_send, _ = lax.optimization_barrier((up_send, small))
     up_other = swap(up_send, "tensor", 1)
-    down_passed, _ = lax.optimization_barrier((down_passed, up_other))
-    down_from_y = swap(down_passed, "tensor", 1)
-
-    def small_over_y(idx, small_ref, other_ref, out_ref):
-        out_ref[...] = small_ref[...] + load_halves(other_ref, row_count)
-
-    (small,) = run(
-        small_over_y, scalars, [small, up_other], [shape_of((small_rows, width), F32)]
-    )
 
     out_shapes = [shape_of((shard_rows, head_width), F32)] * 4
     if staged:
         held, outgoing = partial_rows
         from_core = swap(outgoing, "dp", 1)
 
-        def after_core(idx, held_ref, from_ref, x_send, x_keep, *z_refs):
-            z_sends, z_keep = z_refs[:-1], z_refs[-1]
+        small_core = swap(small, "dp", 1)
+        x_rows = expert_count * shard_rows
+
+        def after_core(idx, small_ref, small_core, held_ref, from_ref, x_send, x_keep, *z_refs):
+            z_sends, z_keep, small_keep = z_refs[:-2], z_refs[-2], z_refs[-1]
+            small = small_ref[...] + small_core[...]
+            small_keep[...] = small
+            x_send[x_rows:, :] = jnp.zeros((2 * small_rows, first_part), BF16)
+            store_halves(x_send, x_rows, small)
 
             def total(number, columns):
                 return held_ref[number, :, columns] + from_ref[number, :, columns].astype(F32)
@@ -779,7 +855,9 @@
             front, rest = slice(0, first_part), slice(first_part, weight_columns)
             for j in range(expert_count):
                 x_keep[j] = total(j, front)
-                x_send[j] = total(expert_count + j, front).astype(BF16)
+                x_send[j * shard_rows : (j + 1) * shard_rows, :] = total(
+                    expert_count + j, front
+                ).astype(BF16)
                 for x in range(2):
                     piece = total(x * expert_count + j, rest)
                     if j == 0:
@@ -788,32 +866,32 @@
                         z_sends[j - 1][x] = piece.astype(BF16)
 
         rest_part = weight_columns - first_part
-        x_send, x_keep, *z_sends, z_keep = run(
+        x_send, x_keep, *z_sends, z_keep, small = run(
             after_core,
             scalars,
-            [held, from_core],
+            [small, small_core, held, from_core],
             [
-                shape_of((expert_count, shard_rows, first_part), BF16),
+                shape_of((x_rows + 2 * small_rows, first_part), BF16),
                 shape_of((expert_count, shard_rows, first_part), F32),
             ]
             + [shape_of((2, shard_rows, rest_part), BF16)] * (expert_count - 1)
-            + [shape_of((2, shard_rows, rest_part), F32)],
+            + [shape_of((2, shard_rows, rest_part), F32), shape_of((small_rows, width), F32)],
         )
         from_x = swap(x_send, "dp", 2)
         from_z = [swap(piece, "dp", z_masks[j + 1]) for j, piece in enumerate(z_sends)]
 
-        small = small + swap(small, "dp", 1)
-        small_x = swap(small, "dp", 2)
-
-        def after_first(idx, small_ref, small_x_ref, x_keep, from_x, z_keep, *refs):
+
+        def after_first(idx, small_ref, x_keep, from_x, z_keep, *refs):
             from_z, refs = refs[: expert_count - 1], refs[expert_count - 1 :]
             z_sends, (front_keep, x_send, rest_keep, small_keep) = refs[:-4], refs[-4:]
-            small = small_ref[...] + small_x_ref[...]
+            small = small_ref[...] + load_halves(from_x, x_rows)
             small_keep[...] = small
-            front_keep[...] = x_keep[0] + from_x[0].astype(F32)
+            front_keep[...] = x_keep[0] + from_x[:shard_rows, :].astype(F32)
             for j in range(1, expert_count):
                 z_sends[j - 1][...] = jnp.zeros(z_sends[j - 1].shape, BF16)
-                z_sends[j - 1][:shard_rows, :] = (x_keep[j] + from_x[j].astype(F32)).astype(BF16)
+                z_sends[j - 1][:shard_rows, :] = (
+                    x_keep[j] + from_x[j * shard_rows : (j + 1) * shard_rows, :].astype(F32)
+                ).astype(BF16)
                 store_halves(z_sends[j - 1], shard_rows, small)
             rest = z_keep[...]
             for ref in from_z:
@@ -824,7 +902,7 @@
         *z_sends, front_keep, x_send, rest_keep, small = run(
             after_first,
             scalars,
-            [small, small_x, x_keep, from_x, z_keep] + from_z,
+            [small, x_keep, from_x, z_keep] + from_z,
             [shape_of((shard_rows + 2 * small_rows, first_part), BF16)] * (expert_count - 1)
             + [
                 shape_of((shard_rows, first_part), F32),
@@ -888,29 +966,26 @@
         table = lax.dynamic_slice_in_dim(small, expert_count + 2 + y_index, 1, 0)
         table = table[0, : local_heads * LANES].reshape(local_heads, LANES)[:, :bucket_count].T
 
-    (grad_w_out,) = run(
+    grad_w_out, _ = run(
         fold_grad(1),
         scalars,
-        [grads_own, from_c, down_from_y],
-        [shape_of(weight_shape, F32)],
+        [grads_own, from_c, up_other],
+        [shape_of(weight_shape, F32), shape_of((8, LANES), F32)],
         after=late,
     )
-    if late:
-        layer_own, _ = lax.optimization_barrier((layer_own, late[0]))
-    layer_other = swap(layer_own, "tensor", 1)
-
     def finish(
-        idx, own_ref, other_ref, layer_ref, layer_other_ref, ga_ref, keep_ref, arrived_ref,
-        tok_ref, gain_ref, layer_out, tokens_out, full
+        idx, own_ref, other_ref, layer_ref, arrived_ref, ga_ref, keep_ref, tok_ref, gain_ref,
+        layer_out, tokens_out, full
     ):
         own_at = pl.multiple_of(idx[Y_AT] * row_count, row_count)
         full[...] = matmul_tn(own_ref[...], layer_ref[...]) + matmul_tn(
-            other_ref[...], layer_other_ref[...]
+            other_ref[...], arrived_ref[:slot_rows, :]
         )
         layer_out[...] = full[pl.ds(own_at, row_count), :].astype(BF16)
         x = tok_ref[...].astype(F32)
         scale = inverse_rms(x)
-        scaled = (keep_ref[...] + arrived_ref[:row_count, :].astype(F32)) * gain_ref[:1, :]
+        scaled = keep_ref[...] + arrived_ref[slot_rows : slot_rows + row_count, :].astype(F32)
+        scaled = scaled * gain_ref[:1, :]
         grad = scale * scaled - x * scale**3 * jnp.mean(scaled * x, axis=-1, keepdims=True)
         grad = grad + ga_ref[pl.ds(own_at, row_count), :].astype(F32)
         tokens_out[...] = grad.astype(BF16)
@@ -919,8 +994,7 @@
         finish,
         scalars,
         [
-            own_select, other_select, layer_own, layer_other, grad_attention, up_keep, up_other,
-            tokens, gains,
+            own_select, other_select, layer_own, up_other, grad_attention, up_keep, tokens, gains,
         ],
         [shape_of((row_count, width), BF16)] * 2,
         [pltpu.VMEM((block_len, width), F32)],

time: 171 us -> 153 us (0.89)
  waiting for transfers between devices: 80.2 us -> 71.5 us
  starting transfers between devices: 56 us -> 50.1 us
  local copies, waits for them, and re-layouts: 5.89 us -> 1.9 us
    ppermute x52, waiting for transfers between devices: 80.2 us -> 71.5 us  [swap(): return lax.ppermute(values, axis, [(i, i ^ mask) for i in range(count)])]
    ppermute x52, starting transfers between devices: 56 us -> 50.1 us  [swap(): return lax.ppermute(values, axis, [(i, i ^ mask) for i in range(count)])]
    unnamed x18 -> x12, local copies, waits for them, and re-layouts: 5.89 us -> 1.9 us
    pallas_call x17 -> x18, Pallas kernels: 27.8 us -> 27.9 us  [run(): pl.pallas_call(wrapped, out_shape=list(outs), in_specs=[pl.BlockSpec(memo...]
  transfers between devices with their start and end apart: 52 -> 52, of which waited for: 27 -> 27; matrix products, arithmetic and copies ran while one was open for 0% -> 0% of each run, Pallas kernels for 5% -> 7%
where the time goes in v3:
time: 153 us; the launch traced here: 152 us
  waiting for transfers between devices  71.5 us (47%)
  starting transfers between devices  50.1 us (33%)
  Pallas kernels  27.9 us (18%)
  local copies, waits for them, and re-layouts  1.9 us (1%)
    ppermute x52, waiting for transfers between devices, swap(): return lax.ppermute(values, axis, [(i, i ^ mask) for i in range(count)])  71.5 us
    ppermute x52, starting transfers between devices, swap(): return lax.ppermute(values, axis, [(i, i ^ mask) for i in range(count)])  50.1 us
    pallas_call x18, Pallas kernels, run(): pl.pallas_call(wrapped, out_shape=list(outs), in_specs=[pl.BlockSpec(memo...  27.9 us
  transfers between devices with their start and end apart: 52, of which 27 were waited for; matrix products, arithmetic and copies ran while one was open for 0% of the time, Pallas kernels for 7%

profile of v3, /device:TPU:0, one launch (start us, length us, event | category | flops | bytes accessed | tf_op | source)
XLA Modules:
  0.0 152.3 jit_solution(16065030616360790311)
XLA Ops:
  0.7 2.9 %shard_map.238 = (bf16[48,1664]{1,0:T(8,128)(2,1)}, bf16[512,768]{1,0:T(8,128)(2,1)}, bf16[512,768]{1,0:T(8,128)(2,1)}, f32[16,512]{1,0:T(8,128)}) custom-call(s32[1]{0:T(128)} %bitcast.place_ref, bf16[48,384]{1,0:T(8,128)(2,1)} %refs_0_.1, bf16[48,384]{1,0:T(8,128)(2,1)} %refs_1_.1, bf16[48,384]{1,0:T(8,128)(2,1)} %refs_2_.1, bf16[48,384]{1,0:T(8,128)(2,1)} %refs_3_.1, ...), custom_call_target="tpu_custom_call" | custom-call | flops 1 | bytes 1 | tf_op jit(solution)/shard_map/pallas_call | solution.py:68
  3.6 3.0 %collective-permute-start = (bf16[512,768]{1,0:T(8,128)(2,1)}, bf16[512,768]{1,0:T(8,128)(2,1)S(1)}, u32[]{:S(2)}, u32[]{:S(2)}) collective-permute-start(bf16[512,768]{1,0:T(8,128)(2,1)} %get-tuple-element.113.refs_1_.refs_14_), channel_id=1, source_target_pairs={{0,1},{1,0},{2,3},{3,2},{4,5},{5,4},{6,7},{7,6},{8,9},{9,8},{10,11... | collective-permute-start | bytes 2359304 | tf_op jit(solution)/shard_map/ppermute | solution.py:96
  6.6 3.6 %collective-permute-start.3 = (bf16[48,1664]{1,0:T(8,128)(2,1)}, bf16[48,1664]{1,0:T(8,128)(2,1)S(1)}, u32[]{:S(2)}, u32[]{:S(2)}) collective-permute-start(bf16[48,1664]{1,0:T(8,128)(2,1)} %get-tuple-element.128.refs_9_), channel_id=1, source_target_pairs={{0,24},{2,26},{4,28},{6,30},{8,16},{10,18},{12,20},{14,22},{16,8},... | collective-permute-start | bytes 479240 | tf_op jit(solution)/shard_map/ppermute | solution.py:96
  12.5 3.2 %collective-permute-done.3.refs_12_ = bf16[48,1664]{1,0:T(8,128)(2,1)S(1)} collective-permute-done((bf16[48,1664]{1,0:T(8,128)(2,1)}, bf16[48,1664]{1,0:T(8,128)(2,1)S(1)}, u32[]{:S(2)}, u32[]{:S(2)}) %collective-permute-start.3) | collective-permute-done | bytes 159776 | tf_op jit(solution)/shard_map/ppermute | solution.py:96
  17.2 6.5 %collective-permute-done.2.refs_11_ = bf16[48,1664]{1,0:T(8,128)(2,1)S(1)} collective-permute-done((bf16[48,1664]{1,0:T(8,128)(2,1)}, bf16[48,1664]{1,0:T(8,128)(2,1)S(1)}, u32[]{:S(2)}, u32[]{:S(2)}) %collective-permute-start.2) | collective-permute-done | bytes 159776 | tf_op jit(solution)/shard_map/ppermute | solution.py:96
  32.0 2.6 %collective-permute-start.5 = (bf16[40,768]{1,0:T(8,128)(2,1)S(1)}, bf16[40,768]{1,0:T(8,128)(2,1)S(1)}, u32[]{:S(2)}, u32[]{:S(2)}) collective-permute-start(bf16[40,768]{1,0:T(8,128)(2,1)S(1)} %get-tuple-element.122), channel_id=1, source_target_pairs={{0,16},{2,18},{4,20},{6,22},{8,24},{10,26},{12,28},{14,30},{16,0},... | collective-permute-start | bytes 184328 | tf_op jit(solution)/shard_map/ppermute | solution.py:96
  35.4 3.1 %collective-permute-done.5.refs_1_.refs_11_ = bf16[40,768]{1,0:T(8,128)(2,1)S(1)} collective-permute-done((bf16[40,768]{1,0:T(8,128)(2,1)S(1)}, bf16[40,768]{1,0:T(8,128)(2,1)S(1)}, u32[]{:S(2)}, u32[]{:S(2)}) %collective-permute-start.5) | collective-permute-done | bytes 61472 | tf_op jit(solution)/shard_map/ppermute | solution.py:96
  38.5 2.2 %collective-permute-done.6.refs_2_.refs_12_ = bf16[40,768]{1,0:T(8,128)(2,1)S(1)} collective-permute-done((bf16[40,768]{1,0:T(8,128)(2,1)S(1)}, bf16[40,768]{1,0:T(8,128)(2,1)S(1)}, u32[]{:S(2)}, u32[]{:S(2)}) %collective-permute-start.6) | collective-permute-done | bytes 61472 | tf_op jit(solution)/shard_map/ppermute | solution.py:96
  43.4 3.1 %shard_map.240 = (bf16[160,768]{1,0:T(8,128)(2,1)S(1)}, f32[160,768]{1,0:T(8,128)S(1)}, bf16[256,768]{1,0:T(8,128)(2,1)S(1)}, bf16[256,1152]{1,0:T(8,128)(2,1)S(...) custom-call(s32[1]{0:T(128)} %bitcast.place_ref, ...), custom_call_target="tpu_custom_call" | custom-call | flops 1 | bytes 1 | tf_op jit(solution)/shard_map/pallas_call | solution.py:68
  47.7 6.9 %collective-permute-done.22.refs_4_ = bf16[160,768]{1,0:T(8,128)(2,1)S(1)} collective-permute-done((bf16[160,768]{1,0:T(8,128)(2,1)S(1)}, bf16[160,768]{1,0:T(8,128)(2,1)S(1)}, u32[]{:S(2)}, u32[]{:S(2)}) %collective-permute-start.22) | collective-permute-done | bytes 245792 | tf_op jit(solution)/shard_map/ppermute | solution.py:96
  56.8 3.1 %collective-permute-start.25 = (bf16[40,768]{1,0:T(8,128)(2,1)S(1)}, bf16[40,768]{1,0:T(8,128)(2,1)S(1)}, u32[]{:S(2)}, u32[]{:S(2)}) collective-permute-start(bf16[40,768]{1,0:T(8,128)(2,1)S(1)} %get-tuple-element.144), channel_id=1, source_target_pairs={{0,24},{2,26},{4,28},{6,30},{8,16},{10,18},{12,20},{14,22},{16,8},... | collective-permute-start | bytes 184328 | tf_op jit(solution)/shard_map/ppermute | solution.py:96
  59.9 3.2 %collective-permute-done.30.refs_13_ = bf16[160,768]{1,0:T(8,128)(2,1)S(1)} collective-permute-done((bf16[160,768]{1,0:T(8,128)(2,1)S(1)}, bf16[160,768]{1,0:T(8,128)(2,1)S(1)}, u32[]{:S(2)}, u32[]{:S(2)}) %collective-permute-start.30) | collective-permute-done | bytes 245792 | tf_op jit(solution)/shard_map/ppermute | solution.py:96
  70.7 5.0 %shard_map.242 = (bf16[160,1536]{1,0:T(8,128)(2,1)S(1)}, f32[160,1536]{1,0:T(8,128)S(1)}, bf16[320,768]{1,0:T(8,128)(2,1)S(1)}, bf16[320,768]{1,0:T(8,128)(2,1)S...) custom-call(s32[1]{0:T(128)} %bitcast.place_ref, ...), custom_call_target="tpu_custom_call" | custom-call | flops 1 | bytes 1 | tf_op jit(solution)/shard_map/pallas_call | solution.py:68
  82.8 8.2 %collective-permute-done.33.refs_1_ = bf16[160,1536]{1,0:T(8,128)(2,1)S(1)} collective-permute-done((bf16[160,1536]{1,0:T(8,128)(2,1)S(1)}, bf16[160,1536]{1,0:T(8,128)(2,1)S(1)}, u32[]{:S(2)}, u32[]{:S(2)}) %collective-permute-start.33) | collective-permute-done | bytes 491552 | tf_op jit(solution)/shard_map/ppermute | solution.py:96
  92.5 3.1 %collective-permute-start.38 = (bf16[40,1536]{1,0:T(8,128)(2,1)S(1)}, bf16[40,1536]{1,0:T(8,128)(2,1)S(1)}, u32[]{:S(2)}, u32[]{:S(2)}) collective-permute-start(bf16[40,1536]{1,0:T(8,128)(2,1)S(1)} %get-tuple-element.161), channel_id=1, source_target_pairs={{0,24},{2,26},{4,28},{6,30},{8,16},{10,18},{12,20},{14,22},{16,8},... | collective-permute-start | bytes 368648 | tf_op jit(solution)/shard_map/ppermute | solution.py:96
  98.8 4.7 %collective-permute-done.37.refs_3_ = bf16[40,1536]{1,0:T(8,128)(2,1)S(1)} collective-permute-done((bf16[40,1536]{1,0:T(8,128)(2,1)S(1)}, bf16[40,1536]{1,0:T(8,128)(2,1)S(1)}, u32[]{:S(2)}, u32[]{:S(2)}) %collective-permute-start.37) | collective-permute-done | bytes 122912 | tf_op jit(solution)/shard_map/ppermute | solution.py:96
  105.6 5.7 %collective-permute-done.39.refs_3_ = bf16[160,768]{1,0:T(8,128)(2,1)S(1)} collective-permute-done((bf16[160,768]{1,0:T(8,128)(2,1)S(1)}, bf16[160,768]{1,0:T(8,128)(2,1)S(1)}, u32[]{:S(2)}, u32[]{:S(2)}) %collective-permute-start.39) | collective-permute-done | bytes 245792 | tf_op jit(solution)/shard_map/ppermute | solution.py:96
  111.3 5.6 %shard_map.249 = (bf16[256,768]{1,0:T(8,128)(2,1)S(1)}, f32[128,768]{1,0:T(8,128)S(1)}, bf16[672,768]{1,0:T(8,128)(2,1)S(1)}, f32[8,768]{1,0:T(8,128)S(1)}, f32[...) custom-call(s32[1]{0:T(128)} %bitcast.place_ref, ...), custom_call_target="tpu_custom_call" | custom-call | flops 1 | bytes 1 | tf_op jit(solution)/shard_map/pallas_call | solution.py:68
  117.6 3.3 %collective-permute-done.40.refs_1_ = f32[8,768]{1,0:T(8,128)S(1)} collective-permute-done((f32[8,768]{1,0:T(8,128)S(1)}, f32[8,768]{1,0:T(8,128)S(1)}, u32[]{:S(2)}, u32[]{:S(2)}) %collective-permute-start.40) | collective-permute-done | bytes 24608 | tf_op jit(solution)/shard_map/ppermute | solution.py:96
  126.0 2.4 %collective-permute-start.46 = (bf16[2,48,384]{2,1,0:T(8,128)(2,1)S(1)}, bf16[2,48,384]{2,1,0:T(8,128)(2,1)S(1)}, u32[]{:S(2)}, u32[]{:S(2)}) collective-permute-start(bf16[2,48,384]{2,1,0:T(8,128)(2,1)S(1)} %get-tuple-element.188), channel_id=1, source_target_pairs={{0,24},{2,26},{4,28},{6,30},{8,16},{10,18},{12,20},{14,22},{16,8},... | collective-permute-start | bytes 221192 | tf_op jit(solution)/shard_map/ppermute | solution.py:96
  128.6 5.8 %collective-permute-done.45.refs_5_ = bf16[2,48,384]{2,1,0:T(8,128)(2,1)S(1)} collective-permute-done((bf16[2,48,384]{2,1,0:T(8,128)(2,1)S(1)}, bf16[2,48,384]{2,1,0:T(8,128)(2,1)S(1)}, u32[]{:S(2)}, u32[]{:S(2)}) %collective-permute-start.45) | collective-permute-done | bytes 73760 | tf_op jit(solution)/shard_map/ppermute | solution.py:96
  138.1 2.4 %collective-permute-start.51 = (bf16[64,1152]{1,0:T(8,128)(2,1)S(1)}, bf16[64,1152]{1,0:T(8,128)(2,1)S(1)}, u32[]{:S(2)}, u32[]{:S(2)}) collective-permute-start(bf16[64,1152]{1,0:T(8,128)(2,1)S(1)} %get-tuple-element.201), channel_id=1, source_target_pairs={{0,24},{2,26},{4,28},{6,30},{8,16},{10,18},{12,20},{14,22},{16,8},... | collective-permute-start | bytes 442376 | tf_op jit(solution)/shard_map/ppermute | solution.py:96
  141.6 3.2 %collective-permute-done.47.refs_4_.refs_3_ = bf16[672,768]{1,0:T(8,128)(2,1)S(1)} collective-permute-done((bf16[672,768]{1,0:T(8,128)(2,1)S(1)}, bf16[672,768]{1,0:T(8,128)(2,1)S(1)}, u32[]{:S(2)}, u32[]{:S(2)}) %collective-permute-start.47) | collective-permute-done | bytes 1032224 | tf_op jit(solution)/shard_map/ppermute | solution.py:96
  147.3 3.9 %collective-permute-done.50.refs_5_ = bf16[64,1152]{1,0:T(8,128)(2,1)S(1)} collective-permute-done((bf16[64,1152]{1,0:T(8,128)(2,1)S(1)}, bf16[64,1152]{1,0:T(8,128)(2,1)S(1)}, u32[]{:S(2)}, u32[]{:S(2)}) %collective-permute-start.50) | collective-permute-done | bytes 147488 | tf_op jit(solution)/shard_map/ppermute | solution.py:96
  (111 shorter events, 54.8 us)
Async XLA Ops:
  3.6 21.6 %collective-permute-start = (bf16[512,768]{1,0:T(8,128)(2,1)}, bf16[512,768]{1,0:T(8,128)(2,1)S(1)}, u32[]{:S(2)}, u32[]{:S(2)}) collective-permute-start(bf16[512,768]{1,0:T(8,128)(2,1)} %get-tuple-element.113.refs_1_.refs_14_), channel_id=1, source_target_pairs={{0,1},{1,0},{2,3},{3,2},{4,5},{5,4},{6,7},{7,6},{8,9},{9,8},{10,11... | collective-permute-start | bytes 2359304 | tf_op jit(solution)/shard_map/ppermute | solution.py:96
  6.6 9.1 %collective-permute-start.3 = (bf16[48,1664]{1,0:T(8,128)(2,1)}, bf16[48,1664]{1,0:T(8,128)(2,1)S(1)}, u32[]{:S(2)}, u32[]{:S(2)}) collective-permute-start(bf16[48,1664]{1,0:T(8,128)(2,1)} %get-tuple-element.128.refs_9_), channel_id=1, source_target_pairs={{0,24},{2,26},{4,28},{6,30},{8,16},{10,18},{12,20},{14,22},{16,8},... | collective-permute-start | bytes 479240 | tf_op jit(solution)/shard_map/ppermute | solution.py:96
  10.2 13.5 %collective-permute-start.2 = (bf16[48,1664]{1,0:T(8,128)(2,1)}, bf16[48,1664]{1,0:T(8,128)(2,1)S(1)}, u32[]{:S(2)}, u32[]{:S(2)}) collective-permute-start(bf16[48,1664]{1,0:T(8,128)(2,1)} %get-tuple-element.128.refs_9_), channel_id=1, source_target_pairs={{0,16},{2,18},{4,20},{6,22},{8,24},{10,26},{12,28},{14,30},{16,0},... | collective-permute-start | bytes 479240 | tf_op jit(solution)/shard_map/ppermute | solution.py:96
  10.2 15.9 %collective-permute-start.1 = (bf16[48,1664]{1,0:T(8,128)(2,1)}, bf16[48,1664]{1,0:T(8,128)(2,1)S(1)}, u32[]{:S(2)}, u32[]{:S(2)}) collective-permute-start(bf16[48,1664]{1,0:T(8,128)(2,1)} %get-tuple-element.128.refs_9_), channel_id=1, source_target_pairs={{0,8},{2,10},{4,12},{6,14},{8,0},{10,2},{12,4},{14,6},{16,24},{18,... | collective-permute-start | bytes 479240 | tf_op jit(solution)/shard_map/ppermute | solution.py:96
  11.0 19.4 %collective-permute-start.7 = (bf16[48,1664]{1,0:T(8,128)(2,1)}, bf16[48,1664]{1,0:T(8,128)(2,1)S(1)}, u32[]{:S(2)}, u32[]{:S(2)}) collective-permute-start(bf16[48,1664]{1,0:T(8,128)(2,1)} %get-tuple-element.128.refs_9_), channel_id=1, source_target_pairs={{0,4},{2,6},{4,0},{6,2},{8,12},{10,14},{12,8},{14,10},{16,20},{18,... | collective-permute-start | bytes 479240 | tf_op jit(solution)/shard_map/ppermute | solution.py:96
  15.7 16.3 %collective-permute-start.10 = (bf16[48,1664]{1,0:T(8,128)(2,1)S(1)}, bf16[48,1664]{1,0:T(8,128)(2,1)S(1)}, u32[]{:S(2)}, u32[]{:S(2)}) collective-permute-start(bf16[48,1664]{1,0:T(8,128)(2,1)S(1)} %collective-permute-done.3.refs_12_), channel_id=1, source_target_pairs={{0,4},{2,6},{4,0},{6,2},{8,12},{10,14},{12,8},{14,10},{16,20},{18,... | collective-permute-start | bytes 479240 | tf_op jit(solution)/shard_map/ppermute | solution.py:96
  23.7 10.9 %collective-permute-start.9 = (bf16[48,1664]{1,0:T(8,128)(2,1)S(1)}, bf16[48,1664]{1,0:T(8,128)(2,1)S(1)}, u32[]{:S(2)}, u32[]{:S(2)}) collective-permute-start(bf16[48,1664]{1,0:T(8,128)(2,1)S(1)} %collective-permute-done.2.refs_11_), channel_id=1, source_target_pairs={{0,4},{2,6},{4,0},{6,2},{8,12},{10,14},{12,8},{14,10},{16,20},{18,... | collective-permute-start | bytes 479240 | tf_op jit(solution)/shard_map/ppermute | solution.py:96
  25.2 29.4 %collective-permute-start.31 = (bf16[512,768]{1,0:T(8,128)(2,1)}, bf16[512,768]{1,0:T(8,128)(2,1)S(1)}, u32[]{:S(2)}, u32[]{:S(2)}) collective-permute-start(bf16[512,768]{1,0:T(8,128)(2,1)} %get-tuple-element.146.refs_15_), channel_id=1, source_target_pairs={{0,1},{1,0},{2,3},{3,2},{4,5},{5,4},{6,7},{7,6},{8,9},{9,8},{10,11... | collective-permute-start | bytes 2359304 | tf_op jit(solution)/shard_map/ppermute | solution.py:96
  26.1 8.7 %collective-permute-start.8 = (bf16[48,1664]{1,0:T(8,128)(2,1)S(1)}, bf16[48,1664]{1,0:T(8,128)(2,1)S(1)}, u32[]{:S(2)}, u32[]{:S(2)}) collective-permute-start(bf16[48,1664]{1,0:T(8,128)(2,1)S(1)} %collective-permute-done.1.refs_10_), channel_id=1, source_target_pairs={{0,4},{2,6},{4,0},{6,2},{8,12},{10,14},{12,8},{14,10},{16,20},{18,... | collective-permute-start | bytes 479240 | tf_op jit(solution)/shard_map/ppermute | solution.py:96
  54.6 16.0 %collective-permute-start.32 = (bf16[512,768]{1,0:T(8,128)(2,1)S(1)}, bf16[512,768]{1,0:T(8,128)(2,1)S(1)}, u32[]{:S(2)}, u32[]{:S(2)}) collective-permute-start(bf16[512,768]{1,0:T(8,128)(2,1)S(1)} %collective-permute-done.31.refs_17_), channel_id=1, source_target_pairs={{0,2},{2,0},{4,6},{6,4},{8,10},{10,8},{12,14},{14,12},{16,18},{18,... | collective-permute-start | bytes 2359304 | tf_op jit(solution)/shard_map/ppermute | solution.py:96
  54.6 8.4 %collective-permute-start.30 = (bf16[160,768]{1,0:T(8,128)(2,1)S(1)}, bf16[160,768]{1,0:T(8,128)(2,1)S(1)}, u32[]{:S(2)}, u32[]{:S(2)}) collective-permute-start(bf16[160,768]{1,0:T(8,128)(2,1)S(1)} %pad_maximum_fusion), channel_id=1, source_target_pairs={{0,4},{2,6},{4,0},{6,2},{8,12},{10,14},{12,8},{14,10},{16,20},{18,... | collective-permute-start | bytes 737288 | tf_op jit(solution)/shard_map/ppermute | solution.py:96
  55.5 9.6 %collective-permute-start.24 = (bf16[40,768]{1,0:T(8,128)(2,1)S(1)}, bf16[40,768]{1,0:T(8,128)(2,1)S(1)}, u32[]{:S(2)}, u32[]{:S(2)}) collective-permute-start(bf16[40,768]{1,0:T(8,128)(2,1)S(1)} %get-tuple-element.143), channel_id=1, source_target_pairs={{0,16},{2,18},{4,20},{6,22},{8,24},{10,26},{12,28},{14,30},{16,0},... | collective-permute-start | bytes 184328 | tf_op jit(solution)/shard_map/ppermute | solution.py:96
  56.8 8.8 %collective-permute-start.25 = (bf16[40,768]{1,0:T(8,128)(2,1)S(1)}, bf16[40,768]{1,0:T(8,128)(2,1)S(1)}, u32[]{:S(2)}, u32[]{:S(2)}) collective-permute-start(bf16[40,768]{1,0:T(8,128)(2,1)S(1)} %get-tuple-element.144), channel_id=1, source_target_pairs={{0,24},{2,26},{4,28},{6,30},{8,16},{10,18},{12,20},{14,22},{16,8},... | collective-permute-start | bytes 184328 | tf_op jit(solution)/shard_map/ppermute | solution.py:96
  77.4 13.6 %collective-permute-start.33 = (bf16[160,1536]{1,0:T(8,128)(2,1)S(1)}, bf16[160,1536]{1,0:T(8,128)(2,1)S(1)}, u32[]{:S(2)}, u32[]{:S(2)}) collective-permute-start(bf16[160,1536]{1,0:T(8,128)(2,1)S(1)} %get-tuple-element.149), channel_id=1, source_target_pairs={{0,4},{2,6},{4,0},{6,2},{8,12},{10,14},{12,8},{14,10},{16,20},{18,... | collective-permute-start | bytes 1474568 | tf_op jit(solution)/shard_map/ppermute | solution.py:96
  82.2 15.4 %collective-permute-start.35 = (bf16[768,384]{1,0:T(8,128)(2,1)S(1)}, bf16[768,384]{1,0:T(8,128)(2,1)S(1)}, u32[]{:S(2)}, u32[]{:S(2)}) collective-permute-start(bf16[768,384]{1,0:T(8,128)(2,1)S(1)} %get-tuple-element.157), channel_id=1, source_target_pairs={{0,1},{1,0},{2,3},{3,2},{4,5},{5,4},{6,7},{7,6},{8,9},{9,8},{10,11... | collective-permute-start | bytes 1769480 | tf_op jit(solution)/shard_map/ppermute | solution.py:96
  91.2 12.3 %collective-permute-start.37 = (bf16[40,1536]{1,0:T(8,128)(2,1)S(1)}, bf16[40,1536]{1,0:T(8,128)(2,1)S(1)}, u32[]{:S(2)}, u32[]{:S(2)}) collective-permute-start(bf16[40,1536]{1,0:T(8,128)(2,1)S(1)} %get-tuple-element.160), channel_id=1, source_target_pairs={{0,16},{2,18},{4,20},{6,22},{8,24},{10,26},{12,28},{14,30},{16,0},... | collective-permute-start | bytes 368648 | tf_op jit(solution)/shard_map/ppermute | solution.py:96
  92.5 10.9 %collective-permute-start.38 = (bf16[40,1536]{1,0:T(8,128)(2,1)S(1)}, bf16[40,1536]{1,0:T(8,128)(2,1)S(1)}, u32[]{:S(2)}, u32[]{:S(2)}) collective-permute-start(bf16[40,1536]{1,0:T(8,128)(2,1)S(1)} %get-tuple-element.161), channel_id=1, source_target_pairs={{0,24},{2,26},{4,28},{6,30},{8,16},{10,18},{12,20},{14,22},{16,8},... | collective-permute-start | bytes 368648 | tf_op jit(solution)/shard_map/ppermute | solution.py:96
  120.9 24.0 %collective-permute-start.47 = (bf16[672,768]{1,0:T(8,128)(2,1)S(1)}, bf16[672,768]{1,0:T(8,128)(2,1)S(1)}, u32[]{:S(2)}, u32[]{:S(2)}) collective-permute-start(bf16[672,768]{1,0:T(8,128)(2,1)S(1)} %get-tuple-element.191), channel_id=1, source_target_pairs={{0,1},{1,0},{2,3},{3,2},{4,5},{5,4},{6,7},{7,6},{8,9},{9,8},{10,11... | collective-permute-start | bytes 3096584 | tf_op jit(solution)/shard_map/ppermute | solution.py:96
  122.8 13.1 %collective-permute-start.43 = (bf16[208,1152]{1,0:T(8,128)(2,1)S(1)}, bf16[208,1152]{1,0:T(8,128)(2,1)S(1)}, u32[]{:S(2)}, u32[]{:S(2)}) collective-permute-start(bf16[208,1152]{1,0:T(8,128)(2,1)S(1)} %get-tuple-element.184), channel_id=1, source_target_pairs={{0,4},{2,6},{4,0},{6,2},{8,12},{10,14},{12,8},{14,10},{16,20},{18,... | collective-permute-start | bytes 1437704 | tf_op jit(solution)/shard_map/ppermute | solution.py:96
  126.0 8.4 %collective-permute-start.45 = (bf16[2,48,384]{2,1,0:T(8,128)(2,1)S(1)}, bf16[2,48,384]{2,1,0:T(8,128)(2,1)S(1)}, u32[]{:S(2)}, u32[]{:S(2)}) collective-permute-start(bf16[2,48,384]{2,1,0:T(8,128)(2,1)S(1)} %get-tuple-element.187), channel_id=1, source_target_pairs={{0,16},{2,18},{4,20},{6,22},{8,24},{10,26},{12,28},{14,30},{16,0},... | collective-permute-start | bytes 221192 | tf_op jit(solution)/shard_map/ppermute | solution.py:96
  126.0 8.4 %collective-permute-start.46 = (bf16[2,48,384]{2,1,0:T(8,128)(2,1)S(1)}, bf16[2,48,384]{2,1,0:T(8,128)(2,1)S(1)}, u32[]{:S(2)}, u32[]{:S(2)}) collective-permute-start(bf16[2,48,384]{2,1,0:T(8,128)(2,1)S(1)} %get-tuple-element.188), channel_id=1, source_target_pairs={{0,24},{2,26},{4,28},{6,30},{8,16},{10,18},{12,20},{14,22},{16,8},... | collective-permute-start | bytes 221192 | tf_op jit(solution)/shard_map/ppermute | solution.py:96
  136.0 11.3 %collective-permute-start.49 = (bf16[64,1152]{1,0:T(8,128)(2,1)S(1)}, bf16[64,1152]{1,0:T(8,128)(2,1)S(1)}, u32[]{:S(2)}, u32[]{:S(2)}) collective-permute-start(bf16[64,1152]{1,0:T(8,128)(2,1)S(1)} %get-tuple-element.199), channel_id=1, source_target_pairs={{0,8},{2,10},{4,12},{6,14},{8,0},{10,2},{12,4},{14,6},{16,24},{18,... | collective-permute-start | bytes 442376 | tf_op jit(solution)/shard_map/ppermute | solution.py:96
  138.1 13.1 %collective-permute-start.50 = (bf16[64,1152]{1,0:T(8,128)(2,1)S(1)}, bf16[64,1152]{1,0:T(8,128)(2,1)S(1)}, u32[]{:S(2)}, u32[]{:S(2)}) collective-permute-start(bf16[64,1152]{1,0:T(8,128)(2,1)S(1)} %get-tuple-element.200), channel_id=1, source_target_pairs={{0,16},{2,18},{4,20},{6,22},{8,24},{10,26},{12,28},{14,30},{16,0},... | collective-permute-start | bytes 442376 | tf_op jit(solution)/shard_map/ppermute | solution.py:96
  138.1 13.1 %collective-permute-start.51 = (bf16[64,1152]{1,0:T(8,128)(2,1)S(1)}, bf16[64,1152]{1,0:T(8,128)(2,1)S(1)}, u32[]{:S(2)}, u32[]{:S(2)}) collective-permute-start(bf16[64,1152]{1,0:T(8,128)(2,1)S(1)} %get-tuple-element.201), channel_id=1, source_target_pairs={{0,24},{2,26},{4,28},{6,30},{8,16},{10,18},{12,20},{14,22},{16,8},... | collective-permute-start | bytes 442376 | tf_op jit(solution)/shard_map/ppermute | solution.py:96
  (34 other events, 156.1 us)

commit v4 on v3

--- a/solution.py
+++ b/solution.py
@@ -664,7 +664,9 @@
     mid_other = swap(mid_own, "tensor", 1)
 
     half_pieces = 2 * expert_count
-    first_part = weight_columns * 3 // 4 // LANES * LANES
+    rest_part = 2 * LANES
+    first_part = weight_columns - rest_part
+    small_blocks = width // rest_part
 
     def emit_rows(idx, full_ref, outs):
         if not staged:
@@ -689,13 +691,20 @@
 
     def store_halves(ref, at, values):
         high = values.astype(BF16)
-        ref[at : at + 2 * small_rows, :width] = jnp.concatenate(
-            [high.astype(F32), values - high.astype(F32)], axis=0
-        ).astype(BF16)
+        both = jnp.concatenate([high.astype(F32), values - high.astype(F32)], axis=0).astype(BF16)
+        for block in range(small_blocks):
+            row = at + 2 * small_rows * block
+            ref[row : row + 2 * small_rows, :] = both[
+                :, block * rest_part : (block + 1) * rest_part
+            ]
 
     def load_halves(ref, at):
-        both = ref[at : at + 2 * small_rows, :width].astype(F32)
-        return both[:small_rows] + both[small_rows:]
+        blocks = []
+        for block in range(small_blocks):
+            row = at + 2 * small_rows * block
+            both = ref[row : row + 2 * small_rows, :].astype(F32)
+            blocks.append(both[:small_rows] + both[small_rows:])
+        return jnp.concatenate(blocks, axis=1)
 
     def attend_back(
         idx,
@@ -840,14 +849,12 @@
         from_core = swap(outgoing, "dp", 1)
 
         small_core = swap(small, "dp", 1)
-        x_rows = expert_count * shard_rows
+        extra_rows = 2 * small_rows * small_blocks
 
         def after_core(idx, small_ref, small_core, held_ref, from_ref, x_send, x_keep, *z_refs):
             z_sends, z_keep, small_keep = z_refs[:-2], z_refs[-2], z_refs[-1]
             small = small_ref[...] + small_core[...]
             small_keep[...] = small
-            x_send[x_rows:, :] = jnp.zeros((2 * small_rows, first_part), BF16)
-            store_halves(x_send, x_rows, small)
 
             def total(number, columns):
                 return held_ref[number, :, columns] + from_ref[number, :, columns].astype(F32)
@@ -855,26 +862,27 @@
             front, rest = slice(0, first_part), slice(first_part, weight_columns)
             for j in range(expert_count):
                 x_keep[j] = total(j, front)
-                x_send[j * shard_rows : (j + 1) * shard_rows, :] = total(
-                    expert_count + j, front
-                ).astype(BF16)
+                x_send[j] = total(expert_count + j, front).astype(BF16)
+                if j > 0:
+                    store_halves(z_sends[j - 1], 2 * shard_rows, small)
                 for x in range(2):
                     piece = total(x * expert_count + j, rest)
                     if j == 0:
                         z_keep[x] = piece
                     else:
-                        z_sends[j - 1][x] = piece.astype(BF16)
-
-        rest_part = weight_columns - first_part
+                        z_sends[j - 1][x * shard_rows : (x + 1) * shard_rows, :] = piece.astype(
+                            BF16
+                        )
+
         x_send, x_keep, *z_sends, z_keep, small = run(
             after_core,
             scalars,
             [small, small_core, held, from_core],
             [
-                shape_of((x_rows + 2 * small_rows, first_part), BF16),
+                shape_of((expert_count, shard_rows, first_part), BF16),
                 shape_of((expert_count, shard_rows, first_part), F32),
             ]
-            + [shape_of((2, shard_rows, rest_part), BF16)] * (expert_count - 1)
+            + [shape_of((2 * shard_rows + extra_rows, rest_part), BF16)] * (expert_count - 1)
             + [shape_of((2, shard_rows, rest_part), F32), shape_of((small_rows, width), F32)],
         )
         from_x = swap(x_send, "dp", 2)
@@ -884,29 +892,28 @@
         def after_first(idx, small_ref, x_keep, from_x, z_keep, *refs):
             from_z, refs = refs[: expert_count - 1], refs[expert_count - 1 :]
             z_sends, (front_keep, x_send, rest_keep, small_keep) = refs[:-4], refs[-4:]
-            small = small_ref[...] + load_halves(from_x, x_rows)
+            front_keep[...] = x_keep[0] + from_x[0].astype(F32)
+            for j in range(1, expert_count):
+                z_sends[j - 1][...] = (x_keep[j] + from_x[j].astype(F32)).astype(BF16)
+            small = small_ref[...]
+            rest = [z_keep[0], z_keep[1]]
+            for ref in from_z:
+                small = small + load_halves(ref, 2 * shard_rows)
+                for x in range(2):
+                    rest[x] = rest[x] + ref[x * shard_rows : (x + 1) * shard_rows, :].astype(F32)
             small_keep[...] = small
-            front_keep[...] = x_keep[0] + from_x[:shard_rows, :].astype(F32)
-            for j in range(1, expert_count):
-                z_sends[j - 1][...] = jnp.zeros(z_sends[j - 1].shape, BF16)
-                z_sends[j - 1][:shard_rows, :] = (
-                    x_keep[j] + from_x[j * shard_rows : (j + 1) * shard_rows, :].astype(F32)
-                ).astype(BF16)
-                store_halves(z_sends[j - 1], shard_rows, small)
-            rest = z_keep[...]
-            for ref in from_z:
-                rest = rest + ref[...].astype(F32)
+            store_halves(x_send, shard_rows, small)
             rest_keep[...] = rest[0]
-            x_send[...] = rest[1].astype(BF16)
+            x_send[:shard_rows, :] = rest[1].astype(BF16)
 
         *z_sends, front_keep, x_send, rest_keep, small = run(
             after_first,
             scalars,
             [small, x_keep, from_x, z_keep] + from_z,
-            [shape_of((shard_rows + 2 * small_rows, first_part), BF16)] * (expert_count - 1)
+            [shape_of((shard_rows, first_part), BF16)] * (expert_count - 1)
             + [
                 shape_of((shard_rows, first_part), F32),
-                shape_of((shard_rows, rest_part), BF16),
+                shape_of((shard_rows + extra_rows, rest_part), BF16),
                 shape_of((shard_rows, rest_part), F32),
                 shape_of((small_rows, width), F32),
             ],
@@ -919,10 +926,9 @@
             from_z, refs = refs[: expert_count - 1], refs[expert_count - 1 :]
             outs, (attn_out, moe_out, router_out, table_out, full) = refs[:-5], refs[-5:]
             front = front_keep[...]
-            small = small_ref[...]
+            small = small_ref[...] + load_halves(from_x, shard_rows)
             for ref in from_z:
-                front = front + ref[:shard_rows, :].astype(F32)
-                small = small + load_halves(ref, shard_rows)
+                front = front + ref[...].astype(F32)
             column = iota((LANES, width), 1) - idx[DATA_AT] * shard_rows
             select = (column == iota((LANES, width), 0)).astype(F32)
             shard = matmul_nt(small, select, HIGHEST)
@@ -934,7 +940,7 @@
             lines = [line[:, head * LANES : (head + 1) * LANES] for head in range(local_heads)]
             table_out[...] = jnp.concatenate(lines, axis=0)[:, :bucket_count]
             full[:, :first_part] = front
-            full[:, first_part:] = rest_keep[...] + from_x[...].astype(F32)
+            full[:, first_part:] = rest_keep[...] + from_x[:shard_rows, :].astype(F32)
             for number, out in enumerate(outs):
                 out[...] = full[:, number * head_width : (number + 1) * head_width]
 

time: 153 us -> 151 us (0.987)
    ppermute x52, waiting for transfers between devices: 71.5 us -> 70 us  [swap(): return lax.ppermute(values, axis, [(i, i ^ mask) for i in range(count)])]
where the time goes in v4:
time: 151 us
  waiting for transfers between devices  70 us (46%)
  starting transfers between devices  50.1 us (33%)
  Pallas kernels  27.8 us (18%)
  local copies, waits for them, and re-layouts  1.9 us (1%)
    ppermute x52, waiting for transfers between devices, swap(): return lax.ppermute(values, axis, [(i, i ^ mask) for i in range(count)])  70 us
    ppermute x52, starting transfers between devices, swap(): return lax.ppermute(values, axis, [(i, i ^ mask) for i in range(count)])  50.1 us
    pallas_call x18, Pallas kernels, run(): pl.pallas_call(wrapped, out_shape=list(outs), in_specs=[pl.BlockSpec(memo...  27.8 us
  transfers between devices with their start and end apart: 52, of which 27 were waited for; matrix products, arithmetic and copies ran while one was open for 0% of the time, Pallas kernels for 7%

profile of v4, /device:TPU:0, one launch (start us, length us, event | category | flops | bytes accessed | tf_op | source)
XLA Modules:
  0.0 150.7 jit_solution(868763538822292303)
XLA Ops:
  0.7 2.9 %shard_map.238 = (bf16[48,1664]{1,0:T(8,128)(2,1)}, bf16[512,768]{1,0:T(8,128)(2,1)}, bf16[512,768]{1,0:T(8,128)(2,1)}, f32[16,512]{1,0:T(8,128)}) custom-call(s32[1]{0:T(128)} %bitcast.place_ref, bf16[48,384]{1,0:T(8,128)(2,1)} %refs_0_.1, bf16[48,384]{1,0:T(8,128)(2,1)} %refs_1_.1, bf16[48,384]{1,0:T(8,128)(2,1)} %refs_2_.1, bf16[48,384]{1,0:T(8,128)(2,1)} %refs_3_.1, ...), custom_call_target="tpu_custom_call" | custom-call | flops 1 | bytes 1 | tf_op jit(solution)/shard_map/pallas_call | solution.py:68
  3.6 3.0 %collective-permute-start = (bf16[512,768]{1,0:T(8,128)(2,1)}, bf16[512,768]{1,0:T(8,128)(2,1)S(1)}, u32[]{:S(2)}, u32[]{:S(2)}) collective-permute-start(bf16[512,768]{1,0:T(8,128)(2,1)} %get-tuple-element.113.refs_1_.refs_14_), channel_id=1, source_target_pairs={{0,1},{1,0},{2,3},{3,2},{4,5},{5,4},{6,7},{7,6},{8,9},{9,8},{10,11... | collective-permute-start | bytes 2359304 | tf_op jit(solution)/shard_map/ppermute | solution.py:96
  6.6 3.6 %collective-permute-start.3 = (bf16[48,1664]{1,0:T(8,128)(2,1)}, bf16[48,1664]{1,0:T(8,128)(2,1)S(1)}, u32[]{:S(2)}, u32[]{:S(2)}) collective-permute-start(bf16[48,1664]{1,0:T(8,128)(2,1)} %get-tuple-element.128.refs_9_), channel_id=1, source_target_pairs={{0,24},{2,26},{4,28},{6,30},{8,16},{10,18},{12,20},{14,22},{16,8},... | collective-permute-start | bytes 479240 | tf_op jit(solution)/shard_map/ppermute | solution.py:96
  12.5 3.2 %collective-permute-done.3.refs_12_ = bf16[48,1664]{1,0:T(8,128)(2,1)S(1)} collective-permute-done((bf16[48,1664]{1,0:T(8,128)(2,1)}, bf16[48,1664]{1,0:T(8,128)(2,1)S(1)}, u32[]{:S(2)}, u32[]{:S(2)}) %collective-permute-start.3) | collective-permute-done | bytes 159776 | tf_op jit(solution)/shard_map/ppermute | solution.py:96
  17.2 6.5 %collective-permute-done.2.refs_11_ = bf16[48,1664]{1,0:T(8,128)(2,1)S(1)} collective-permute-done((bf16[48,1664]{1,0:T(8,128)(2,1)}, bf16[48,1664]{1,0:T(8,128)(2,1)S(1)}, u32[]{:S(2)}, u32[]{:S(2)}) %collective-permute-start.2) | collective-permute-done | bytes 159776 | tf_op jit(solution)/shard_map/ppermute | solution.py:96
  32.0 2.6 %collective-permute-start.5 = (bf16[40,768]{1,0:T(8,128)(2,1)S(1)}, bf16[40,768]{1,0:T(8,128)(2,1)S(1)}, u32[]{:S(2)}, u32[]{:S(2)}) collective-permute-start(bf16[40,768]{1,0:T(8,128)(2,1)S(1)} %get-tuple-element.122), channel_id=1, source_target_pairs={{0,16},{2,18},{4,20},{6,22},{8,24},{10,26},{12,28},{14,30},{16,0},... | collective-permute-start | bytes 184328 | tf_op jit(solution)/shard_map/ppermute | solution.py:96
  35.4 3.1 %collective-permute-done.5.refs_1_.refs_11_ = bf16[40,768]{1,0:T(8,128)(2,1)S(1)} collective-permute-done((bf16[40,768]{1,0:T(8,128)(2,1)S(1)}, bf16[40,768]{1,0:T(8,128)(2,1)S(1)}, u32[]{:S(2)}, u32[]{:S(2)}) %collective-permute-start.5) | collective-permute-done | bytes 61472 | tf_op jit(solution)/shard_map/ppermute | solution.py:96
  38.5 2.2 %collective-permute-done.6.refs_2_.refs_12_ = bf16[40,768]{1,0:T(8,128)(2,1)S(1)} collective-permute-done((bf16[40,768]{1,0:T(8,128)(2,1)S(1)}, bf16[40,768]{1,0:T(8,128)(2,1)S(1)}, u32[]{:S(2)}, u32[]{:S(2)}) %collective-permute-start.6) | collective-permute-done | bytes 61472 | tf_op jit(solution)/shard_map/ppermute | solution.py:96
  43.4 3.1 %shard_map.240 = (bf16[160,768]{1,0:T(8,128)(2,1)S(1)}, f32[160,768]{1,0:T(8,128)S(1)}, bf16[256,768]{1,0:T(8,128)(2,1)S(1)}, bf16[256,1152]{1,0:T(8,128)(2,1)S(...) custom-call(s32[1]{0:T(128)} %bitcast.place_ref, ...), custom_call_target="tpu_custom_call" | custom-call | flops 1 | bytes 1 | tf_op jit(solution)/shard_map/pallas_call | solution.py:68
  47.7 6.9 %collective-permute-done.22.refs_4_ = bf16[160,768]{1,0:T(8,128)(2,1)S(1)} collective-permute-done((bf16[160,768]{1,0:T(8,128)(2,1)S(1)}, bf16[160,768]{1,0:T(8,128)(2,1)S(1)}, u32[]{:S(2)}, u32[]{:S(2)}) %collective-permute-start.22) | collective-permute-done | bytes 245792 | tf_op jit(solution)/shard_map/ppermute | solution.py:96
  56.8 3.1 %collective-permute-start.25 = (bf16[40,768]{1,0:T(8,128)(2,1)S(1)}, bf16[40,768]{1,0:T(8,128)(2,1)S(1)}, u32[]{:S(2)}, u32[]{:S(2)}) collective-permute-start(bf16[40,768]{1,0:T(8,128)(2,1)S(1)} %get-tuple-element.144), channel_id=1, source_target_pairs={{0,24},{2,26},{4,28},{6,30},{8,16},{10,18},{12,20},{14,22},{16,8},... | collective-permute-start | bytes 184328 | tf_op jit(solution)/shard_map/ppermute | solution.py:96
  59.9 3.2 %collective-permute-done.30.refs_13_ = bf16[160,768]{1,0:T(8,128)(2,1)S(1)} collective-permute-done((bf16[160,768]{1,0:T(8,128)(2,1)S(1)}, bf16[160,768]{1,0:T(8,128)(2,1)S(1)}, u32[]{:S(2)}, u32[]{:S(2)}) %collective-permute-start.30) | collective-permute-done | bytes 245792 | tf_op jit(solution)/shard_map/ppermute | solution.py:96
  70.7 5.0 %shard_map.242 = (bf16[160,1536]{1,0:T(8,128)(2,1)S(1)}, f32[160,1536]{1,0:T(8,128)S(1)}, bf16[320,768]{1,0:T(8,128)(2,1)S(1)}, bf16[320,768]{1,0:T(8,128)(2,1)S...) custom-call(s32[1]{0:T(128)} %bitcast.place_ref, ...), custom_call_target="tpu_custom_call" | custom-call | flops 1 | bytes 1 | tf_op jit(solution)/shard_map/pallas_call | solution.py:68
  82.8 8.2 %collective-permute-done.33.refs_1_ = bf16[160,1536]{1,0:T(8,128)(2,1)S(1)} collective-permute-done((bf16[160,1536]{1,0:T(8,128)(2,1)S(1)}, bf16[160,1536]{1,0:T(8,128)(2,1)S(1)}, u32[]{:S(2)}, u32[]{:S(2)}) %collective-permute-start.33) | collective-permute-done | bytes 491552 | tf_op jit(solution)/shard_map/ppermute | solution.py:96
  92.5 3.1 %collective-permute-start.38 = (bf16[40,1536]{1,0:T(8,128)(2,1)S(1)}, bf16[40,1536]{1,0:T(8,128)(2,1)S(1)}, u32[]{:S(2)}, u32[]{:S(2)}) collective-permute-start(bf16[40,1536]{1,0:T(8,128)(2,1)S(1)} %get-tuple-element.161), channel_id=1, source_target_pairs={{0,24},{2,26},{4,28},{6,30},{8,16},{10,18},{12,20},{14,22},{16,8},... | collective-permute-start | bytes 368648 | tf_op jit(solution)/shard_map/ppermute | solution.py:96
  98.8 4.7 %collective-permute-done.37.refs_3_ = bf16[40,1536]{1,0:T(8,128)(2,1)S(1)} collective-permute-done((bf16[40,1536]{1,0:T(8,128)(2,1)S(1)}, bf16[40,1536]{1,0:T(8,128)(2,1)S(1)}, u32[]{:S(2)}, u32[]{:S(2)}) %collective-permute-start.37) | collective-permute-done | bytes 122912 | tf_op jit(solution)/shard_map/ppermute | solution.py:96
  105.6 5.7 %collective-permute-done.39.refs_3_ = bf16[160,768]{1,0:T(8,128)(2,1)S(1)} collective-permute-done((bf16[160,768]{1,0:T(8,128)(2,1)S(1)}, bf16[160,768]{1,0:T(8,128)(2,1)S(1)}, u32[]{:S(2)}, u32[]{:S(2)}) %collective-permute-start.39) | collective-permute-done | bytes 245792 | tf_op jit(solution)/shard_map/ppermute | solution.py:96
  111.3 5.6 %shard_map.249 = (bf16[256,768]{1,0:T(8,128)(2,1)S(1)}, f32[128,768]{1,0:T(8,128)S(1)}, bf16[672,768]{1,0:T(8,128)(2,1)S(1)}, f32[8,768]{1,0:T(8,128)S(1)}, f32[...) custom-call(s32[1]{0:T(128)} %bitcast.place_ref, ...), custom_call_target="tpu_custom_call" | custom-call | flops 1 | bytes 1 | tf_op jit(solution)/shard_map/pallas_call | solution.py:68
  117.5 3.3 %collective-permute-done.40.refs_1_ = f32[8,768]{1,0:T(8,128)S(1)} collective-permute-done((f32[8,768]{1,0:T(8,128)S(1)}, f32[8,768]{1,0:T(8,128)S(1)}, u32[]{:S(2)}, u32[]{:S(2)}) %collective-permute-start.40) | collective-permute-done | bytes 24608 | tf_op jit(solution)/shard_map/ppermute | solution.py:96
  126.0 2.4 %collective-permute-start.46 = (bf16[144,256]{1,0:T(8,128)(2,1)S(1)}, bf16[144,256]{1,0:T(8,128)(2,1)S(1)}, u32[]{:S(2)}, u32[]{:S(2)}) collective-permute-start(bf16[144,256]{1,0:T(8,128)(2,1)S(1)} %get-tuple-element.188), channel_id=1, source_target_pairs={{0,24},{2,26},{4,28},{6,30},{8,16},{10,18},{12,20},{14,22},{16,8},... | collective-permute-start | bytes 221192 | tf_op jit(solution)/shard_map/ppermute | solution.py:96
  128.6 5.8 %collective-permute-done.45.refs_5_ = bf16[144,256]{1,0:T(8,128)(2,1)S(1)} collective-permute-done((bf16[144,256]{1,0:T(8,128)(2,1)S(1)}, bf16[144,256]{1,0:T(8,128)(2,1)S(1)}, u32[]{:S(2)}, u32[]{:S(2)}) %collective-permute-start.45) | collective-permute-done | bytes 73760 | tf_op jit(solution)/shard_map/ppermute | solution.py:96
  138.3 2.4 %collective-permute-start.51 = (bf16[48,1280]{1,0:T(8,128)(2,1)S(1)}, bf16[48,1280]{1,0:T(8,128)(2,1)S(1)}, u32[]{:S(2)}, u32[]{:S(2)}) collective-permute-start(bf16[48,1280]{1,0:T(8,128)(2,1)S(1)} %get-tuple-element.201), channel_id=1, source_target_pairs={{0,24},{2,26},{4,28},{6,30},{8,16},{10,18},{12,20},{14,22},{16,8},... | collective-permute-start | bytes 368648 | tf_op jit(solution)/shard_map/ppermute | solution.py:96
  141.9 3.0 %collective-permute-done.47.refs_4_.refs_3_ = bf16[672,768]{1,0:T(8,128)(2,1)S(1)} collective-permute-done((bf16[672,768]{1,0:T(8,128)(2,1)S(1)}, bf16[672,768]{1,0:T(8,128)(2,1)S(1)}, u32[]{:S(2)}, u32[]{:S(2)}) %collective-permute-start.47) | collective-permute-done | bytes 1032224 | tf_op jit(solution)/shard_map/ppermute | solution.py:96
  147.3 2.3 %collective-permute-done.50.refs_5_ = bf16[48,1280]{1,0:T(8,128)(2,1)S(1)} collective-permute-done((bf16[48,1280]{1,0:T(8,128)(2,1)S(1)}, bf16[48,1280]{1,0:T(8,128)(2,1)S(1)}, u32[]{:S(2)}, u32[]{:S(2)}) %collective-permute-start.50) | collective-permute-done | bytes 122912 | tf_op jit(solution)/shard_map/ppermute | solution.py:96
  (111 shorter events, 55.1 us)
Async XLA Ops:
  3.6 21.6 %collective-permute-start = (bf16[512,768]{1,0:T(8,128)(2,1)}, bf16[512,768]{1,0:T(8,128)(2,1)S(1)}, u32[]{:S(2)}, u32[]{:S(2)}) collective-permute-start(bf16[512,768]{1,0:T(8,128)(2,1)} %get-tuple-element.113.refs_1_.refs_14_), channel_id=1, source_target_pairs={{0,1},{1,0},{2,3},{3,2},{4,5},{5,4},{6,7},{7,6},{8,9},{9,8},{10,11... | collective-permute-start | bytes 2359304 | tf_op jit(solution)/shard_map/ppermute | solution.py:96
  6.6 9.1 %collective-permute-start.3 = (bf16[48,1664]{1,0:T(8,128)(2,1)}, bf16[48,1664]{1,0:T(8,128)(2,1)S(1)}, u32[]{:S(2)}, u32[]{:S(2)}) collective-permute-start(bf16[48,1664]{1,0:T(8,128)(2,1)} %get-tuple-element.128.refs_9_), channel_id=1, source_target_pairs={{0,24},{2,26},{4,28},{6,30},{8,16},{10,18},{12,20},{14,22},{16,8},... | collective-permute-start | bytes 479240 | tf_op jit(solution)/shard_map/ppermute | solution.py:96
  10.2 13.5 %collective-permute-start.2 = (bf16[48,1664]{1,0:T(8,128)(2,1)}, bf16[48,1664]{1,0:T(8,128)(2,1)S(1)}, u32[]{:S(2)}, u32[]{:S(2)}) collective-permute-start(bf16[48,1664]{1,0:T(8,128)(2,1)} %get-tuple-element.128.refs_9_), channel_id=1, source_target_pairs={{0,16},{2,18},{4,20},{6,22},{8,24},{10,26},{12,28},{14,30},{16,0},... | collective-permute-start | bytes 479240 | tf_op jit(solution)/shard_map/ppermute | solution.py:96
  10.2 15.9 %collective-permute-start.1 = (bf16[48,1664]{1,0:T(8,128)(2,1)}, bf16[48,1664]{1,0:T(8,128)(2,1)S(1)}, u32[]{:S(2)}, u32[]{:S(2)}) collective-permute-start(bf16[48,1664]{1,0:T(8,128)(2,1)} %get-tuple-element.128.refs_9_), channel_id=1, source_target_pairs={{0,8},{2,10},{4,12},{6,14},{8,0},{10,2},{12,4},{14,6},{16,24},{18,... | collective-permute-start | bytes 479240 | tf_op jit(solution)/shard_map/ppermute | solution.py:96
  11.0 19.4 %collective-permute-start.7 = (bf16[48,1664]{1,0:T(8,128)(2,1)}, bf16[48,1664]{1,0:T(8,128)(2,1)S(1)}, u32[]{:S(2)}, u32[]{:S(2)}) collective-permute-start(bf16[48,1664]{1,0:T(8,128)(2,1)} %get-tuple-element.128.refs_9_), channel_id=1, source_target_pairs={{0,4},{2,6},{4,0},{6,2},{8,12},{10,14},{12,8},{14,10},{16,20},{18,... | collective-permute-start | bytes 479240 | tf_op jit(solution)/shard_map/ppermute | solution.py:96
  15.7 16.3 %collective-permute-start.10 = (bf16[48,1664]{1,0:T(8,128)(2,1)S(1)}, bf16[48,1664]{1,0:T(8,128)(2,1)S(1)}, u32[]{:S(2)}, u32[]{:S(2)}) collective-permute-start(bf16[48,1664]{1,0:T(8,128)(2,1)S(1)} %collective-permute-done.3.refs_12_), channel_id=1, source_target_pairs={{0,4},{2,6},{4,0},{6,2},{8,12},{10,14},{12,8},{14,10},{16,20},{18,... | collective-permute-start | bytes 479240 | tf_op jit(solution)/shard_map/ppermute | solution.py:96
  23.7 10.9 %collective-permute-start.9 = (bf16[48,1664]{1,0:T(8,128)(2,1)S(1)}, bf16[48,1664]{1,0:T(8,128)(2,1)S(1)}, u32[]{:S(2)}, u32[]{:S(2)}) collective-permute-start(bf16[48,1664]{1,0:T(8,128)(2,1)S(1)} %collective-permute-done.2.refs_11_), channel_id=1, source_target_pairs={{0,4},{2,6},{4,0},{6,2},{8,12},{10,14},{12,8},{14,10},{16,20},{18,... | collective-permute-start | bytes 479240 | tf_op jit(solution)/shard_map/ppermute | solution.py:96
  25.2 29.4 %collective-permute-start.31 = (bf16[512,768]{1,0:T(8,128)(2,1)}, bf16[512,768]{1,0:T(8,128)(2,1)S(1)}, u32[]{:S(2)}, u32[]{:S(2)}) collective-permute-start(bf16[512,768]{1,0:T(8,128)(2,1)} %get-tuple-element.146.refs_15_), channel_id=1, source_target_pairs={{0,1},{1,0},{2,3},{3,2},{4,5},{5,4},{6,7},{7,6},{8,9},{9,8},{10,11... | collective-permute-start | bytes 2359304 | tf_op jit(solution)/shard_map/ppermute | solution.py:96
  26.1 8.7 %collective-permute-start.8 = (bf16[48,1664]{1,0:T(8,128)(2,1)S(1)}, bf16[48,1664]{1,0:T(8,128)(2,1)S(1)}, u32[]{:S(2)}, u32[]{:S(2)}) collective-permute-start(bf16[48,1664]{1,0:T(8,128)(2,1)S(1)} %collective-permute-done.1.refs_10_), channel_id=1, source_target_pairs={{0,4},{2,6},{4,0},{6,2},{8,12},{10,14},{12,8},{14,10},{16,20},{18,... | collective-permute-start | bytes 479240 | tf_op jit(solution)/shard_map/ppermute | solution.py:96
  54.6 16.0 %collective-permute-start.32 = (bf16[512,768]{1,0:T(8,128)(2,1)S(1)}, bf16[512,768]{1,0:T(8,128)(2,1)S(1)}, u32[]{:S(2)}, u32[]{:S(2)}) collective-permute-start(bf16[512,768]{1,0:T(8,128)(2,1)S(1)} %collective-permute-done.31.refs_17_), channel_id=1, source_target_pairs={{0,2},{2,0},{4,6},{6,4},{8,10},{10,8},{12,14},{14,12},{16,18},{18,... | collective-permute-start | bytes 2359304 | tf_op jit(solution)/shard_map/ppermute | solution.py:96
  54.6 8.4 %collective-permute-start.30 = (bf16[160,768]{1,0:T(8,128)(2,1)S(1)}, bf16[160,768]{1,0:T(8,128)(2,1)S(1)}, u32[]{:S(2)}, u32[]{:S(2)}) collective-permute-start(bf16[160,768]{1,0:T(8,128)(2,1)S(1)} %pad_maximum_fusion), channel_id=1, source_target_pairs={{0,4},{2,6},{4,0},{6,2},{8,12},{10,14},{12,8},{14,10},{16,20},{18,... | collective-permute-start | bytes 737288 | tf_op jit(solution)/shard_map/ppermute | solution.py:96
  55.5 9.6 %collective-permute-start.24 = (bf16[40,768]{1,0:T(8,128)(2,1)S(1)}, bf16[40,768]{1,0:T(8,128)(2,1)S(1)}, u32[]{:S(2)}, u32[]{:S(2)}) collective-permute-start(bf16[40,768]{1,0:T(8,128)(2,1)S(1)} %get-tuple-element.143), channel_id=1, source_target_pairs={{0,16},{2,18},{4,20},{6,22},{8,24},{10,26},{12,28},{14,30},{16,0},... | collective-permute-start | bytes 184328 | tf_op jit(solution)/shard_map/ppermute | solution.py:96
  56.8 8.8 %collective-permute-start.25 = (bf16[40,768]{1,0:T(8,128)(2,1)S(1)}, bf16[40,768]{1,0:T(8,128)(2,1)S(1)}, u32[]{:S(2)}, u32[]{:S(2)}) collective-permute-start(bf16[40,768]{1,0:T(8,128)(2,1)S(1)} %get-tuple-element.144), channel_id=1, source_target_pairs={{0,24},{2,26},{4,28},{6,30},{8,16},{10,18},{12,20},{14,22},{16,8},... | collective-permute-start | bytes 184328 | tf_op jit(solution)/shard_map/ppermute | solution.py:96
  77.4 13.6 %collective-permute-start.33 = (bf16[160,1536]{1,0:T(8,128)(2,1)S(1)}, bf16[160,1536]{1,0:T(8,128)(2,1)S(1)}, u32[]{:S(2)}, u32[]{:S(2)}) collective-permute-start(bf16[160,1536]{1,0:T(8,128)(2,1)S(1)} %get-tuple-element.149), channel_id=1, source_target_pairs={{0,4},{2,6},{4,0},{6,2},{8,12},{10,14},{12,8},{14,10},{16,20},{18,... | collective-permute-start | bytes 1474568 | tf_op jit(solution)/shard_map/ppermute | solution.py:96
  82.2 15.4 %collective-permute-start.35 = (bf16[768,384]{1,0:T(8,128)(2,1)S(1)}, bf16[768,384]{1,0:T(8,128)(2,1)S(1)}, u32[]{:S(2)}, u32[]{:S(2)}) collective-permute-start(bf16[768,384]{1,0:T(8,128)(2,1)S(1)} %get-tuple-element.157), channel_id=1, source_target_pairs={{0,1},{1,0},{2,3},{3,2},{4,5},{5,4},{6,7},{7,6},{8,9},{9,8},{10,11... | collective-permute-start | bytes 1769480 | tf_op jit(solution)/shard_map/ppermute | solution.py:96
  91.2 12.3 %collective-permute-start.37 = (bf16[40,1536]{1,0:T(8,128)(2,1)S(1)}, bf16[40,1536]{1,0:T(8,128)(2,1)S(1)}, u32[]{:S(2)}, u32[]{:S(2)}) collective-permute-start(bf16[40,1536]{1,0:T(8,128)(2,1)S(1)} %get-tuple-element.160), channel_id=1, source_target_pairs={{0,16},{2,18},{4,20},{6,22},{8,24},{10,26},{12,28},{14,30},{16,0},... | collective-permute-start | bytes 368648 | tf_op jit(solution)/shard_map/ppermute | solution.py:96
  92.5 10.9 %collective-permute-start.38 = (bf16[40,1536]{1,0:T(8,128)(2,1)S(1)}, bf16[40,1536]{1,0:T(8,128)(2,1)S(1)}, u32[]{:S(2)}, u32[]{:S(2)}) collective-permute-start(bf16[40,1536]{1,0:T(8,128)(2,1)S(1)} %get-tuple-element.161), channel_id=1, source_target_pairs={{0,24},{2,26},{4,28},{6,30},{8,16},{10,18},{12,20},{14,22},{16,8},... | collective-permute-start | bytes 368648 | tf_op jit(solution)/shard_map/ppermute | solution.py:96
  120.9 24.0 %collective-permute-start.47 = (bf16[672,768]{1,0:T(8,128)(2,1)S(1)}, bf16[672,768]{1,0:T(8,128)(2,1)S(1)}, u32[]{:S(2)}, u32[]{:S(2)}) collective-permute-start(bf16[672,768]{1,0:T(8,128)(2,1)S(1)} %get-tuple-element.191), channel_id=1, source_target_pairs={{0,1},{1,0},{2,3},{3,2},{4,5},{5,4},{6,7},{7,6},{8,9},{9,8},{10,11... | collective-permute-start | bytes 3096584 | tf_op jit(solution)/shard_map/ppermute | solution.py:96
  122.8 13.4 %collective-permute-start.43 = (bf16[4,48,1280]{2,1,0:T(8,128)(2,1)S(1)}, bf16[4,48,1280]{2,1,0:T(8,128)(2,1)S(1)}, u32[]{:S(2)}, u32[]{:S(2)}) collective-permute-start(bf16[4,48,1280]{2,1,0:T(8,128)(2,1)S(1)} %get-tuple-element.184), channel_id=1, source_target_pairs={{0,4},{2,6},{4,0},{6,2},{8,12},{10,14},{12,8},{14,10},{16,20},{18,... | collective-permute-start | bytes 1474568 | tf_op jit(solution)/shard_map/ppermute | solution.py:96
  126.0 8.4 %collective-permute-start.45 = (bf16[144,256]{1,0:T(8,128)(2,1)S(1)}, bf16[144,256]{1,0:T(8,128)(2,1)S(1)}, u32[]{:S(2)}, u32[]{:S(2)}) collective-permute-start(bf16[144,256]{1,0:T(8,128)(2,1)S(1)} %get-tuple-element.187), channel_id=1, source_target_pairs={{0,16},{2,18},{4,20},{6,22},{8,24},{10,26},{12,28},{14,30},{16,0},... | collective-permute-start | bytes 221192 | tf_op jit(solution)/shard_map/ppermute | solution.py:96
  126.0 8.4 %collective-permute-start.46 = (bf16[144,256]{1,0:T(8,128)(2,1)S(1)}, bf16[144,256]{1,0:T(8,128)(2,1)S(1)}, u32[]{:S(2)}, u32[]{:S(2)}) collective-permute-start(bf16[144,256]{1,0:T(8,128)(2,1)S(1)} %get-tuple-element.188), channel_id=1, source_target_pairs={{0,24},{2,26},{4,28},{6,30},{8,16},{10,18},{12,20},{14,22},{16,8},... | collective-permute-start | bytes 221192 | tf_op jit(solution)/shard_map/ppermute | solution.py:96
  136.3 11.1 %collective-permute-start.49 = (bf16[48,1280]{1,0:T(8,128)(2,1)S(1)}, bf16[48,1280]{1,0:T(8,128)(2,1)S(1)}, u32[]{:S(2)}, u32[]{:S(2)}) collective-permute-start(bf16[48,1280]{1,0:T(8,128)(2,1)S(1)} %get-tuple-element.199), channel_id=1, source_target_pairs={{0,8},{2,10},{4,12},{6,14},{8,0},{10,2},{12,4},{14,6},{16,24},{18,... | collective-permute-start | bytes 368648 | tf_op jit(solution)/shard_map/ppermute | solution.py:96
  138.3 11.3 %collective-permute-start.50 = (bf16[48,1280]{1,0:T(8,128)(2,1)S(1)}, bf16[48,1280]{1,0:T(8,128)(2,1)S(1)}, u32[]{:S(2)}, u32[]{:S(2)}) collective-permute-start(bf16[48,1280]{1,0:T(8,128)(2,1)S(1)} %get-tuple-element.200), channel_id=1, source_target_pairs={{0,16},{2,18},{4,20},{6,22},{8,24},{10,26},{12,28},{14,30},{16,0},... | collective-permute-start | bytes 368648 | tf_op jit(solution)/shard_map/ppermute | solution.py:96
  138.3 11.3 %collective-permute-start.51 = (bf16[48,1280]{1,0:T(8,128)(2,1)S(1)}, bf16[48,1280]{1,0:T(8,128)(2,1)S(1)}, u32[]{:S(2)}, u32[]{:S(2)}) collective-permute-start(bf16[48,1280]{1,0:T(8,128)(2,1)S(1)} %get-tuple-element.201), channel_id=1, source_target_pairs={{0,24},{2,26},{4,28},{6,30},{8,16},{10,18},{12,20},{14,22},{16,8},... | collective-permute-start | bytes 368648 | tf_op jit(solution)/shard_map/ppermute | solution.py:96
  (34 other events, 155.8 us)

commit v5 on v4

--- a/solution.py
+++ b/solution.py
@@ -483,18 +483,21 @@
         total_ref[...] = total
         forward = jnp.zeros((expert_in, width), F32)
         backward = jnp.zeros((expert_in, width), F32)
-        for part in range(parts):
-            at = part * hidden_local
-            head, rest = weights[2 * part : 2 * part + 2]
+        pair_width = 2 * hidden_local
+        for pair in range(parts // 2):
+            at = pair * pair_width
             up, down = [
                 jnp.concatenate(
                     [
-                        head[2 * row_count :, number * hidden_local : (number + 1) * hidden_local],
-                        rest[:, number * hidden_local : (number + 1) * hidden_local],
+                        jnp.concatenate([head[2 * row_count :, columns], rest[:, columns]], axis=0)
+                        for head, rest in (
+                            weights[4 * pair : 4 * pair + 2],
+                            weights[4 * pair + 2 : 4 * pair + 4],
+                        )
                     ],
-                    axis=0,
+                    axis=1,
                 )
-                for number in range(2)
+                for columns in (slice(0, hidden_local), slice(hidden_local, pair_width))
             ]
             pre = matmul(rows, up)
             square = pre * pre
@@ -504,9 +507,9 @@
             slope = 0.5 * (1.0 + tanh) + 0.5 * pre * (1.0 - tanh * tanh) * (
                 0.7978845608028654 * (1.0 + 3.0 * 0.044715 * square)
             )
-            hidden_ref[:, at : at + hidden_local] = hidden
+            hidden_ref[:, at : at + pair_width] = hidden
             grad_pre = (matmul(total, down) * slope).astype(BF16)
-            pre_ref[:, at : at + hidden_local] = grad_pre
+            pre_ref[:, at : at + pair_width] = grad_pre
             forward += matmul_nt(hidden, down)
             backward += matmul_nt(grad_pre, up)
         keep_ref[:, :width] = forward[:slot_rows]
@@ -531,10 +534,13 @@
 
     def expert_grads(first):
         def grads(idx, rows_ref, total_ref, hidden_ref, pre_ref, *outs):
+            at = first * hidden_local
+            both = slice(at, at + 2 * hidden_local)
+            up_grads = matmul_tn(rows_ref[...], pre_ref[:, both])
+            down_grads = matmul_tn(total_ref[...], hidden_ref[:, both])
             for part in range(2):
-                at = (first + part) * hidden_local
-                up_grad = matmul_tn(rows_ref[...], pre_ref[:, at : at + hidden_local])
-                down_grad = matmul_tn(total_ref[...], hidden_ref[:, at : at + hidden_local])
+                columns = slice(part * hidden_local, (part + 1) * hidden_local)
+                up_grad, down_grad = up_grads[:, columns], down_grads[:, columns]
                 ref, place = (outs[0], 2 * part) if len(outs) == 1 else (outs[part], 0)
                 ref[place] = up_grad.astype(ref.dtype)
                 ref[place + 1] = down_grad.astype(ref.dtype)

time: 151 us -> 150 us (level)
  no operation moved by 1% of the time
where the time goes in v5:
time: 150 us
  waiting for transfers between devices  69.9 us (47%)
  starting transfers between devices  50.9 us (34%)
  Pallas kernels  26.6 us (18%)
  local copies, waits for them, and re-layouts  1.9 us (1%)
    ppermute x52, waiting for transfers between devices, swap(): return lax.ppermute(values, axis, [(i, i ^ mask) for i in range(count)])  69.9 us
    ppermute x52, starting transfers between devices, swap(): return lax.ppermute(values, axis, [(i, i ^ mask) for i in range(count)])  50.9 us
    pallas_call x18, Pallas kernels, run(): pl.pallas_call(wrapped, out_shape=list(outs), in_specs=[pl.BlockSpec(memo...  26.6 us
  transfers between devices with their start and end apart: 52, of which 27 were waited for; matrix products, arithmetic and copies ran while one was open for 0% of the time, Pallas kernels for 7%

profile of v5, /device:TPU:0, one launch (start us, length us, event | category | flops | bytes accessed | tf_op | source)
XLA Modules:
  0.0 150.2 jit_solution(18312019983896126572)
XLA Ops:
  0.7 2.9 %shard_map.238 = (bf16[48,1664]{1,0:T(8,128)(2,1)}, bf16[512,768]{1,0:T(8,128)(2,1)}, bf16[512,768]{1,0:T(8,128)(2,1)}, f32[16,512]{1,0:T(8,128)}) custom-call(s32[1]{0:T(128)} %bitcast.place_ref, bf16[48,384]{1,0:T(8,128)(2,1)} %refs_0_.1, bf16[48,384]{1,0:T(8,128)(2,1)} %refs_1_.1, bf16[48,384]{1,0:T(8,128)(2,1)} %refs_2_.1, bf16[48,384]{1,0:T(8,128)(2,1)} %refs_3_.1, ...), custom_call_target="tpu_custom_call" | custom-call | flops 1 | bytes 1 | tf_op jit(solution)/shard_map/pallas_call | solution.py:68
  3.6 3.0 %collective-permute-start = (bf16[512,768]{1,0:T(8,128)(2,1)}, bf16[512,768]{1,0:T(8,128)(2,1)S(1)}, u32[]{:S(2)}, u32[]{:S(2)}) collective-permute-start(bf16[512,768]{1,0:T(8,128)(2,1)} %get-tuple-element.113.refs_1_.refs_14_), channel_id=1, source_target_pairs={{0,1},{1,0},{2,3},{3,2},{4,5},{5,4},{6,7},{7,6},{8,9},{9,8},{10,11... | collective-permute-start | bytes 2359304 | tf_op jit(solution)/shard_map/ppermute | solution.py:96
  6.6 3.6 %collective-permute-start.3 = (bf16[48,1664]{1,0:T(8,128)(2,1)}, bf16[48,1664]{1,0:T(8,128)(2,1)S(1)}, u32[]{:S(2)}, u32[]{:S(2)}) collective-permute-start(bf16[48,1664]{1,0:T(8,128)(2,1)} %get-tuple-element.128.refs_9_), channel_id=1, source_target_pairs={{0,24},{2,26},{4,28},{6,30},{8,16},{10,18},{12,20},{14,22},{16,8},... | collective-permute-start | bytes 479240 | tf_op jit(solution)/shard_map/ppermute | solution.py:96
  12.5 3.2 %collective-permute-done.3.refs_12_ = bf16[48,1664]{1,0:T(8,128)(2,1)S(1)} collective-permute-done((bf16[48,1664]{1,0:T(8,128)(2,1)}, bf16[48,1664]{1,0:T(8,128)(2,1)S(1)}, u32[]{:S(2)}, u32[]{:S(2)}) %collective-permute-start.3) | collective-permute-done | bytes 159776 | tf_op jit(solution)/shard_map/ppermute | solution.py:96
  17.2 6.5 %collective-permute-done.2.refs_11_ = bf16[48,1664]{1,0:T(8,128)(2,1)S(1)} collective-permute-done((bf16[48,1664]{1,0:T(8,128)(2,1)}, bf16[48,1664]{1,0:T(8,128)(2,1)S(1)}, u32[]{:S(2)}, u32[]{:S(2)}) %collective-permute-start.2) | collective-permute-done | bytes 159776 | tf_op jit(solution)/shard_map/ppermute | solution.py:96
  32.0 2.6 %collective-permute-start.5 = (bf16[40,768]{1,0:T(8,128)(2,1)S(1)}, bf16[40,768]{1,0:T(8,128)(2,1)S(1)}, u32[]{:S(2)}, u32[]{:S(2)}) collective-permute-start(bf16[40,768]{1,0:T(8,128)(2,1)S(1)} %get-tuple-element.122), channel_id=1, source_target_pairs={{0,16},{2,18},{4,20},{6,22},{8,24},{10,26},{12,28},{14,30},{16,0},... | collective-permute-start | bytes 184328 | tf_op jit(solution)/shard_map/ppermute | solution.py:96
  35.4 3.1 %collective-permute-done.5.refs_1_.refs_11_ = bf16[40,768]{1,0:T(8,128)(2,1)S(1)} collective-permute-done((bf16[40,768]{1,0:T(8,128)(2,1)S(1)}, bf16[40,768]{1,0:T(8,128)(2,1)S(1)}, u32[]{:S(2)}, u32[]{:S(2)}) %collective-permute-start.5) | collective-permute-done | bytes 61472 | tf_op jit(solution)/shard_map/ppermute | solution.py:96
  43.4 3.1 %shard_map.240 = (bf16[160,768]{1,0:T(8,128)(2,1)S(1)}, f32[160,768]{1,0:T(8,128)S(1)}, bf16[256,768]{1,0:T(8,128)(2,1)S(1)}, bf16[256,1152]{1,0:T(8,128)(2,1)S(...) custom-call(s32[1]{0:T(128)} %bitcast.place_ref, ...), custom_call_target="tpu_custom_call" | custom-call | flops 1 | bytes 1 | tf_op jit(solution)/shard_map/pallas_call | solution.py:68
  47.7 6.9 %collective-permute-done.22.refs_4_ = bf16[160,768]{1,0:T(8,128)(2,1)S(1)} collective-permute-done((bf16[160,768]{1,0:T(8,128)(2,1)S(1)}, bf16[160,768]{1,0:T(8,128)(2,1)S(1)}, u32[]{:S(2)}, u32[]{:S(2)}) %collective-permute-start.22) | collective-permute-done | bytes 245792 | tf_op jit(solution)/shard_map/ppermute | solution.py:96
  56.8 3.1 %collective-permute-start.25 = (bf16[40,768]{1,0:T(8,128)(2,1)S(1)}, bf16[40,768]{1,0:T(8,128)(2,1)S(1)}, u32[]{:S(2)}, u32[]{:S(2)}) collective-permute-start(bf16[40,768]{1,0:T(8,128)(2,1)S(1)} %get-tuple-element.144), channel_id=1, source_target_pairs={{0,24},{2,26},{4,28},{6,30},{8,16},{10,18},{12,20},{14,22},{16,8},... | collective-permute-start | bytes 184328 | tf_op jit(solution)/shard_map/ppermute | solution.py:96
  59.9 3.2 %collective-permute-done.30.refs_13_ = bf16[160,768]{1,0:T(8,128)(2,1)S(1)} collective-permute-done((bf16[160,768]{1,0:T(8,128)(2,1)S(1)}, bf16[160,768]{1,0:T(8,128)(2,1)S(1)}, u32[]{:S(2)}, u32[]{:S(2)}) %collective-permute-start.30) | collective-permute-done | bytes 245792 | tf_op jit(solution)/shard_map/ppermute | solution.py:96
  70.7 4.0 %shard_map.242 = (bf16[160,1536]{1,0:T(8,128)(2,1)S(1)}, f32[160,1536]{1,0:T(8,128)S(1)}, bf16[320,768]{1,0:T(8,128)(2,1)S(1)}, bf16[320,768]{1,0:T(8,128)(2,1)S...) custom-call(s32[1]{0:T(128)} %bitcast.place_ref, ...), custom_call_target="tpu_custom_call" | custom-call | flops 1 | bytes 1 | tf_op jit(solution)/shard_map/pallas_call | solution.py:68
  81.6 8.2 %collective-permute-done.33.refs_1_ = bf16[160,1536]{1,0:T(8,128)(2,1)S(1)} collective-permute-done((bf16[160,1536]{1,0:T(8,128)(2,1)S(1)}, bf16[160,1536]{1,0:T(8,128)(2,1)S(1)}, u32[]{:S(2)}, u32[]{:S(2)}) %collective-permute-start.33) | collective-permute-done | bytes 491552 | tf_op jit(solution)/shard_map/ppermute | solution.py:96
  91.3 3.1 %collective-permute-start.38 = (bf16[40,1536]{1,0:T(8,128)(2,1)S(1)}, bf16[40,1536]{1,0:T(8,128)(2,1)S(1)}, u32[]{:S(2)}, u32[]{:S(2)}) collective-permute-start(bf16[40,1536]{1,0:T(8,128)(2,1)S(1)} %get-tuple-element.161), channel_id=1, source_target_pairs={{0,24},{2,26},{4,28},{6,30},{8,16},{10,18},{12,20},{14,22},{16,8},... | collective-permute-start | bytes 368648 | tf_op jit(solution)/shard_map/ppermute | solution.py:96
  97.6 4.8 %collective-permute-done.37.refs_3_ = bf16[40,1536]{1,0:T(8,128)(2,1)S(1)} collective-permute-done((bf16[40,1536]{1,0:T(8,128)(2,1)S(1)}, bf16[40,1536]{1,0:T(8,128)(2,1)S(1)}, u32[]{:S(2)}, u32[]{:S(2)}) %collective-permute-start.37) | collective-permute-done | bytes 122912 | tf_op jit(solution)/shard_map/ppermute | solution.py:96
  104.5 5.7 %collective-permute-done.39.refs_3_ = bf16[160,768]{1,0:T(8,128)(2,1)S(1)} collective-permute-done((bf16[160,768]{1,0:T(8,128)(2,1)S(1)}, bf16[160,768]{1,0:T(8,128)(2,1)S(1)}, u32[]{:S(2)}, u32[]{:S(2)}) %collective-permute-start.39) | collective-permute-done | bytes 245792 | tf_op jit(solution)/shard_map/ppermute | solution.py:96
  110.2 5.6 %shard_map.249 = (bf16[256,768]{1,0:T(8,128)(2,1)S(1)}, f32[128,768]{1,0:T(8,128)S(1)}, bf16[672,768]{1,0:T(8,128)(2,1)S(1)}, f32[8,768]{1,0:T(8,128)S(1)}, f32[...) custom-call(s32[1]{0:T(128)} %bitcast.place_ref, ...), custom_call_target="tpu_custom_call" | custom-call | flops 1 | bytes 1 | tf_op jit(solution)/shard_map/pallas_call | solution.py:68
  116.5 3.3 %collective-permute-done.40.refs_1_ = f32[8,768]{1,0:T(8,128)S(1)} collective-permute-done((f32[8,768]{1,0:T(8,128)S(1)}, f32[8,768]{1,0:T(8,128)S(1)}, u32[]{:S(2)}, u32[]{:S(2)}) %collective-permute-start.40) | collective-permute-done | bytes 24608 | tf_op jit(solution)/shard_map/ppermute | solution.py:96
  122.9 2.6 %collective-permute-start.44 = (bf16[144,256]{1,0:T(8,128)(2,1)S(1)}, bf16[144,256]{1,0:T(8,128)(2,1)S(1)}, u32[]{:S(2)}, u32[]{:S(2)}) collective-permute-start(bf16[144,256]{1,0:T(8,128)(2,1)S(1)} %get-tuple-element.186), channel_id=1, source_target_pairs={{0,8},{2,10},{4,12},{6,14},{8,0},{10,2},{12,4},{14,6},{16,24},{18,... | collective-permute-start | bytes 221192 | tf_op jit(solution)/shard_map/ppermute | solution.py:96
  128.1 5.4 %collective-permute-done.45.refs_5_ = bf16[144,256]{1,0:T(8,128)(2,1)S(1)} collective-permute-done((bf16[144,256]{1,0:T(8,128)(2,1)S(1)}, bf16[144,256]{1,0:T(8,128)(2,1)S(1)}, u32[]{:S(2)}, u32[]{:S(2)}) %collective-permute-start.45) | collective-permute-done | bytes 73760 | tf_op jit(solution)/shard_map/ppermute | solution.py:96
  135.2 2.6 %collective-permute-start.49 = (bf16[48,1280]{1,0:T(8,128)(2,1)S(1)}, bf16[48,1280]{1,0:T(8,128)(2,1)S(1)}, u32[]{:S(2)}, u32[]{:S(2)}) collective-permute-start(bf16[48,1280]{1,0:T(8,128)(2,1)S(1)} %get-tuple-element.199), channel_id=1, source_target_pairs={{0,8},{2,10},{4,12},{6,14},{8,0},{10,2},{12,4},{14,6},{16,24},{18,... | collective-permute-start | bytes 368648 | tf_op jit(solution)/shard_map/ppermute | solution.py:96
  137.8 2.4 %collective-permute-start.51 = (bf16[48,1280]{1,0:T(8,128)(2,1)S(1)}, bf16[48,1280]{1,0:T(8,128)(2,1)S(1)}, u32[]{:S(2)}, u32[]{:S(2)}) collective-permute-start(bf16[48,1280]{1,0:T(8,128)(2,1)S(1)} %get-tuple-element.201), channel_id=1, source_target_pairs={{0,24},{2,26},{4,28},{6,30},{8,16},{10,18},{12,20},{14,22},{16,8},... | collective-permute-start | bytes 368648 | tf_op jit(solution)/shard_map/ppermute | solution.py:96
  141.3 2.5 %collective-permute-done.47.refs_4_.refs_3_ = bf16[672,768]{1,0:T(8,128)(2,1)S(1)} collective-permute-done((bf16[672,768]{1,0:T(8,128)(2,1)S(1)}, bf16[672,768]{1,0:T(8,128)(2,1)S(1)}, u32[]{:S(2)}, u32[]{:S(2)}) %collective-permute-start.47) | collective-permute-done | bytes 1032224 | tf_op jit(solution)/shard_map/ppermute | solution.py:96
  146.2 2.9 %collective-permute-done.50.refs_5_ = bf16[48,1280]{1,0:T(8,128)(2,1)S(1)} collective-permute-done((bf16[48,1280]{1,0:T(8,128)(2,1)S(1)}, bf16[48,1280]{1,0:T(8,128)(2,1)S(1)}, u32[]{:S(2)}, u32[]{:S(2)}) %collective-permute-start.50) | collective-permute-done | bytes 122912 | tf_op jit(solution)/shard_map/ppermute | solution.py:96
  (111 shorter events, 55.1 us)
Async XLA Ops:
  3.6 21.6 %collective-permute-start = (bf16[512,768]{1,0:T(8,128)(2,1)}, bf16[512,768]{1,0:T(8,128)(2,1)S(1)}, u32[]{:S(2)}, u32[]{:S(2)}) collective-permute-start(bf16[512,768]{1,0:T(8,128)(2,1)} %get-tuple-element.113.refs_1_.refs_14_), channel_id=1, source_target_pairs={{0,1},{1,0},{2,3},{3,2},{4,5},{5,4},{6,7},{7,6},{8,9},{9,8},{10,11... | collective-permute-start | bytes 2359304 | tf_op jit(solution)/shard_map/ppermute | solution.py:96
  6.6 9.1 %collective-permute-start.3 = (bf16[48,1664]{1,0:T(8,128)(2,1)}, bf16[48,1664]{1,0:T(8,128)(2,1)S(1)}, u32[]{:S(2)}, u32[]{:S(2)}) collective-permute-start(bf16[48,1664]{1,0:T(8,128)(2,1)} %get-tuple-element.128.refs_9_), channel_id=1, source_target_pairs={{0,24},{2,26},{4,28},{6,30},{8,16},{10,18},{12,20},{14,22},{16,8},... | collective-permute-start | bytes 479240 | tf_op jit(solution)/shard_map/ppermute | solution.py:96
  10.2 13.5 %collective-permute-start.2 = (bf16[48,1664]{1,0:T(8,128)(2,1)}, bf16[48,1664]{1,0:T(8,128)(2,1)S(1)}, u32[]{:S(2)}, u32[]{:S(2)}) collective-permute-start(bf16[48,1664]{1,0:T(8,128)(2,1)} %get-tuple-element.128.refs_9_), channel_id=1, source_target_pairs={{0,16},{2,18},{4,20},{6,22},{8,24},{10,26},{12,28},{14,30},{16,0},... | collective-permute-start | bytes 479240 | tf_op jit(solution)/shard_map/ppermute | solution.py:96
  10.2 15.9 %collective-permute-start.1 = (bf16[48,1664]{1,0:T(8,128)(2,1)}, bf16[48,1664]{1,0:T(8,128)(2,1)S(1)}, u32[]{:S(2)}, u32[]{:S(2)}) collective-permute-start(bf16[48,1664]{1,0:T(8,128)(2,1)} %get-tuple-element.128.refs_9_), channel_id=1, source_target_pairs={{0,8},{2,10},{4,12},{6,14},{8,0},{10,2},{12,4},{14,6},{16,24},{18,... | collective-permute-start | bytes 479240 | tf_op jit(solution)/shard_map/ppermute | solution.py:96
  11.0 19.4 %collective-permute-start.7 = (bf16[48,1664]{1,0:T(8,128)(2,1)}, bf16[48,1664]{1,0:T(8,128)(2,1)S(1)}, u32[]{:S(2)}, u32[]{:S(2)}) collective-permute-start(bf16[48,1664]{1,0:T(8,128)(2,1)} %get-tuple-element.128.refs_9_), channel_id=1, source_target_pairs={{0,4},{2,6},{4,0},{6,2},{8,12},{10,14},{12,8},{14,10},{16,20},{18,... | collective-permute-start | bytes 479240 | tf_op jit(solution)/shard_map/ppermute | solution.py:96
  15.7 16.3 %collective-permute-start.10 = (bf16[48,1664]{1,0:T(8,128)(2,1)S(1)}, bf16[48,1664]{1,0:T(8,128)(2,1)S(1)}, u32[]{:S(2)}, u32[]{:S(2)}) collective-permute-start(bf16[48,1664]{1,0:T(8,128)(2,1)S(1)} %collective-permute-done.3.refs_12_), channel_id=1, source_target_pairs={{0,4},{2,6},{4,0},{6,2},{8,12},{10,14},{12,8},{14,10},{16,20},{18,... | collective-permute-start | bytes 479240 | tf_op jit(solution)/shard_map/ppermute | solution.py:96
  23.7 10.9 %collective-permute-start.9 = (bf16[48,1664]{1,0:T(8,128)(2,1)S(1)}, bf16[48,1664]{1,0:T(8,128)(2,1)S(1)}, u32[]{:S(2)}, u32[]{:S(2)}) collective-permute-start(bf16[48,1664]{1,0:T(8,128)(2,1)S(1)} %collective-permute-done.2.refs_11_), channel_id=1, source_target_pairs={{0,4},{2,6},{4,0},{6,2},{8,12},{10,14},{12,8},{14,10},{16,20},{18,... | collective-permute-start | bytes 479240 | tf_op jit(solution)/shard_map/ppermute | solution.py:96
  25.2 29.4 %collective-permute-start.31 = (bf16[512,768]{1,0:T(8,128)(2,1)}, bf16[512,768]{1,0:T(8,128)(2,1)S(1)}, u32[]{:S(2)}, u32[]{:S(2)}) collective-permute-start(bf16[512,768]{1,0:T(8,128)(2,1)} %get-tuple-element.146.refs_15_), channel_id=1, source_target_pairs={{0,1},{1,0},{2,3},{3,2},{4,5},{5,4},{6,7},{7,6},{8,9},{9,8},{10,11... | collective-permute-start | bytes 2359304 | tf_op jit(solution)/shard_map/ppermute | solution.py:96
  26.1 8.7 %collective-permute-start.8 = (bf16[48,1664]{1,0:T(8,128)(2,1)S(1)}, bf16[48,1664]{1,0:T(8,128)(2,1)S(1)}, u32[]{:S(2)}, u32[]{:S(2)}) collective-permute-start(bf16[48,1664]{1,0:T(8,128)(2,1)S(1)} %collective-permute-done.1.refs_10_), channel_id=1, source_target_pairs={{0,4},{2,6},{4,0},{6,2},{8,12},{10,14},{12,8},{14,10},{16,20},{18,... | collective-permute-start | bytes 479240 | tf_op jit(solution)/shard_map/ppermute | solution.py:96
  47.1 8.1 %collective-permute-start.20 = (bf16[512,768]{1,0:T(8,128)(2,1)S(1)}, bf16[512,768]{1,0:T(8,128)(2,1)S(1)}, u32[]{:S(2)}, u32[]{:S(2)}) collective-permute-start(bf16[512,768]{1,0:T(8,128)(2,1)S(1)} %copy-done.3), channel_id=1, source_target_pairs={{0,2},{2,0},{4,6},{6,4},{8,10},{10,8},{12,14},{14,12},{16,18},{18,... | collective-permute-start | bytes 2359304 | tf_op jit(solution)/shard_map/ppermute | solution.py:96
  54.6 16.0 %collective-permute-start.32 = (bf16[512,768]{1,0:T(8,128)(2,1)S(1)}, bf16[512,768]{1,0:T(8,128)(2,1)S(1)}, u32[]{:S(2)}, u32[]{:S(2)}) collective-permute-start(bf16[512,768]{1,0:T(8,128)(2,1)S(1)} %collective-permute-done.31.refs_17_), channel_id=1, source_target_pairs={{0,2},{2,0},{4,6},{6,4},{8,10},{10,8},{12,14},{14,12},{16,18},{18,... | collective-permute-start | bytes 2359304 | tf_op jit(solution)/shard_map/ppermute | solution.py:96
  54.6 8.4 %collective-permute-start.30 = (bf16[160,768]{1,0:T(8,128)(2,1)S(1)}, bf16[160,768]{1,0:T(8,128)(2,1)S(1)}, u32[]{:S(2)}, u32[]{:S(2)}) collective-permute-start(bf16[160,768]{1,0:T(8,128)(2,1)S(1)} %pad_maximum_fusion), channel_id=1, source_target_pairs={{0,4},{2,6},{4,0},{6,2},{8,12},{10,14},{12,8},{14,10},{16,20},{18,... | collective-permute-start | bytes 737288 | tf_op jit(solution)/shard_map/ppermute | solution.py:96
  55.4 8.2 %collective-permute-start.23 = (bf16[40,768]{1,0:T(8,128)(2,1)S(1)}, bf16[40,768]{1,0:T(8,128)(2,1)S(1)}, u32[]{:S(2)}, u32[]{:S(2)}) collective-permute-start(bf16[40,768]{1,0:T(8,128)(2,1)S(1)} %get-tuple-element.142), channel_id=1, source_target_pairs={{0,8},{2,10},{4,12},{6,14},{8,0},{10,2},{12,4},{14,6},{16,24},{18,... | collective-permute-start | bytes 184328 | tf_op jit(solution)/shard_map/ppermute | solution.py:96
  55.5 9.6 %collective-permute-start.24 = (bf16[40,768]{1,0:T(8,128)(2,1)S(1)}, bf16[40,768]{1,0:T(8,128)(2,1)S(1)}, u32[]{:S(2)}, u32[]{:S(2)}) collective-permute-start(bf16[40,768]{1,0:T(8,128)(2,1)S(1)} %get-tuple-element.143), channel_id=1, source_target_pairs={{0,16},{2,18},{4,20},{6,22},{8,24},{10,26},{12,28},{14,30},{16,0},... | collective-permute-start | bytes 184328 | tf_op jit(solution)/shard_map/ppermute | solution.py:96
  56.8 8.8 %collective-permute-start.25 = (bf16[40,768]{1,0:T(8,128)(2,1)S(1)}, bf16[40,768]{1,0:T(8,128)(2,1)S(1)}, u32[]{:S(2)}, u32[]{:S(2)}) collective-permute-start(bf16[40,768]{1,0:T(8,128)(2,1)S(1)} %get-tuple-element.144), channel_id=1, source_target_pairs={{0,24},{2,26},{4,28},{6,30},{8,16},{10,18},{12,20},{14,22},{16,8},... | collective-permute-start | bytes 184328 | tf_op jit(solution)/shard_map/ppermute | solution.py:96
  76.2 13.6 %collective-permute-start.33 = (bf16[160,1536]{1,0:T(8,128)(2,1)S(1)}, bf16[160,1536]{1,0:T(8,128)(2,1)S(1)}, u32[]{:S(2)}, u32[]{:S(2)}) collective-permute-start(bf16[160,1536]{1,0:T(8,128)(2,1)S(1)} %get-tuple-element.149), channel_id=1, source_target_pairs={{0,4},{2,6},{4,0},{6,2},{8,12},{10,14},{12,8},{14,10},{16,20},{18,... | collective-permute-start | bytes 1474568 | tf_op jit(solution)/shard_map/ppermute | solution.py:96
  81.0 15.4 %collective-permute-start.35 = (bf16[768,384]{1,0:T(8,128)(2,1)S(1)}, bf16[768,384]{1,0:T(8,128)(2,1)S(1)}, u32[]{:S(2)}, u32[]{:S(2)}) collective-permute-start(bf16[768,384]{1,0:T(8,128)(2,1)S(1)} %get-tuple-element.157), channel_id=1, source_target_pairs={{0,1},{1,0},{2,3},{3,2},{4,5},{5,4},{6,7},{7,6},{8,9},{9,8},{10,11... | collective-permute-start | bytes 1769480 | tf_op jit(solution)/shard_map/ppermute | solution.py:96
  90.0 12.4 %collective-permute-start.37 = (bf16[40,1536]{1,0:T(8,128)(2,1)S(1)}, bf16[40,1536]{1,0:T(8,128)(2,1)S(1)}, u32[]{:S(2)}, u32[]{:S(2)}) collective-permute-start(bf16[40,1536]{1,0:T(8,128)(2,1)S(1)} %get-tuple-element.160), channel_id=1, source_target_pairs={{0,16},{2,18},{4,20},{6,22},{8,24},{10,26},{12,28},{14,30},{16,0},... | collective-permute-start | bytes 368648 | tf_op jit(solution)/shard_map/ppermute | solution.py:96
  91.3 11.1 %collective-permute-start.38 = (bf16[40,1536]{1,0:T(8,128)(2,1)S(1)}, bf16[40,1536]{1,0:T(8,128)(2,1)S(1)}, u32[]{:S(2)}, u32[]{:S(2)}) collective-permute-start(bf16[40,1536]{1,0:T(8,128)(2,1)S(1)} %get-tuple-element.161), channel_id=1, source_target_pairs={{0,24},{2,26},{4,28},{6,30},{8,16},{10,18},{12,20},{14,22},{16,8},... | collective-permute-start | bytes 368648 | tf_op jit(solution)/shard_map/ppermute | solution.py:96
  119.8 24.0 %collective-permute-start.47 = (bf16[672,768]{1,0:T(8,128)(2,1)S(1)}, bf16[672,768]{1,0:T(8,128)(2,1)S(1)}, u32[]{:S(2)}, u32[]{:S(2)}) collective-permute-start(bf16[672,768]{1,0:T(8,128)(2,1)S(1)} %get-tuple-element.191), channel_id=1, source_target_pairs={{0,1},{1,0},{2,3},{3,2},{4,5},{5,4},{6,7},{7,6},{8,9},{9,8},{10,11... | collective-permute-start | bytes 3096584 | tf_op jit(solution)/shard_map/ppermute | solution.py:96
  121.7 13.4 %collective-permute-start.43 = (bf16[4,48,1280]{2,1,0:T(8,128)(2,1)S(1)}, bf16[4,48,1280]{2,1,0:T(8,128)(2,1)S(1)}, u32[]{:S(2)}, u32[]{:S(2)}) collective-permute-start(bf16[4,48,1280]{2,1,0:T(8,128)(2,1)S(1)} %get-tuple-element.184), channel_id=1, source_target_pairs={{0,4},{2,6},{4,0},{6,2},{8,12},{10,14},{12,8},{14,10},{16,20},{18,... | collective-permute-start | bytes 1474568 | tf_op jit(solution)/shard_map/ppermute | solution.py:96
  135.2 11.1 %collective-permute-start.49 = (bf16[48,1280]{1,0:T(8,128)(2,1)S(1)}, bf16[48,1280]{1,0:T(8,128)(2,1)S(1)}, u32[]{:S(2)}, u32[]{:S(2)}) collective-permute-start(bf16[48,1280]{1,0:T(8,128)(2,1)S(1)} %get-tuple-element.199), channel_id=1, source_target_pairs={{0,8},{2,10},{4,12},{6,14},{8,0},{10,2},{12,4},{14,6},{16,24},{18,... | collective-permute-start | bytes 368648 | tf_op jit(solution)/shard_map/ppermute | solution.py:96
  137.8 11.3 %collective-permute-start.50 = (bf16[48,1280]{1,0:T(8,128)(2,1)S(1)}, bf16[48,1280]{1,0:T(8,128)(2,1)S(1)}, u32[]{:S(2)}, u32[]{:S(2)}) collective-permute-start(bf16[48,1280]{1,0:T(8,128)(2,1)S(1)} %get-tuple-element.200), channel_id=1, source_target_pairs={{0,16},{2,18},{4,20},{6,22},{8,24},{10,26},{12,28},{14,30},{16,0},... | collective-permute-start | bytes 368648 | tf_op jit(solution)/shard_map/ppermute | solution.py:96
  137.8 11.3 %collective-permute-start.51 = (bf16[48,1280]{1,0:T(8,128)(2,1)S(1)}, bf16[48,1280]{1,0:T(8,128)(2,1)S(1)}, u32[]{:S(2)}, u32[]{:S(2)}) collective-permute-start(bf16[48,1280]{1,0:T(8,128)(2,1)S(1)} %get-tuple-element.201), channel_id=1, source_target_pairs={{0,24},{2,26},{4,28},{6,30},{8,16},{10,18},{12,20},{14,22},{16,8},... | collective-permute-start | bytes 368648 | tf_op jit(solution)/shard_map/ppermute | solution.py:96
  (34 other events, 155.7 us)
